TPU v7x, 32 devices: a whole 2x2x4 slice. The times are simulated.
32 devices in a mesh: rad: 2 (over x), ang: 8 (over z, y), ax: 2 (over core).
Axes of the slice: x: 2, y: 2, z: 4, core: 2. Of those that a mesh axis runs over, the one named last changes fastest.
Arguments:
- start_potential: float32 [32, 384, 256], P('rad', 'ang', 'ax'), may hold values from -6 to 6
- charge_density: float32 [32, 384, 256], P('rad', 'ang', 'ax'), may hold values from -12 to 12
- box_anchor: int32 [3, 128], replicated, may hold values from 0 to 7, as said below
- box_extent: int32 [3, 128], replicated, may hold values from 1 to 2, as said below
- atom_center: float32 [3, 128], replicated, as said below
- atom_charge: float32 [128], replicated, may hold values from 0.5 to 2
- atom_place: int32 [128], replicated, may hold values from 0 to 127, each once
Outputs:
- potential: float32 [32, 384, 256], P('rad', 'ang', 'ax')
- forces: float32 [3, 128], P(None, ('rad', 'ang', 'ax'))
Inputs may be any that keep to these rules, and one draw needn't show every extreme that they name: `box_anchor`: box anchors per dimension lie within that dimension's block count, the radial anchor plus extent never passes the last radial block, and at most 8 atoms share one anchor block. `box_extent`: at most 64 atom boxes cover any one block, and in every draw some block is covered by exactly 64. `atom_center`: each atom's center lies inside its box, in the box's unwrapped cell coordinates.
All inputs are finite; a program needn't handle non-finite values.
Results may differ from a plain program's by a relative error of at most 0.0003.
Values sent between devices are 32-bit elements; how exact they have to be, the bound alone decides.
No kernel may reach another device: no remote copies, remote signals or barrier semaphores. Data moves between devices by JAX's collectives and lax.ppermute only.
A program may use at most 64 MiB of HBM per device.

v0:
```python
import math

import jax
import jax.numpy as jnp
from jax import lax
from jax.sharding import PartitionSpec as P

SWEEPS = 3
SLOTS = 64


cheb_low = 0.2
cheb_high = 2.0
highest = lax.Precision.HIGHEST


def with_halo(block, sides, width, periodic):
    for axis, dim in sides:
        count = lax.axis_size(axis)
        forward = [(i, i + 1) for i in range(count - 1)]
        if periodic:
            forward.append((count - 1, 0))
        backward = [(target, source) for source, target in forward]
        low = lax.ppermute(
            lax.slice_in_dim(block, block.shape[dim] - width, None, axis=dim), axis, forward
        )
        high = lax.ppermute(lax.slice_in_dim(block, 0, width, axis=dim), axis, backward)
        block = jnp.concatenate([low, block, high], axis=dim)
    return block


def sweep_weights(total_sweeps):
    middle = 0.5 * (cheb_high + cheb_low)
    spread = 0.5 * (cheb_high - cheb_low)
    return [
        1.0 / (middle + spread * math.cos(math.pi * (2 * number + 1) / (2 * total_sweeps)))
        for number in range(total_sweeps)
    ]


def relax_step(
    center,
    radial_up,
    radial_down,
    angle_next,
    angle_prev,
    axial_next,
    axial_prev,
    source,
    radius,
    angle_step,
    weight,
):
    lower_face = radius - 0.5
    upper_face = radius + 0.5
    angular = 1.0 / (radius * radius * (angle_step * angle_step))
    doubled = 2.0 * center
    applied = (upper_face * (center - radial_up) + lower_face * (center - radial_down)) / radius
    applied = (
        applied
        + angular * (doubled - angle_next - angle_prev)
        + (doubled - axial_next - axial_prev)
    )
    diagonal = (upper_face + lower_face) / radius + 2.0 * angular + 2.0
    return center + weight * (source - applied) / diagonal


def gaussian_pair(coords, middle_point, width):
    distance = coords - middle_point
    profile = jnp.exp(-(distance * distance) / (2.0 * width * width))
    return (profile, profile * (-distance / (width * width)))


def radius_rows(first_row, row_count, rad_total):
    row_index = first_row + jnp.arange(row_count, dtype=jnp.int32)
    radius = 0.5 * rad_total + row_index.astype(jnp.float32) + 0.5
    inside = (row_index >= 0) & (row_index < rad_total)
    return (radius[:, None, None], inside[:, None, None])


def shards(
    start_potential, charge_density, box_anchor, box_extent, atom_center, atom_charge, atom_place
):
    rad_cells, ang_cells, axial_cells = start_potential.shape
    rad_total = rad_cells * lax.axis_size("rad")
    angle_step = 2.0 * math.pi / (ang_cells * lax.axis_size("ang"))
    rad_start = lax.axis_index("rad") * rad_cells
    weights = sweep_weights(SWEEPS)
    radius, inside = radius_rows(rad_start, rad_cells, rad_total)
    potential = start_potential
    for sweep_index in range(SWEEPS):
        wrapped = with_halo(potential, (("ang", 1), ("ax", 2)), 1, True)
        layered = with_halo(potential, (("rad", 0),), 1, False)
        potential = relax_step(
            potential,
            layered[2:],
            layered[:-2],
            wrapped[:, 2:, 1:-1],
            wrapped[:, :-2, 1:-1],
            wrapped[:, 1:-1, 2:],
            wrapped[:, 1:-1, :-2],
            charge_density,
            radius,
            angle_step,
            weights[sweep_index],
        )
    width_rad = rad_cells / 3.0
    width_ang = ang_cells / 3.0
    width_axial = axial_cells / 3.0
    amplitude = 1.0 / math.sqrt(width_ang * width_axial / width_rad)
    offset_rad = lax.axis_index("rad") - box_anchor[0]
    offset_ang = jnp.remainder(lax.axis_index("ang") - box_anchor[1], lax.axis_size("ang"))
    offset_axial = jnp.remainder(lax.axis_index("ax") - box_anchor[2], lax.axis_size("ax"))
    covered = (
        (offset_rad >= 0)
        & (offset_rad < box_extent[0])
        & (offset_ang < box_extent[1])
        & (offset_axial < box_extent[2])
    )
    picked = jnp.nonzero(covered, size=SLOTS, fill_value=0)[0].astype(jnp.int32)
    occupied = jnp.arange(SLOTS, dtype=jnp.int32) < jnp.sum(covered.astype(jnp.int32))
    centers = atom_center[:, picked]
    coord_rad = (rad_start + jnp.arange(rad_cells, dtype=jnp.int32)).astype(jnp.float32)[:, None]
    rad_profile, rad_slope = gaussian_pair(coord_rad, centers[0][None, :], width_rad)
    start_ang = (box_anchor[1, picked] + offset_ang[picked]) * ang_cells
    coord_ang = (start_ang[None, :] + jnp.arange(ang_cells, dtype=jnp.int32)[:, None]).astype(
        jnp.float32
    )
    ang_profile, ang_slope = gaussian_pair(coord_ang, centers[1][None, :], width_ang)
    start_axial = (box_anchor[2, picked] + offset_axial[picked]) * axial_cells
    coord_axial = (start_axial[None, :] + jnp.arange(axial_cells, dtype=jnp.int32)[:, None]).astype(
        jnp.float32
    )
    axial_profile, axial_slope = gaussian_pair(coord_axial, centers[2][None, :], width_axial)
    axial_factors = jnp.concatenate([axial_profile, axial_slope], axis=1)
    projected = jnp.dot(
        potential.reshape(rad_cells * ang_cells, axial_cells),
        axial_factors,
        precision=highest,
        preferred_element_type=jnp.float32,
    )
    projected = projected.reshape(rad_cells, ang_cells, 2 * SLOTS)
    plain_part = projected[:, :, :SLOTS]
    sloped = projected[:, :, SLOTS:]
    along_r = jnp.einsum("ijs,js->is", plain_part, ang_profile, precision=highest)
    along_a = jnp.einsum("ijs,js->is", plain_part, ang_slope, precision=highest)
    along_z = jnp.einsum("ijs,js->is", sloped, ang_profile, precision=highest)
    radius_col = 0.5 * rad_total + coord_rad + 0.5
    weight_rad = angle_step * radius_col
    force_r = jnp.sum(weight_rad * rad_slope * along_r, axis=0)
    force_a = jnp.sum(rad_profile * along_a, axis=0)
    force_z = jnp.sum(weight_rad * rad_profile * along_z, axis=0)
    strength = jnp.where(occupied, atom_charge[picked] * amplitude, 0.0)
    pieces = jnp.stack([force_r, force_a, force_z]) * strength[None, :]
    places = atom_place[picked]
    onehot = (places[:, None] == jnp.arange(atom_place.shape[0], dtype=jnp.int32)[None, :]).astype(
        jnp.float32
    )
    partial_forces = jnp.dot(pieces, onehot, precision=highest, preferred_element_type=jnp.float32)
    forces = lax.psum_scatter(partial_forces, ("rad", "ang", "ax"), scatter_dimension=1, tiled=True)
    return (potential, forces)


def solution(mesh):
    placed = (P("rad", "ang", "ax"), P("rad", "ang", "ax"), P(), P(), P(), P(), P())
    return jax.shard_map(
        shards,
        mesh=mesh,
        in_specs=placed,
        out_specs=(P("rad", "ang", "ax"), P(None, ("rad", "ang", "ax"))),
        check_vma=False,
    )
```

profile of v0, /device:TPU:0, one launch (start us, length us, event | category | flops | bytes accessed | tf_op | source)
XLA Modules:
  0.0 98.3 jit_solution(8405876661147166156)
XLA Ops:
  0.6 0.9 fusion.106
  1.5 6.1 %collective-permute-start.2 = (f32[16,1,128]{2,1,0:T(1,128)S(1)}, f32[16,1,128]{2,1,0:T(1,128)S(1)}, u32[]{:S(2)}, u32[]{:S(2)}) collective-permute-start(f32[16,1,128]{2,1,0:T(1,128)S(1)} %get-tuple-element.35), channel_id=1, source_target_pairs={{2,0},{4,2},{6,4},{8,6},{10,8},{12,10},{14,12},{0,14},{3,1},{5,3},... | collective-permute-start | bytes 24584 | tf_op jit(solution)/shard_map/ppermute | solution.py:27
  7.6 0.8 fusion.105
  8.4 1.3 %collective-permute-start = (f32[1,48,128]{2,1,0:T(8,128)S(1)}, f32[1,48,128]{2,1,0:T(8,128)S(1)}, u32[]{:S(2)}, u32[]{:S(2)}) collective-permute-start(f32[1,48,128]{2,1,0:T(8,128)S(1)} %get-tuple-element.32), channel_id=1, source_target_pairs={{16,0},{17,1},{18,2},{19,3},{20,4},{21,5},{22,6},{23,7},{24,8},{25... | collective-permute-start | bytes 73736 | tf_op jit(solution)/shard_map/ppermute | solution.py:27
  9.6 4.5 %collective-permute-start.1 = (f32[1,48,128]{2,1,0:T(8,128)S(1)}, f32[1,48,128]{2,1,0:T(8,128)S(1)}, u32[]{:S(2)}, u32[]{:S(2)}) collective-permute-start(f32[1,48,128]{2,1,0:T(8,128)S(1)} %get-tuple-element.33), channel_id=1, source_target_pairs={{0,16},{1,17},{2,18},{3,19},{4,20},{5,21},{6,22},{7,23},{8,24},{9,... | collective-permute-start | bytes 73736 | tf_op jit(solution)/shard_map/ppermute | solution.py:24
  16.5 1.4 %scatter_custom_fusion = s32[64]{0:T(128)S(1)} fusion(s32[128]{0:T(128)S(1)} %fusion.57, s32[128]{0:T(128)S(1)} %rem.108, s32[]{:T(128)} %constant.120.clone.1), kind=kCustom, calls=%fused_computation.186 | custom fusion | flops 128 | bytes 260 | tf_op jit(solution)/shard_map/scatter-add | solution.py:120
  18.1 0.8 or_reduce_fusion.1
  19.0 0.9 gather_fusion.3
  20.0 0.8 gather_fusion.4
  21.5 0.8 gather_fusion.2
  22.3 0.9 gather_fusion.1
  23.2 0.8 gather_fusion.5
  25.7 1.3 %collective-permute-done.4 = f32[16,50,1]{2,1,0:T(8,128)S(1)} collective-permute-done((f32[16,50,1]{2,1,0:T(8,128)S(1)}, f32[16,50,1]{2,1,0:T(8,128)S(1)}, u32[]{:S(2)}, u32[]{:S(2)}) %collective-permute-start.4) | collective-permute-done | bytes 3232 | tf_op jit(solution)/shard_map/ppermute | solution.py:27
  27.6 0.8 fusion.41
  28.4 4.8 %collective-permute-start.8 = (f32[16,1,128]{2,1,0:T(1,128)S(1)}, f32[16,1,128]{2,1,0:T(1,128)S(1)}, u32[]{:S(2)}, u32[]{:S(2)}) collective-permute-start(f32[16,1,128]{2,1,0:T(1,128)S(1)} %get-tuple-element.31), channel_id=1, source_target_pairs={{2,0},{4,2},{6,4},{8,6},{10,8},{12,10},{14,12},{0,14},{3,1},{5,3},... | collective-permute-start | bytes 24584 | tf_op jit(solution)/shard_map/ppermute | solution.py:27
  33.2 1.3 %collective-permute-start.6 = (f32[1,48,128]{2,1,0:T(8,128)S(1)}, f32[1,48,128]{2,1,0:T(8,128)S(1)}, u32[]{:S(2)}, u32[]{:S(2)}) collective-permute-start(f32[1,48,128]{2,1,0:T(8,128)S(1)} %get-tuple-element.28), channel_id=1, source_target_pairs={{16,0},{17,1},{18,2},{19,3},{20,4},{21,5},{22,6},{23,7},{24,8},{25... | collective-permute-start | bytes 73736 | tf_op jit(solution)/shard_map/ppermute | solution.py:27
  34.5 4.5 %collective-permute-start.7 = (f32[1,48,128]{2,1,0:T(8,128)S(1)}, f32[1,48,128]{2,1,0:T(8,128)S(1)}, u32[]{:S(2)}, u32[]{:S(2)}) collective-permute-start(f32[1,48,128]{2,1,0:T(8,128)S(1)} %get-tuple-element.29), channel_id=1, source_target_pairs={{0,16},{1,17},{2,18},{3,19},{4,20},{5,21},{6,22},{7,23},{8,24},{9,... | collective-permute-start | bytes 73736 | tf_op jit(solution)/shard_map/ppermute | solution.py:24
  40.4 1.3 %collective-permute-done.10 = f32[16,50,1]{2,1,0:T(8,128)S(1)} collective-permute-done((f32[16,50,1]{2,1,0:T(8,128)S(1)}, f32[16,50,1]{2,1,0:T(8,128)S(1)}, u32[]{:S(2)}, u32[]{:S(2)}) %collective-permute-start.10) | collective-permute-done | bytes 3232 | tf_op jit(solution)/shard_map/ppermute | solution.py:27
  42.3 0.7 fusion.24
  43.1 4.3 %collective-permute-start.14 = (f32[16,1,128]{2,1,0:T(1,128)S(1)}, f32[16,1,128]{2,1,0:T(1,128)S(1)}, u32[]{:S(2)}, u32[]{:S(2)}) collective-permute-start(f32[16,1,128]{2,1,0:T(1,128)S(1)} %get-tuple-element.27), channel_id=1, source_target_pairs={{2,0},{4,2},{6,4},{8,6},{10,8},{12,10},{14,12},{0,14},{3,1},{5,3},... | collective-permute-start | bytes 24584 | tf_op jit(solution)/shard_map/ppermute | solution.py:27
  47.4 1.3 %collective-permute-start.12 = (f32[1,48,128]{2,1,0:T(8,128)S(1)}, f32[1,48,128]{2,1,0:T(8,128)S(1)}, u32[]{:S(2)}, u32[]{:S(2)}) collective-permute-start(f32[1,48,128]{2,1,0:T(8,128)S(1)} %get-tuple-element.24), channel_id=1, source_target_pairs={{16,0},{17,1},{18,2},{19,3},{20,4},{21,5},{22,6},{23,7},{24,8},{25... | collective-permute-start | bytes 73736 | tf_op jit(solution)/shard_map/ppermute | solution.py:27
  48.7 4.5 %collective-permute-start.13 = (f32[1,48,128]{2,1,0:T(8,128)S(1)}, f32[1,48,128]{2,1,0:T(8,128)S(1)}, u32[]{:S(2)}, u32[]{:S(2)}) collective-permute-start(f32[1,48,128]{2,1,0:T(8,128)S(1)} %get-tuple-element.25), channel_id=1, source_target_pairs={{0,16},{1,17},{2,18},{3,19},{4,20},{5,21},{6,22},{7,23},{8,24},{9,... | collective-permute-start | bytes 73736 | tf_op jit(solution)/shard_map/ppermute | solution.py:24
  54.6 0.8 gather_fusion.6
  58.6 39.1 %all-reduce.2 = f32[3,128]{1,0:T(4,128)S(1)} all-reduce(f32[3,128]{1,0:T(4,128)S(1)} %fusion.66), channel_id=2, replica_groups=mesh['rad'=2,'ang'=8,'ax'=2] {'rad','ang','ax'}, use_global_device_ids=true, to_apply=%region_7.8.clone | all-reduce | flops 384 | bytes 3072
  (85 shorter events, 12.8 us)
Async XLA Ops:
  0.6 22.6 %copy-start = (f32[128]{0:T(128)S(1)}, f32[128]{0:T(128)}, u32[]{:S(2)}) copy-start(f32[128]{0:T(128)} %param.12) | copy-start | bytes 1540
  1.5 23.3 %collective-permute-start.2 = (f32[16,1,128]{2,1,0:T(1,128)S(1)}, f32[16,1,128]{2,1,0:T(1,128)S(1)}, u32[]{:S(2)}, u32[]{:S(2)}) collective-permute-start(f32[16,1,128]{2,1,0:T(1,128)S(1)} %get-tuple-element.35), channel_id=1, source_target_pairs={{2,0},{4,2},{6,4},{8,6},{10,8},{12,10},{14,12},{0,14},{3,1},{5,3},... | collective-permute-start | bytes 24584 | tf_op jit(solution)/shard_map/ppermute | solution.py:27
  7.6 17.2 %collective-permute-start.3 = (f32[16,1,128]{2,1,0:T(1,128)S(1)}, f32[16,1,128]{2,1,0:T(1,128)S(1)}, u32[]{:S(2)}, u32[]{:S(2)}) collective-permute-start(f32[16,1,128]{2,1,0:T(1,128)S(1)} %get-tuple-element.34), channel_id=1, source_target_pairs={{0,2},{2,4},{4,6},{6,8},{8,10},{10,12},{12,14},{14,0},{1,3},{3,5},... | collective-permute-start | bytes 24584 | tf_op jit(solution)/shard_map/ppermute | solution.py:24
  8.4 19.3 %collective-permute-start = (f32[1,48,128]{2,1,0:T(8,128)S(1)}, f32[1,48,128]{2,1,0:T(8,128)S(1)}, u32[]{:S(2)}, u32[]{:S(2)}) collective-permute-start(f32[1,48,128]{2,1,0:T(8,128)S(1)} %get-tuple-element.32), channel_id=1, source_target_pairs={{16,0},{17,1},{18,2},{19,3},{20,4},{21,5},{22,6},{23,7},{24,8},{25... | collective-permute-start | bytes 73736 | tf_op jit(solution)/shard_map/ppermute | solution.py:27
  9.6 18.0 %collective-permute-start.1 = (f32[1,48,128]{2,1,0:T(8,128)S(1)}, f32[1,48,128]{2,1,0:T(8,128)S(1)}, u32[]{:S(2)}, u32[]{:S(2)}) collective-permute-start(f32[1,48,128]{2,1,0:T(8,128)S(1)} %get-tuple-element.33), channel_id=1, source_target_pairs={{0,16},{1,17},{2,18},{3,19},{4,20},{5,21},{6,22},{7,23},{8,24},{9,... | collective-permute-start | bytes 73736 | tf_op jit(solution)/shard_map/ppermute | solution.py:24
  19.0 0.9 copy-start.7
  23.2 1.6 %copy-start.4 = (f32[16,48,128]{2,1,0:T(8,128)S(1)}, f32[16,48,128]{2,1,0:T(8,128)}, u32[]{:S(2)}) copy-start(f32[16,48,128]{2,1,0:T(8,128)} %param.7) | copy-start | bytes 1179652
  24.9 2.7 %copy-start.3 = (f32[16,48,128]{2,1,0:T(8,128)S(1)}, f32[16,48,128]{2,1,0:T(8,128)}, u32[]{:S(2)}) copy-start(f32[16,48,128]{2,1,0:T(8,128)} %param.8) | copy-start | bytes 1179652
  25.1 1.9 %collective-permute-start.4 = (f32[16,50,1]{2,1,0:T(8,128)S(1)}, f32[16,50,1]{2,1,0:T(8,128)S(1)}, u32[]{:S(2)}, u32[]{:S(2)}) collective-permute-start(f32[16,50,1]{2,1,0:T(8,128)S(1)} %get-tuple-element.22), channel_id=1, source_target_pairs={{1,0},{0,1},{3,2},{2,3},{5,4},{4,5},{7,6},{6,7},{9,8},{8,9},{11,10... | collective-permute-start | bytes 9608 | tf_op jit(solution)/shard_map/ppermute | solution.py:27
  25.2 2.5 %collective-permute-start.5 = (f32[16,50,1]{2,1,0:T(8,128)S(1)}, f32[16,50,1]{2,1,0:T(8,128)S(1)}, u32[]{:S(2)}, u32[]{:S(2)}) collective-permute-start(f32[16,50,1]{2,1,0:T(8,128)S(1)} %get-tuple-element.23), channel_id=1, source_target_pairs={{0,1},{1,0},{2,3},{3,2},{4,5},{5,4},{6,7},{7,6},{8,9},{9,8},{10,11... | collective-permute-start | bytes 9608 | tf_op jit(solution)/shard_map/ppermute | solution.py:24
  28.4 10.6 %collective-permute-start.8 = (f32[16,1,128]{2,1,0:T(1,128)S(1)}, f32[16,1,128]{2,1,0:T(1,128)S(1)}, u32[]{:S(2)}, u32[]{:S(2)}) collective-permute-start(f32[16,1,128]{2,1,0:T(1,128)S(1)} %get-tuple-element.31), channel_id=1, source_target_pairs={{2,0},{4,2},{6,4},{8,6},{10,8},{12,10},{14,12},{0,14},{3,1},{5,3},... | collective-permute-start | bytes 24584 | tf_op jit(solution)/shard_map/ppermute | solution.py:27
  33.2 6.3 %collective-permute-start.9 = (f32[16,1,128]{2,1,0:T(1,128)S(1)}, f32[16,1,128]{2,1,0:T(1,128)S(1)}, u32[]{:S(2)}, u32[]{:S(2)}) collective-permute-start(f32[16,1,128]{2,1,0:T(1,128)S(1)} %get-tuple-element.30), channel_id=1, source_target_pairs={{0,2},{2,4},{4,6},{6,8},{8,10},{10,12},{12,14},{14,0},{1,3},{3,5},... | collective-permute-start | bytes 24584 | tf_op jit(solution)/shard_map/ppermute | solution.py:24
  33.2 9.1 %collective-permute-start.6 = (f32[1,48,128]{2,1,0:T(8,128)S(1)}, f32[1,48,128]{2,1,0:T(8,128)S(1)}, u32[]{:S(2)}, u32[]{:S(2)}) collective-permute-start(f32[1,48,128]{2,1,0:T(8,128)S(1)} %get-tuple-element.28), channel_id=1, source_target_pairs={{16,0},{17,1},{18,2},{19,3},{20,4},{21,5},{22,6},{23,7},{24,8},{25... | collective-permute-start | bytes 73736 | tf_op jit(solution)/shard_map/ppermute | solution.py:27
  34.5 7.8 %collective-permute-start.7 = (f32[1,48,128]{2,1,0:T(8,128)S(1)}, f32[1,48,128]{2,1,0:T(8,128)S(1)}, u32[]{:S(2)}, u32[]{:S(2)}) collective-permute-start(f32[1,48,128]{2,1,0:T(8,128)S(1)} %get-tuple-element.29), channel_id=1, source_target_pairs={{0,16},{1,17},{2,18},{3,19},{4,20},{5,21},{6,22},{7,23},{8,24},{9,... | collective-permute-start | bytes 73736 | tf_op jit(solution)/shard_map/ppermute | solution.py:24
  39.8 1.9 %collective-permute-start.10 = (f32[16,50,1]{2,1,0:T(8,128)S(1)}, f32[16,50,1]{2,1,0:T(8,128)S(1)}, u32[]{:S(2)}, u32[]{:S(2)}) collective-permute-start(f32[16,50,1]{2,1,0:T(8,128)S(1)} %get-tuple-element.20), channel_id=1, source_target_pairs={{1,0},{0,1},{3,2},{2,3},{5,4},{4,5},{7,6},{6,7},{9,8},{8,9},{11,10... | collective-permute-start | bytes 9608 | tf_op jit(solution)/shard_map/ppermute | solution.py:27
  39.9 2.5 %collective-permute-start.11 = (f32[16,50,1]{2,1,0:T(8,128)S(1)}, f32[16,50,1]{2,1,0:T(8,128)S(1)}, u32[]{:S(2)}, u32[]{:S(2)}) collective-permute-start(f32[16,50,1]{2,1,0:T(8,128)S(1)} %get-tuple-element.21), channel_id=1, source_target_pairs={{0,1},{1,0},{2,3},{3,2},{4,5},{5,4},{6,7},{7,6},{8,9},{9,8},{10,11... | collective-permute-start | bytes 9608 | tf_op jit(solution)/shard_map/ppermute | solution.py:24
  43.1 10.2 %collective-permute-start.14 = (f32[16,1,128]{2,1,0:T(1,128)S(1)}, f32[16,1,128]{2,1,0:T(1,128)S(1)}, u32[]{:S(2)}, u32[]{:S(2)}) collective-permute-start(f32[16,1,128]{2,1,0:T(1,128)S(1)} %get-tuple-element.27), channel_id=1, source_target_pairs={{2,0},{4,2},{6,4},{8,6},{10,8},{12,10},{14,12},{0,14},{3,1},{5,3},... | collective-permute-start | bytes 24584 | tf_op jit(solution)/shard_map/ppermute | solution.py:27
  47.4 6.3 %collective-permute-start.15 = (f32[16,1,128]{2,1,0:T(1,128)S(1)}, f32[16,1,128]{2,1,0:T(1,128)S(1)}, u32[]{:S(2)}, u32[]{:S(2)}) collective-permute-start(f32[16,1,128]{2,1,0:T(1,128)S(1)} %get-tuple-element.26), channel_id=1, source_target_pairs={{0,2},{2,4},{4,6},{6,8},{8,10},{10,12},{12,14},{14,0},{1,3},{3,5},... | collective-permute-start | bytes 24584 | tf_op jit(solution)/shard_map/ppermute | solution.py:24
  47.4 9.1 %collective-permute-start.12 = (f32[1,48,128]{2,1,0:T(8,128)S(1)}, f32[1,48,128]{2,1,0:T(8,128)S(1)}, u32[]{:S(2)}, u32[]{:S(2)}) collective-permute-start(f32[1,48,128]{2,1,0:T(8,128)S(1)} %get-tuple-element.24), channel_id=1, source_target_pairs={{16,0},{17,1},{18,2},{19,3},{20,4},{21,5},{22,6},{23,7},{24,8},{25... | collective-permute-start | bytes 73736 | tf_op jit(solution)/shard_map/ppermute | solution.py:27
  48.7 7.8 %collective-permute-start.13 = (f32[1,48,128]{2,1,0:T(8,128)S(1)}, f32[1,48,128]{2,1,0:T(8,128)S(1)}, u32[]{:S(2)}, u32[]{:S(2)}) collective-permute-start(f32[1,48,128]{2,1,0:T(8,128)S(1)} %get-tuple-element.25), channel_id=1, source_target_pairs={{0,16},{1,17},{2,18},{3,19},{4,20},{5,21},{6,22},{7,23},{8,24},{9,... | collective-permute-start | bytes 73736 | tf_op jit(solution)/shard_map/ppermute | solution.py:24
  53.8 0.8 copy-start.2
  54.0 1.9 %collective-permute-start.16 = (f32[16,50,1]{2,1,0:T(8,128)S(1)}, f32[16,50,1]{2,1,0:T(8,128)S(1)}, u32[]{:S(2)}, u32[]{:S(2)}) collective-permute-start(f32[16,50,1]{2,1,0:T(8,128)S(1)} %get-tuple-element.18), channel_id=1, source_target_pairs={{1,0},{0,1},{3,2},{2,3},{5,4},{4,5},{7,6},{6,7},{9,8},{8,9},{11,10... | collective-permute-start | bytes 9608 | tf_op jit(solution)/shard_map/ppermute | solution.py:27
  54.1 2.5 %collective-permute-start.17 = (f32[16,50,1]{2,1,0:T(8,128)S(1)}, f32[16,50,1]{2,1,0:T(8,128)S(1)}, u32[]{:S(2)}, u32[]{:S(2)}) collective-permute-start(f32[16,50,1]{2,1,0:T(8,128)S(1)} %get-tuple-element.19), channel_id=1, source_target_pairs={{0,1},{1,0},{2,3},{3,2},{4,5},{5,4},{6,7},{7,6},{8,9},{9,8},{10,11... | collective-permute-start | bytes 9608 | tf_op jit(solution)/shard_map/ppermute | solution.py:24
  57.3 0.7 copy-start.5
  (2 other events, 1.4 us)
where the time goes:
time: 98.7 us; the launch traced here: 98.3 us
  blocking collectives  39.1 us (40%)
  starting transfers between devices  34.3 us (35%)
  local copies, waits for them, and re-layouts  10.3 us (10%)
  other arithmetic  6.86 us (7%)
  waiting for transfers between devices  6.08 us (6%)
    unnamed x1, blocking collectives  39.1 us
    ppermute x9, starting transfers between devices, with_halo(): lax.ppermute(lax.slice_in_dim(block, 0, width, axis=dim), axis, backward)  19.2 us
    ppermute x9, starting transfers between devices, with_halo(): lax.ppermute(lax.slice_in_dim(block, block.shape[dim] - width, None, axis...  15.1 us
    ppermute x9, waiting for transfers between devices, with_halo(): lax.ppermute(lax.slice_in_dim(block, 0, width, axis=dim), axis, backward)  3.14 us
    ppermute x9, waiting for transfers between devices, with_halo(): lax.ppermute(lax.slice_in_dim(block, block.shape[dim] - width, None, axis...  2.94 us
    add x3, other arithmetic, relax_step(): return center + weight * (source - applied) / diagonal  2.24 us
  transfers between devices with their start and end apart: 18, of which 8 were waited for; matrix products, arithmetic and copies ran while one was open for 12% of the time, Pallas kernels for 0%

commit v1 on v0

v1 whole, which is shorter than its diff:
```python
import functools
import math

import jax
import jax.numpy as jnp
from jax import lax
from jax.experimental import pallas as pl
from jax.experimental.pallas import tpu as pltpu
from jax.sharding import PartitionSpec as P

SWEEPS = 3
LANES = 128
AXES = ("rad", "ang", "ax")

cheb_low = 0.2
cheb_high = 2.0
highest = lax.Precision.HIGHEST


def sweep_weights(total_sweeps):
    middle = 0.5 * (cheb_high + cheb_low)
    spread = 0.5 * (cheb_high - cheb_low)
    return [
        1.0 / (middle + spread * math.cos(math.pi * (2 * number + 1) / (2 * total_sweeps)))
        for number in range(total_sweeps)
    ]


class Plan:
    def __init__(self, mesh, block, atoms):
        self.n_rad, self.n_ang, self.n_ax = (mesh.shape[name] for name in AXES)
        self.cells_r, self.cells_a, self.cells_z = block
        self.atoms = atoms
        self.chunks = atoms // LANES
        self.ring = self.cells_a + 8
        self.total_r = self.cells_r * self.n_rad
        self.total_a = self.cells_a * self.n_ang
        self.total_z = self.cells_z * self.n_ax
        self.angle_step = 2.0 * math.pi / self.total_a
        self.sides = 0 if self.n_rad == 1 else 1 if self.n_rad == 2 else 2
        self.slots = self.cells_r + SWEEPS * self.sides
        self.guard = SWEEPS + 1

    def sign(self, side, rad):
        if self.sides == 1:
            return 1 - 2 * rad
        return 1 - 2 * side

    def side_row(self, side, rad, step):
        sign = self.sign(side, rad)
        return (self.cells_r - 1) * (1 + sign) // 2 + sign * step

    def landing_row(self, side, rad, step):
        sign = self.sign(side, rad)
        return (self.cells_r - 1) * (1 + sign) // 2 - sign * (step - 1)

    def device(self, rad, ang, ax):
        return (rad * self.n_ang + ang) * self.n_ax + ax

    def pairs(self, core, move):
        found = []
        for rad in range(self.n_rad):
            for ang in range(self.n_ang):
                target = move(rad, ang)
                if target is not None:
                    found.append((self.device(rad, ang, core), self.device(*target, core)))
        return found


def factors_kernel(plan, anchor, extent, center, charge, place, z_out, a_out, r_out):
    rad, ang, ax = (lax.axis_index(name) for name in AXES)
    width_r, width_a, width_z = plan.cells_r / 3.0, plan.cells_a / 3.0, plan.cells_z / 3.0
    amplitude = 1.0 / math.sqrt(width_a * width_z / width_r)
    table = jnp.concatenate(
        [
            anchor[...].astype(jnp.float32),
            extent[...].astype(jnp.float32),
            center[...],
            charge[...],
            jnp.zeros((6, plan.atoms), jnp.float32),
        ],
        axis=0,
    )

    def pair(cell, start, span, middle, width, total):
        shifted = cell - start
        if total is not None:
            shifted = jnp.where(shifted < 0.0, shifted + total, shifted)
        distance = shifted + start - middle
        inside = (shifted >= 0.0) & (shifted < span)
        profile = jnp.where(inside, jnp.exp(-(distance * distance) / (2.0 * width * width)), 0.0)
        return profile, profile * (-distance / (width * width))

    def chunk(number, carry):
        rows = lax.broadcasted_iota(jnp.int32, (LANES, plan.atoms), 0) + number * LANES
        onehot = (place[...] == rows).astype(jnp.float32)
        ordered = lax.dot_general(
            table,
            onehot,
            (((1,), (1,)), ((), ())),
            precision=highest,
            preferred_element_type=jnp.float32,
        )
        row = [ordered[k : k + 1, :] for k in range(10)]
        depth = lax.broadcasted_iota(jnp.int32, (plan.total_z, LANES), 0) + ax * plan.cells_z
        depth = jnp.where(depth >= plan.total_z, depth - plan.total_z, depth).astype(jnp.float32)
        profile, slope = pair(
            depth, row[2] * plan.cells_z, row[5] * plan.cells_z, row[8], width_z, plan.total_z
        )
        z_out[number, :, :LANES] = profile
        z_out[number, :, LANES:] = slope
        spot = lax.broadcasted_iota(jnp.int32, (plan.ring, LANES), 0)
        spot = jnp.where(spot < plan.cells_a + 4, spot, spot - plan.ring) + ang * plan.cells_a
        spot = jnp.where(spot < 0, spot + plan.total_a, spot)
        spot = jnp.where(spot >= plan.total_a, spot - plan.total_a, spot).astype(jnp.float32)
        profile, slope = pair(
            spot, row[1] * plan.cells_a, row[4] * plan.cells_a, row[7], width_a, plan.total_a
        )
        a_out[number, 0] = profile
        a_out[number, 1] = slope
        slot = lax.broadcasted_iota(jnp.int32, (plan.slots, LANES), 0)
        level = slot
        for side in range(plan.sides):
            first = plan.cells_r + SWEEPS * side
            level = jnp.where(slot >= first, plan.side_row(side, rad, slot - first + 1), level)
        level = (level + rad * plan.cells_r).astype(jnp.float32)
        profile, slope = pair(
            level, row[0] * plan.cells_r, row[3] * plan.cells_r, row[6], width_r, None
        )
        radius = 0.5 * plan.total_r + level + 0.5
        strength = row[9] * amplitude
        r_out[number, 0] = strength * (plan.angle_step * radius) * slope
        r_out[number, 1] = strength * profile
        r_out[number, 2] = strength * (plan.angle_step * radius) * profile
        return carry

    if plan.chunks == 1:
        chunk(0, 0)
    else:
        lax.fori_loop(0, plan.chunks, chunk, 0)


def sweeps_kernel(
    plan,
    pot_own,
    pot_other,
    rho_own,
    rho_other,
    z_fac,
    a_fac,
    r_fac,
    own_out,
    hal_out,
    rad_out,
    force_out,
    first,
    second,
    grown,
    coef,
):
    rad, ax = lax.axis_index("rad"), lax.axis_index("ax")
    guard, rows, ring, depth = plan.guard, plan.cells_r, plan.ring, plan.total_z
    weights = sweep_weights(SWEEPS)

    level = lax.broadcasted_iota(jnp.int32, (coef.shape[1], depth), 0) - guard + rad * rows
    valid = (level >= 0) & (level < plan.total_r)
    radius = 0.5 * plan.total_r + level.astype(jnp.float32) + 0.5
    upper, lower = (radius + 0.5) / radius, (radius - 0.5) / radius
    angular = 1.0 / (radius * radius * (plan.angle_step * plan.angle_step))
    diagonal = upper + lower + 2.0 * angular + 2.0
    inverse = jnp.where(valid, 1.0 / diagonal, 0.0)
    coef[0] = upper
    coef[1] = lower
    coef[2] = angular
    coef[3] = inverse

    blank = jnp.zeros((ring, depth), jnp.float32)
    for buffer in (first, second):
        for row in range(guard):
            buffer[row] = blank
            buffer[guard + rows + row] = blank
    tail = jnp.zeros((ring - plan.cells_a, depth), jnp.float32)

    def whole(own, other, row):
        return jnp.concatenate([jnp.concatenate([own[row], other[row]], axis=1), tail], axis=0)

    for row in range(rows):
        first[guard + row] = whole(pot_own, pot_other, row)

    def relaxed(source, row, weight, charge):
        center = source[row]
        up, down, turn, inverse = (coef[k, pl.ds(row, 1), :] for k in range(4))
        total = pltpu.roll(center, 1, 1) + pltpu.roll(center, depth - 1, 1)
        total += turn * (pltpu.roll(center, 1, 0) + pltpu.roll(center, ring - 1, 0))
        total += up * source[row + 1] + down * source[row - 1]
        if charge is not None:
            total += charge
        return (1.0 - weight) * center + (weight * inverse) * total

    source, target = first, second
    for sweep in range(SWEEPS):
        last = sweep == SWEEPS - 1
        for row in range(rows):
            fresh = relaxed(source, guard + row, weights[sweep], whole(rho_own, rho_other, row))
            if last:
                grown[row] = fresh
                own_out[row] = fresh[: plan.cells_a, : plan.cells_z]
                hal_out[row] = fresh[plan.cells_a :, :]
            else:
                target[guard + row] = fresh
        for side in range(plan.sides):
            for step in range(1, sweep + 2):
                place = guard + plan.side_row(side, rad, step)
                fresh = relaxed(source, place, weights[sweep], None)
                if last:
                    slot = SWEEPS * side + step - 1
                    grown[rows + slot] = fresh
                    rad_out[slot] = fresh
                else:
                    target[place] = fresh
        source, target = target, source

    force_out[...] = jnp.zeros_like(force_out)

    @pl.when(ax == plan.n_ax - 1)
    def _():
        def chunk(number, carry):
            spread = jnp.dot(
                grown[...].reshape(plan.slots * ring, depth),
                z_fac[number],
                precision=highest,
                preferred_element_type=jnp.float32,
            )
            sums = [jnp.zeros((ring, LANES), jnp.float32) for _ in range(3)]
            for slot in range(plan.slots):
                piece = spread[slot * ring : (slot + 1) * ring]
                for k, part in enumerate((piece[:, :LANES], piece[:, :LANES], piece[:, LANES:])):
                    sums[k] += r_fac[number, k, pl.ds(slot, 1), :] * part
            for k, turn in enumerate((0, 1, 0)):
                force_out[number, pl.ds(k, 1), :] = jnp.sum(
                    a_fac[number, turn] * sums[k], axis=0, keepdims=True
                )
            return carry

        if plan.chunks == 1:
            chunk(0, 0)
        else:
            lax.fori_loop(0, plan.chunks, chunk, 0)


def turn_kernel(plan, *refs):
    hal, landed = refs[0], refs[1 : 1 + plan.sides]
    even_out, odd_out, held = refs[1 + plan.sides :]
    rad, ang = lax.axis_index("rad"), lax.axis_index("ang")
    held[...] = hal[...]
    for side in range(plan.sides):
        for step in range(1, SWEEPS + 1):
            row = plan.landing_row(side, rad, step)
            held[row] = held[row] + landed[side][step - 1, plan.cells_a :, :]
    low_half = lax.broadcasted_iota(jnp.int32, (8, plan.total_z), 0) < 4
    is_even = (lax.broadcasted_iota(jnp.int32, (8, plan.total_z), 0) * 0 + ang) % 2 == 0
    for tile in range(plan.cells_r // 2):
        front, back = held[2 * tile], held[2 * tile + 1]
        above = jnp.where(low_half, front, pltpu.roll(back, 4, 0))
        below = jnp.where(low_half, pltpu.roll(front, 4, 0), back)
        even_out[tile] = jnp.where(is_even, above, below)
        odd_out[tile] = jnp.where(is_even, below, above)


def final_kernel(plan, *refs):
    own, here, there, out = refs[0], refs[1 : 3 + plan.sides], refs[3 + plan.sides : -1], refs[-1]
    rad, ang = lax.axis_index("rad"), lax.axis_index("ang")
    width = plan.cells_z

    def landed(number, index):
        return here[number][index][:, :width] + there[number][index][:, width:]

    low_half = lax.broadcasted_iota(jnp.int32, (8, width), 0) < 4
    is_even = (lax.broadcasted_iota(jnp.int32, (8, width), 0) * 0 + ang) % 2 == 0
    top = plan.cells_a - 8
    for tile in range(plan.cells_r // 2):
        even, odd = landed(plan.sides, tile), landed(plan.sides + 1, tile)
        above, below = jnp.where(is_even, even, odd), jnp.where(is_even, odd, even)
        for half in range(2):
            row = 2 * tile + half
            from_below = below if half == 0 else pltpu.roll(below, 4, 0)
            from_above = above if half == 1 else pltpu.roll(above, 4, 0)
            out[row] = own[row]
            out[row, 0:8, :] += jnp.where(low_half, from_below, 0.0)
            out[row, top:, :] += jnp.where(low_half, 0.0, from_above)
    for side in range(plan.sides):
        for step in range(1, SWEEPS + 1):
            row = plan.landing_row(side, rad, step)
            out[row] += landed(side, step - 1)[: plan.cells_a]


def call(kernel, plan, outs, scratch, flops, bytes_moved, args):
    in_vmem = pl.BlockSpec(memory_space=pltpu.VMEM)
    return pl.pallas_call(
        functools.partial(kernel, plan),
        out_shape=[jax.ShapeDtypeStruct(shape, jnp.float32) for shape in outs],
        in_specs=[in_vmem] * len(args),
        out_specs=[in_vmem] * len(outs),
        scratch_shapes=[pltpu.VMEM(shape, jnp.float32) for shape in scratch],
        compiler_params=pltpu.CompilerParams(vmem_limit_bytes=24 * 2**20),
        cost_estimate=pl.CostEstimate(flops=flops, bytes_accessed=bytes_moved, transcendentals=0),
    )(*args)


def shards(plan, potential, density, anchor, extent, center, charge, place):
    ring, depth, slots, chunks = plan.ring, plan.total_z, plan.slots, plan.chunks
    rows = plan.cells_r
    swap = [(0, 1), (1, 0)]
    potential_other = lax.ppermute(potential, "ax", swap)
    density_other = lax.ppermute(density, "ax", swap)
    factors = call(
        factors_kernel,
        plan,
        [(chunks, depth, 2 * LANES), (chunks, 2, ring, LANES), (chunks, 3, slots, LANES)],
        [],
        10**6,
        10**6,
        (anchor, extent, center, charge.reshape(1, -1), place.reshape(1, -1)),
    )
    outs = [(rows, plan.cells_a, plan.cells_z), (rows, 8, depth)]
    outs += [(max(1, SWEEPS * plan.sides), ring, depth), (chunks, 8, LANES)]
    tall = rows + 2 * plan.guard
    scratch = [(tall, ring, depth)] * 2 + [(slots, ring, depth), (4, tall, depth)]
    own, hal, side_rows, force = call(
        sweeps_kernel,
        plan,
        outs,
        scratch,
        10**9,
        10**7,
        (potential, potential_other, density, density_other, *factors),
    )

    core, messenger = 0, plan.n_ax - 1

    def send(value, perm):
        return lax.ppermute(value, AXES, perm)

    landed = []
    if plan.sides == 1:
        landed.append(send(side_rows, plan.pairs(core, lambda r, a: (1 - r, a))))
    elif plan.sides == 2:
        down = plan.pairs(core, lambda r, a: (r - 1, a) if r > 0 else None)
        up = plan.pairs(core, lambda r, a: (r + 1, a) if r + 1 < plan.n_rad else None)
        landed.append(send(side_rows[SWEEPS:], down))
        landed.append(send(side_rows[:SWEEPS], up))
    packed = (rows // 2, 8, depth)
    even, odd = call(
        turn_kernel, plan, [packed] * 2, [(rows, 8, depth)], 10**5, 10**6, (hal, *landed)
    )
    landed.append(send(even, plan.pairs(core, lambda r, a: (r, a ^ 1))))
    landed.append(send(odd, plan.pairs(core, lambda r, a: (r, (a + 1 - 2 * (1 - a % 2)) % plan.n_ang))))

    for axis, count in ((0, plan.n_rad), (1, plan.n_ang)):
        step = 1
        while step < count:
            moved = lambda r, a, step=step: (r ^ step, a) if axis == 0 else (r, a ^ step)
            force = force + send(force, plan.pairs(messenger, moved))
            step *= 2

    hand_on = [(0, messenger)]
    handed = [lax.ppermute(value, "ax", hand_on) for value in landed]
    force = force + lax.ppermute(force, "ax", [(messenger, 0)])
    (final,) = call(
        final_kernel,
        plan,
        [(rows, plan.cells_a, plan.cells_z)],
        [],
        10**5,
        10**6,
        (own, *landed, *handed),
    )
    devices = plan.n_rad * plan.n_ang * plan.n_ax
    share = plan.atoms // devices
    rank = plan.device(*(lax.axis_index(name) for name in AXES))
    first = rank * share
    mine = lax.dynamic_slice(force, (first // LANES, 0, first % LANES), (1, 3, share))
    return final, mine.reshape(3, share)


def solution(mesh):
    whole = P("rad", "ang", "ax")

    def run(potential, density, anchor, extent, center, charge, place):
        sizes = [mesh.shape[name] for name in AXES]
        block = [total // parts for total, parts in zip(potential.shape, sizes)]
        plan = Plan(mesh, block, charge.shape[0])
        return jax.shard_map(
            functools.partial(shards, plan),
            mesh=mesh,
            in_specs=(whole, whole, P(), P(), P(), P(), P()),
            out_specs=(whole, P(None, AXES)),
            check_vma=False,
        )(potential, density, anchor, extent, center, charge, place)

    return run
```

time: 98.7 us -> 40.1 us (0.41)
  blocking collectives: 39.1 us -> 0 us
  starting transfers between devices: 34.3 us -> 23.4 us
  other arithmetic: 6.86 us -> 0.02 us
  local copies, waits for them, and re-layouts: 10.3 us -> 4.67 us
  Pallas kernels: 0 us -> 3.58 us
    unnamed x1 -> x0, blocking collectives: 39.1 us -> none
    ppermute x18 -> x13, starting transfers between devices: 34.3 us -> 23.4 us  [the longest x7 16.9 us: send(): return lax.ppermute(value, AXES, perm)]
    gather x7 -> x0, local copies, waits for them, and re-layouts: 5.49 us -> none  [the longest x2 1.67 us: shards(): start_ang = (box_anchor[1, picked] + offset_ang[picked]) * ang_cells]
    pallas_call x0 -> x4, Pallas kernels: none -> 3.58 us  [call(): pl.pallas_call(functools.partial(kernel, plan), out_shape=[jax.ShapeDtype...]
    slice x10 -> x0, local copies, waits for them, and re-layouts: 2.43 us -> none  [the longest x6 1.33 us: with_halo(): lax.slice_in_dim(block, 0, width, axis=dim)]
    unnamed x18 -> x14, local copies, waits for them, and re-layouts: 1.73 us -> 4.02 us
    add x6 -> x5, other arithmetic: 2.26 us -> 0.02 us  [the longest x4 0.02 us: shards(): force = force + send(force, plan.pairs(messenger, moved))]
    scatter-add x1 -> x0, other arithmetic: 1.43 us -> none  [shards(): picked = jnp.nonzero(covered, size=SLOTS, fill_value=0)[0].astype(jnp.int32)]
  transfers between devices with their start and end apart: 18 -> 13, of which waited for: 8 -> 3; matrix products, arithmetic and copies ran while one was open for 12% -> 2% of each run, Pallas kernels for 0% -> 1%
where the time goes in v1:
time: 40.1 us; the launch traced here: 39.6 us
  starting transfers between devices  23.4 us (58%)
  waiting for transfers between devices  7.06 us (18%)
  local copies, waits for them, and re-layouts  4.67 us (12%)
  Pallas kernels  3.58 us (9%)
  between operations  0.87 us (2%)
    ppermute x7, starting transfers between devices, send(): return lax.ppermute(value, AXES, perm)  16.9 us
    ppermute x3, starting transfers between devices, shards(): handed = [lax.ppermute(value, 'ax', hand_on) for value in landed]  4.66 us
    unnamed x14, local copies, waits for them, and re-layouts  4.02 us
    pallas_call x4, Pallas kernels, call(): pl.pallas_call(functools.partial(kernel, plan), out_shape=[jax.ShapeDtype...  3.58 us
    ppermute x1, waiting for transfers between devices, shards(): force = force + lax.ppermute(force, 'ax', [(messenger, 0)])  3.44 us
    ppermute x7, waiting for transfers between devices, send(): return lax.ppermute(value, AXES, perm)  3.39 us
    ppermute x1, starting transfers between devices, shards(): force = force + lax.ppermute(force, 'ax', [(messenger, 0)])  1.29 us
  transfers between devices with their start and end apart: 13, of which 3 were waited for; matrix products, arithmetic and copies ran while one was open for 2% of the time, Pallas kernels for 1%

profile of v1, /device:TPU:0, one launch (start us, length us, event | category | flops | bytes accessed | tf_op | source)
XLA Modules:
  0.0 39.6 jit_solution(1198989992041215559)
XLA Ops:
  0.6 0.5 %collective-permute-start = (f32[16,48,128]{2,1,0:T(8,128)}, f32[16,48,128]{2,1,0:T(8,128)S(1)}, u32[]{:S(2)}, u32[]{:S(2)}) collective-permute-start(f32[16,48,128]{2,1,0:T(8,128)} %pot_own.1), channel_id=1, source_target_pairs={{0,1},{1,0},{2,3},{3,2},{4,5},{5,4},{6,7},{7,6},{8,9},{9,8},{10,11... | collective-permute-start | bytes 1179656 | tf_op jit(solution)/shard_map/ppermute | solution.py:314
  1.3 0.6 %copy-done.3 = f32[128]{0:T(128)S(1)} copy-done((f32[128]{0:T(128)S(1)}, f32[128]{0:T(128)}, u32[]{:S(2)}) %copy-start.3) | copy-done | bytes 536
  1.9 0.7 %copy-done.1 = s32[3,128]{1,0:T(4,128)S(1)} copy-done((s32[3,128]{1,0:T(4,128)S(1)}, s32[3,128]{1,0:T(4,128)}, u32[]{:S(2)}) %copy-start.1) | copy-done | bytes 1560
  2.6 0.7 %copy-done.2 = f32[3,128]{1,0:T(4,128)S(1)} copy-done((f32[3,128]{1,0:T(4,128)S(1)}, f32[3,128]{1,0:T(4,128)}, u32[]{:S(2)}) %copy-start.2) | copy-done | bytes 1560
  3.3 0.3 shard_map.86
  3.7 1.0 %copy-done.5 = f32[16,48,128]{2,1,0:T(8,128)S(1)} copy-done((f32[16,48,128]{2,1,0:T(8,128)S(1)}, f32[16,48,128]{2,1,0:T(8,128)}, u32[]{:S(2)}) %copy-start.5) | copy-done | bytes 393240
  4.6 1.0 %copy-done.6 = f32[16,48,128]{2,1,0:T(8,128)S(1)} copy-done((f32[16,48,128]{2,1,0:T(8,128)S(1)}, f32[16,48,128]{2,1,0:T(8,128)}, u32[]{:S(2)}) %copy-start.6) | copy-done | bytes 393240
  5.6 2.4 %shard_map.87 = (f32[16,48,128]{2,1,0:T(8,128)S(1)}, f32[16,8,256]{2,1,0:T(8,128)S(1)}, f32[3,56,256]{2,1,0:T(8,128)S(1)}, f32[1,8,128]{2,1,0:T(8,128)S(1)}) custom-call(f32[16,48,128]{2,1,0:T(8,128)S(1)} %copy-done.5, f32[16,48,128]{2,1,0:T(8,128)S(1)} %collective-permute-done.pot_other, f32[16,48,128]{2,1,0:T(8,128)S(1)} %copy-done.6, ...), custom_call_target="tpu_custom_call" | custom-call | flops 1000000000 | bytes 10000000 | tf_op jit(solution)/shard_map/pallas_call | solution.py:299
  8.1 4.8 %collective-permute-start.2 = (f32[3,56,256]{2,1,0:T(8,128)S(1)}, f32[3,56,256]{2,1,0:T(8,128)S(1)}, u32[]{:S(2)}, u32[]{:S(2)}) collective-permute-start(f32[3,56,256]{2,1,0:T(8,128)S(1)} %get-tuple-element.15), channel_id=1, source_target_pairs={{0,16},{2,18},{4,20},{6,22},{8,24},{10,26},{12,28},{14,30},{16,0},... | collective-permute-start | bytes 516104 | tf_op jit(solution)/shard_map/ppermute | solution.py:342
  12.9 3.4 %collective-permute-done.2.refs_1_ = f32[3,56,256]{2,1,0:T(8,128)S(1)} collective-permute-done((f32[3,56,256]{2,1,0:T(8,128)S(1)}, f32[3,56,256]{2,1,0:T(8,128)S(1)}, u32[]{:S(2)}, u32[]{:S(2)}) %collective-permute-start.2) | collective-permute-done | bytes 172064 | tf_op jit(solution)/shard_map/ppermute | solution.py:342
  16.3 3.9 %collective-permute-start.3 = (f32[8,8,256]{2,1,0:T(8,128)S(1)}, f32[8,8,256]{2,1,0:T(8,128)S(1)}, u32[]{:S(2)}, u32[]{:S(2)}) collective-permute-start(f32[8,8,256]{2,1,0:T(8,128)S(1)} %get-tuple-element.17), channel_id=1, source_target_pairs={{0,2},{2,0},{4,6},{6,4},{8,10},{10,8},{12,14},{14,12},{16,18},{18,... | collective-permute-start | bytes 196616 | tf_op jit(solution)/shard_map/ppermute | solution.py:342
  20.3 5.5 %collective-permute-start.4 = (f32[8,8,256]{2,1,0:T(8,128)S(1)}, f32[8,8,256]{2,1,0:T(8,128)S(1)}, u32[]{:S(2)}, u32[]{:S(2)}) collective-permute-start(f32[8,8,256]{2,1,0:T(8,128)S(1)} %get-tuple-element.18), channel_id=1, source_target_pairs={{0,14},{2,4},{4,2},{6,8},{8,6},{10,12},{12,10},{14,0},{16,30},{18,... | collective-permute-start | bytes 196616 | tf_op jit(solution)/shard_map/ppermute | solution.py:342
  25.7 1.3 %collective-permute-start.5 = (f32[3,56,256]{2,1,0:T(8,128)S(1)}, f32[3,56,256]{2,1,0:T(8,128)S(1)}, u32[]{:S(2)}, u32[]{:S(2)}) collective-permute-start(f32[3,56,256]{2,1,0:T(8,128)S(1)} %collective-permute-done.2.refs_1_), channel_id=1, source_target_pairs={{0,1},{2,3},{4,5},{6,7},{8,9},{10,11},{12,13},{14,15},{16,17},{18,... | collective-permute-start | bytes 516104 | tf_op jit(solution)/shard_map/ppermute | solution.py:367
  27.0 0.7 %collective-permute-start.8 = (f32[1,8,128]{2,1,0:T(8,128)S(1)}, f32[1,8,128]{2,1,0:T(8,128)S(1)}, u32[]{:S(2)}, u32[]{:S(2)}) collective-permute-start(f32[1,8,128]{2,1,0:T(8,128)S(1)} %get-tuple-element.19), channel_id=1, source_target_pairs={{1,17},{3,19},{5,21},{7,23},{9,25},{11,27},{13,29},{15,31},{17,1},... | collective-permute-start | bytes 12296 | tf_op jit(solution)/shard_map/ppermute | solution.py:342
  27.7 0.7 %collective-permute-start.9 = (f32[1,8,128]{2,1,0:T(8,128)S(1)}, f32[1,8,128]{2,1,0:T(8,128)S(1)}, u32[]{:S(2)}, u32[]{:S(2)}) collective-permute-start(f32[1,8,128]{2,1,0:T(8,128)S(1)} %add.30), channel_id=1, source_target_pairs={{1,3},{3,1},{5,7},{7,5},{9,11},{11,9},{13,15},{15,13},{17,19},{19,... | collective-permute-start | bytes 12296 | tf_op jit(solution)/shard_map/ppermute | solution.py:342
  28.4 0.7 %collective-permute-start.10 = (f32[1,8,128]{2,1,0:T(8,128)S(1)}, f32[1,8,128]{2,1,0:T(8,128)S(1)}, u32[]{:S(2)}, u32[]{:S(2)}) collective-permute-start(f32[1,8,128]{2,1,0:T(8,128)S(1)} %add.31), channel_id=1, source_target_pairs={{1,5},{3,7},{5,1},{7,3},{9,13},{11,15},{13,9},{15,11},{17,21},{19,... | collective-permute-start | bytes 12296 | tf_op jit(solution)/shard_map/ppermute | solution.py:342
  29.1 0.7 %collective-permute-start.11 = (f32[1,8,128]{2,1,0:T(8,128)S(1)}, f32[1,8,128]{2,1,0:T(8,128)S(1)}, u32[]{:S(2)}, u32[]{:S(2)}) collective-permute-start(f32[1,8,128]{2,1,0:T(8,128)S(1)} %add.32), channel_id=1, source_target_pairs={{1,9},{3,11},{5,13},{7,15},{9,1},{11,3},{13,5},{15,7},{17,25},{19,... | collective-permute-start | bytes 12296 | tf_op jit(solution)/shard_map/ppermute | solution.py:342
  29.8 1.3 %collective-permute-start.12 = (f32[1,8,128]{2,1,0:T(8,128)S(1)}, f32[1,8,128]{2,1,0:T(8,128)S(1)}, u32[]{:S(2)}, u32[]{:S(2)}) collective-permute-start(f32[1,8,128]{2,1,0:T(8,128)S(1)} %add.33), channel_id=1, source_target_pairs={{1,0},{3,2},{5,4},{7,6},{9,8},{11,10},{13,12},{15,14},{17,16},{19,... | collective-permute-start | bytes 12296 | tf_op jit(solution)/shard_map/ppermute | solution.py:368
  31.1 3.4 %collective-permute-done.12 = f32[1,8,128]{2,1,0:T(8,128)S(1)} collective-permute-done((f32[1,8,128]{2,1,0:T(8,128)S(1)}, f32[1,8,128]{2,1,0:T(8,128)S(1)}, u32[]{:S(2)}, u32[]{:S(2)}) %collective-permute-start.12) | collective-permute-done | bytes 4128 | tf_op jit(solution)/shard_map/ppermute | solution.py:368
  34.6 2.1 %collective-permute-start.6 = (f32[8,8,256]{2,1,0:T(8,128)S(1)}, f32[8,8,256]{2,1,0:T(8,128)S(1)}, u32[]{:S(2)}, u32[]{:S(2)}) collective-permute-start(f32[8,8,256]{2,1,0:T(8,128)S(1)} %collective-permute-done.3.refs_2_), channel_id=1, source_target_pairs={{0,1},{2,3},{4,5},{6,7},{8,9},{10,11},{12,13},{14,15},{16,17},{18,... | collective-permute-start | bytes 196616 | tf_op jit(solution)/shard_map/ppermute | solution.py:367
  36.6 1.3 %collective-permute-start.7 = (f32[8,8,256]{2,1,0:T(8,128)S(1)}, f32[8,8,256]{2,1,0:T(8,128)S(1)}, u32[]{:S(2)}, u32[]{:S(2)}) collective-permute-start(f32[8,8,256]{2,1,0:T(8,128)S(1)} %collective-permute-done.4.refs_3_), channel_id=1, source_target_pairs={{0,1},{2,3},{4,5},{6,7},{8,9},{10,11},{12,13},{14,15},{16,17},{18,... | collective-permute-start | bytes 196616 | tf_op jit(solution)/shard_map/ppermute | solution.py:367
  37.9 0.7 %dynamic-slice_bitcast_fusion = f32[3,4]{1,0:T(4,128)} fusion(f32[1,8,128]{2,1,0:T(8,128)S(1)} %add.34, s32[]{:T(128)S(6)} %select_n.14), kind=kLoop, calls=%fused_computation | loop fusion | bytes 100 | tf_op jit(solution)/shard_map/reshape | solution.py:383
  38.6 0.2 collective-permute-done.7.refs_6_
  38.8 0.8 %shard_map.89 = f32[16,48,128]{2,1,0:T(8,128)} custom-call(f32[16,48,128]{2,1,0:T(8,128)S(1)} %get-tuple-element.14.refs_0_, f32[3,56,256]{2,1,0:T(8,128)S(1)} %collective-permute-done.2.refs_1_, f32[8,8,256]{2,1,0:T(8,128)S(1)} %collective-permute-done.3.refs_2_, f32[8,8,256]{2,1,0:T(8,128)S(1)} %collective-permute-done.4.refs_3_, ...), custom_call_target="tpu_custom_call" | custom-call | flops 100000 | bytes 1000000 | tf_op jit(solution)/shard_map/pallas_call | solution.py:299
  (26 shorter events, 0.3 us)
Async XLA Ops:
  0.6 0.7 %copy-start = (s32[3,128]{1,0:T(4,128)S(1)}, s32[3,128]{1,0:T(4,128)}, u32[]{:S(2)}) copy-start(s32[3,128]{1,0:T(4,128)} %anchor.1) | copy-start | bytes 4612
  0.6 3.0 %collective-permute-start = (f32[16,48,128]{2,1,0:T(8,128)}, f32[16,48,128]{2,1,0:T(8,128)S(1)}, u32[]{:S(2)}, u32[]{:S(2)}) collective-permute-start(f32[16,48,128]{2,1,0:T(8,128)} %pot_own.1), channel_id=1, source_target_pairs={{0,1},{1,0},{2,3},{3,2},{4,5},{5,4},{6,7},{7,6},{8,9},{9,8},{10,11... | collective-permute-start | bytes 1179656 | tf_op jit(solution)/shard_map/ppermute | solution.py:314
  1.2 2.5 %collective-permute-start.1 = (f32[16,48,128]{2,1,0:T(8,128)}, f32[16,48,128]{2,1,0:T(8,128)S(1)}, u32[]{:S(2)}, u32[]{:S(2)}) collective-permute-start(f32[16,48,128]{2,1,0:T(8,128)} %rho_own.1), channel_id=1, source_target_pairs={{0,1},{1,0},{2,3},{3,2},{4,5},{5,4},{6,7},{7,6},{8,9},{9,8},{10,11... | collective-permute-start | bytes 1179656 | tf_op jit(solution)/shard_map/ppermute | solution.py:315
  1.2 0.7 %copy-start.3 = (f32[128]{0:T(128)S(1)}, f32[128]{0:T(128)}, u32[]{:S(2)}) copy-start(f32[128]{0:T(128)} %param.12) | copy-start | bytes 1540
  1.2 0.7 %copy-start.4 = (s32[128]{0:T(128)S(1)}, s32[128]{0:T(128)}, u32[]{:S(2)}) copy-start(s32[128]{0:T(128)} %param.13) | copy-start | bytes 1540
  1.9 0.7 %copy-start.1 = (s32[3,128]{1,0:T(4,128)S(1)}, s32[3,128]{1,0:T(4,128)}, u32[]{:S(2)}) copy-start(s32[3,128]{1,0:T(4,128)} %extent.1) | copy-start | bytes 4612
  2.6 0.7 %copy-start.2 = (f32[3,128]{1,0:T(4,128)S(1)}, f32[3,128]{1,0:T(4,128)}, u32[]{:S(2)}) copy-start(f32[3,128]{1,0:T(4,128)} %center.1) | copy-start | bytes 4612
  3.6 1.0 %copy-start.5 = (f32[16,48,128]{2,1,0:T(8,128)S(1)}, f32[16,48,128]{2,1,0:T(8,128)}, u32[]{:S(2)}) copy-start(f32[16,48,128]{2,1,0:T(8,128)} %pot_own.1) | copy-start | bytes 1179652
  4.6 1.0 %copy-start.6 = (f32[16,48,128]{2,1,0:T(8,128)S(1)}, f32[16,48,128]{2,1,0:T(8,128)}, u32[]{:S(2)}) copy-start(f32[16,48,128]{2,1,0:T(8,128)} %rho_own.1) | copy-start | bytes 1179652
  8.1 8.2 %collective-permute-start.2 = (f32[3,56,256]{2,1,0:T(8,128)S(1)}, f32[3,56,256]{2,1,0:T(8,128)S(1)}, u32[]{:S(2)}, u32[]{:S(2)}) collective-permute-start(f32[3,56,256]{2,1,0:T(8,128)S(1)} %get-tuple-element.15), channel_id=1, source_target_pairs={{0,16},{2,18},{4,20},{6,22},{8,24},{10,26},{12,28},{14,30},{16,0},... | collective-permute-start | bytes 516104 | tf_op jit(solution)/shard_map/ppermute | solution.py:342
  16.3 18.3 %collective-permute-start.3 = (f32[8,8,256]{2,1,0:T(8,128)S(1)}, f32[8,8,256]{2,1,0:T(8,128)S(1)}, u32[]{:S(2)}, u32[]{:S(2)}) collective-permute-start(f32[8,8,256]{2,1,0:T(8,128)S(1)} %get-tuple-element.17), channel_id=1, source_target_pairs={{0,2},{2,0},{4,6},{6,4},{8,10},{10,8},{12,14},{14,12},{16,18},{18,... | collective-permute-start | bytes 196616 | tf_op jit(solution)/shard_map/ppermute | solution.py:342
  20.3 16.4 %collective-permute-start.4 = (f32[8,8,256]{2,1,0:T(8,128)S(1)}, f32[8,8,256]{2,1,0:T(8,128)S(1)}, u32[]{:S(2)}, u32[]{:S(2)}) collective-permute-start(f32[8,8,256]{2,1,0:T(8,128)S(1)} %get-tuple-element.18), channel_id=1, source_target_pairs={{0,14},{2,4},{4,2},{6,8},{8,6},{10,12},{12,10},{14,0},{16,30},{18,... | collective-permute-start | bytes 196616 | tf_op jit(solution)/shard_map/ppermute | solution.py:342
  25.7 13.1 %collective-permute-start.5 = (f32[3,56,256]{2,1,0:T(8,128)S(1)}, f32[3,56,256]{2,1,0:T(8,128)S(1)}, u32[]{:S(2)}, u32[]{:S(2)}) collective-permute-start(f32[3,56,256]{2,1,0:T(8,128)S(1)} %collective-permute-done.2.refs_1_), channel_id=1, source_target_pairs={{0,1},{2,3},{4,5},{6,7},{8,9},{10,11},{12,13},{14,15},{16,17},{18,... | collective-permute-start | bytes 516104 | tf_op jit(solution)/shard_map/ppermute | solution.py:367
  27.0 0.7 %collective-permute-start.8 = (f32[1,8,128]{2,1,0:T(8,128)S(1)}, f32[1,8,128]{2,1,0:T(8,128)S(1)}, u32[]{:S(2)}, u32[]{:S(2)}) collective-permute-start(f32[1,8,128]{2,1,0:T(8,128)S(1)} %get-tuple-element.19), channel_id=1, source_target_pairs={{1,17},{3,19},{5,21},{7,23},{9,25},{11,27},{13,29},{15,31},{17,1},... | collective-permute-start | bytes 12296 | tf_op jit(solution)/shard_map/ppermute | solution.py:342
  27.7 0.7 %collective-permute-start.9 = (f32[1,8,128]{2,1,0:T(8,128)S(1)}, f32[1,8,128]{2,1,0:T(8,128)S(1)}, u32[]{:S(2)}, u32[]{:S(2)}) collective-permute-start(f32[1,8,128]{2,1,0:T(8,128)S(1)} %add.30), channel_id=1, source_target_pairs={{1,3},{3,1},{5,7},{7,5},{9,11},{11,9},{13,15},{15,13},{17,19},{19,... | collective-permute-start | bytes 12296 | tf_op jit(solution)/shard_map/ppermute | solution.py:342
  28.4 0.7 %collective-permute-start.10 = (f32[1,8,128]{2,1,0:T(8,128)S(1)}, f32[1,8,128]{2,1,0:T(8,128)S(1)}, u32[]{:S(2)}, u32[]{:S(2)}) collective-permute-start(f32[1,8,128]{2,1,0:T(8,128)S(1)} %add.31), channel_id=1, source_target_pairs={{1,5},{3,7},{5,1},{7,3},{9,13},{11,15},{13,9},{15,11},{17,21},{19,... | collective-permute-start | bytes 12296 | tf_op jit(solution)/shard_map/ppermute | solution.py:342
  29.1 0.7 %collective-permute-start.11 = (f32[1,8,128]{2,1,0:T(8,128)S(1)}, f32[1,8,128]{2,1,0:T(8,128)S(1)}, u32[]{:S(2)}, u32[]{:S(2)}) collective-permute-start(f32[1,8,128]{2,1,0:T(8,128)S(1)} %add.32), channel_id=1, source_target_pairs={{1,9},{3,11},{5,13},{7,15},{9,1},{11,3},{13,5},{15,7},{17,25},{19,... | collective-permute-start | bytes 12296 | tf_op jit(solution)/shard_map/ppermute | solution.py:342
  29.8 4.8 %collective-permute-start.12 = (f32[1,8,128]{2,1,0:T(8,128)S(1)}, f32[1,8,128]{2,1,0:T(8,128)S(1)}, u32[]{:S(2)}, u32[]{:S(2)}) collective-permute-start(f32[1,8,128]{2,1,0:T(8,128)S(1)} %add.33), channel_id=1, source_target_pairs={{1,0},{3,2},{5,4},{7,6},{9,8},{11,10},{13,12},{15,14},{17,16},{19,... | collective-permute-start | bytes 12296 | tf_op jit(solution)/shard_map/ppermute | solution.py:368
  34.6 4.0 %collective-permute-start.6 = (f32[8,8,256]{2,1,0:T(8,128)S(1)}, f32[8,8,256]{2,1,0:T(8,128)S(1)}, u32[]{:S(2)}, u32[]{:S(2)}) collective-permute-start(f32[8,8,256]{2,1,0:T(8,128)S(1)} %collective-permute-done.3.refs_2_), channel_id=1, source_target_pairs={{0,1},{2,3},{4,5},{6,7},{8,9},{10,11},{12,13},{14,15},{16,17},{18,... | collective-permute-start | bytes 196616 | tf_op jit(solution)/shard_map/ppermute | solution.py:367
  36.6 2.2 %collective-permute-start.7 = (f32[8,8,256]{2,1,0:T(8,128)S(1)}, f32[8,8,256]{2,1,0:T(8,128)S(1)}, u32[]{:S(2)}, u32[]{:S(2)}) collective-permute-start(f32[8,8,256]{2,1,0:T(8,128)S(1)} %collective-permute-done.4.refs_3_), channel_id=1, source_target_pairs={{0,1},{2,3},{4,5},{6,7},{8,9},{10,11},{12,13},{14,15},{16,17},{18,... | collective-permute-start | bytes 196616 | tf_op jit(solution)/shard_map/ppermute | solution.py:367

commit v2 on v1

--- a/solution.py
+++ b/solution.py
@@ -40,6 +40,7 @@
         self.sides = 0 if self.n_rad == 1 else 1 if self.n_rad == 2 else 2
         self.slots = self.cells_r + SWEEPS * self.sides
         self.guard = SWEEPS + 1
+        self.side_tiles = self.sides * SWEEPS * (self.ring // 8)
 
     def sign(self, side, rad):
         if self.sides == 1:
@@ -57,17 +58,28 @@
     def device(self, rad, ang, ax):
         return (rad * self.n_ang + ang) * self.n_ax + ax
 
-    def pairs(self, core, move):
+    def moves(self, move):
         found = []
         for rad in range(self.n_rad):
             for ang in range(self.n_ang):
                 target = move(rad, ang)
                 if target is not None:
-                    found.append((self.device(rad, ang, core), self.device(*target, core)))
+                    for ax in range(self.n_ax):
+                        found.append((self.device(rad, ang, ax), self.device(*target, 1 - ax)))
         return found
 
 
-def factors_kernel(plan, anchor, extent, center, charge, place, z_out, a_out, r_out):
+def factors_kernel(plan, *refs):
+    sources, (z_out, a_out, r_out, pot_out, rho_out), held = refs[:7], refs[7:12], refs[12:17]
+    copies = [
+        pltpu.make_async_copy(source, target, refs[17].at[k])
+        for k, (source, target) in enumerate(zip(sources, (*held, pot_out, rho_out)))
+    ]
+    for copy in copies:
+        copy.start()
+    for copy in copies[:5]:
+        copy.wait()
+    anchor, extent, center, charge, place = held
     rad, ang, ax = (lax.axis_index(name) for name in AXES)
     width_r, width_a, width_z = plan.cells_r / 3.0, plan.cells_a / 3.0, plan.cells_z / 3.0
     amplitude = 1.0 / math.sqrt(width_a * width_z / width_r)
@@ -138,6 +150,8 @@
         chunk(0, 0)
     else:
         lax.fori_loop(0, plan.chunks, chunk, 0)
+    for copy in copies[5:]:
+        copy.wait()
 
 
 def sweeps_kernel(
@@ -152,13 +166,12 @@
     own_out,
     hal_out,
     rad_out,
-    force_out,
     first,
     second,
     grown,
     coef,
 ):
-    rad, ax = lax.axis_index("rad"), lax.axis_index("ax")
+    rad = lax.axis_index("rad")
     guard, rows, ring, depth = plan.guard, plan.cells_r, plan.ring, plan.total_z
     weights = sweep_weights(SWEEPS)
 
@@ -197,6 +210,12 @@
             total += charge
         return (1.0 - weight) * center + (weight * inverse) * total
 
+    def send_row(slot, fresh):
+        tiles = ring // 8
+        for tile in range(tiles - 1):
+            rad_out[slot * tiles + tile] = fresh[8 * tile : 8 * tile + 8, plan.cells_z :]
+        rad_out[slot * tiles + tiles - 1] = fresh[plan.cells_a :, : plan.cells_z]
+
     source, target = first, second
     for sweep in range(SWEEPS):
         last = sweep == SWEEPS - 1
@@ -205,7 +224,7 @@
             if last:
                 grown[row] = fresh
                 own_out[row] = fresh[: plan.cells_a, : plan.cells_z]
-                hal_out[row] = fresh[plan.cells_a :, :]
+                hal_out[row] = fresh[plan.cells_a :, plan.cells_z :]
             else:
                 target[guard + row] = fresh
         for side in range(plan.sides):
@@ -215,71 +234,76 @@
                 if last:
                     slot = SWEEPS * side + step - 1
                     grown[rows + slot] = fresh
-                    rad_out[slot] = fresh
+                    send_row(slot, fresh)
                 else:
                     target[place] = fresh
         source, target = target, source
 
-    force_out[...] = jnp.zeros_like(force_out)
-
-    @pl.when(ax == plan.n_ax - 1)
-    def _():
-        def chunk(number, carry):
-            spread = jnp.dot(
-                grown[...].reshape(plan.slots * ring, depth),
-                z_fac[number],
-                precision=highest,
-                preferred_element_type=jnp.float32,
-            )
-            sums = [jnp.zeros((ring, LANES), jnp.float32) for _ in range(3)]
-            for slot in range(plan.slots):
-                piece = spread[slot * ring : (slot + 1) * ring]
-                for k, part in enumerate((piece[:, :LANES], piece[:, :LANES], piece[:, LANES:])):
-                    sums[k] += r_fac[number, k, pl.ds(slot, 1), :] * part
-            for k, turn in enumerate((0, 1, 0)):
-                force_out[number, pl.ds(k, 1), :] = jnp.sum(
-                    a_fac[number, turn] * sums[k], axis=0, keepdims=True
-                )
-            return carry
-
-        if plan.chunks == 1:
-            chunk(0, 0)
-        else:
-            lax.fori_loop(0, plan.chunks, chunk, 0)
+    force_base = plan.side_tiles
+
+    def chunk(number, carry):
+        spread = jnp.dot(
+            grown[...].reshape(plan.slots * ring, depth),
+            z_fac[number],
+            precision=highest,
+            preferred_element_type=jnp.float32,
+        )
+        sums = [jnp.zeros((ring, LANES), jnp.float32) for _ in range(3)]
+        for slot in range(plan.slots):
+            piece = spread[slot * ring : (slot + 1) * ring]
+            for k, part in enumerate((piece[:, :LANES], piece[:, :LANES], piece[:, LANES:])):
+                sums[k] += r_fac[number, k, pl.ds(slot, 1), :] * part
+        total = [
+            jnp.sum(a_fac[number, turn] * sums[k], axis=0, keepdims=True)
+            for k, turn in enumerate((0, 1, 0))
+        ]
+        total.append(jnp.zeros((5, LANES), jnp.float32))
+        rad_out[force_base + number] = jnp.concatenate(total, axis=0)
+        return carry
+
+    if plan.chunks == 1:
+        chunk(0, 0)
+    else:
+        lax.fori_loop(0, plan.chunks, chunk, 0)
 
 
 def turn_kernel(plan, *refs):
-    hal, landed = refs[0], refs[1 : 1 + plan.sides]
-    even_out, odd_out, held = refs[1 + plan.sides :]
+    hal, landed, forces = refs[0], refs[1 : 1 + plan.sides], refs[1 + plan.sides : -3]
+    even_out, odd_out, held = refs[-3:]
     rad, ang = lax.axis_index("rad"), lax.axis_index("ang")
+    width = plan.cells_z
     held[...] = hal[...]
+    tiles = plan.ring // 8
     for side in range(plan.sides):
         for step in range(1, SWEEPS + 1):
             row = plan.landing_row(side, rad, step)
-            held[row] = held[row] + landed[side][step - 1, plan.cells_a :, :]
-    low_half = lax.broadcasted_iota(jnp.int32, (8, plan.total_z), 0) < 4
-    is_even = (lax.broadcasted_iota(jnp.int32, (8, plan.total_z), 0) * 0 + ang) % 2 == 0
-    for tile in range(plan.cells_r // 2):
+            held[row] = held[row] + landed[side][step * tiles - 1]
+    low_half = lax.broadcasted_iota(jnp.int32, (8, width), 0) < 4
+    is_even = (lax.broadcasted_iota(jnp.int32, (8, width), 0) * 0 + ang) % 2 == 0
+    pairs = plan.cells_r // 2
+    for tile in range(pairs):
         front, back = held[2 * tile], held[2 * tile + 1]
         above = jnp.where(low_half, front, pltpu.roll(back, 4, 0))
         below = jnp.where(low_half, pltpu.roll(front, 4, 0), back)
         even_out[tile] = jnp.where(is_even, above, below)
         odd_out[tile] = jnp.where(is_even, below, above)
+    for number in range(plan.chunks):
+        total = forces[0][number - plan.chunks + forces[0].shape[0]]
+        if len(forces) > 1:
+            total = total + forces[1][number - plan.chunks + forces[1].shape[0]]
+        even_out[pairs + number] = total
 
 
 def final_kernel(plan, *refs):
-    own, here, there, out = refs[0], refs[1 : 3 + plan.sides], refs[3 + plan.sides : -1], refs[-1]
+    own, landed, even_in, odd_in, out = refs[0], refs[1 : 1 + plan.sides], *refs[-3:]
     rad, ang = lax.axis_index("rad"), lax.axis_index("ang")
     width = plan.cells_z
-
-    def landed(number, index):
-        return here[number][index][:, :width] + there[number][index][:, width:]
-
     low_half = lax.broadcasted_iota(jnp.int32, (8, width), 0) < 4
     is_even = (lax.broadcasted_iota(jnp.int32, (8, width), 0) * 0 + ang) % 2 == 0
     top = plan.cells_a - 8
+    tiles = plan.ring // 8
     for tile in range(plan.cells_r // 2):
-        even, odd = landed(plan.sides, tile), landed(plan.sides + 1, tile)
+        even, odd = even_in[tile], odd_in[tile]
         above, below = jnp.where(is_even, even, odd), jnp.where(is_even, odd, even)
         for half in range(2):
             row = 2 * tile + half
@@ -291,17 +315,18 @@
     for side in range(plan.sides):
         for step in range(1, SWEEPS + 1):
             row = plan.landing_row(side, rad, step)
-            out[row] += landed(side, step - 1)[: plan.cells_a]
-
-
-def call(kernel, plan, outs, scratch, flops, bytes_moved, args):
+            for tile in range(tiles - 1):
+                out[row, 8 * tile : 8 * tile + 8, :] += landed[side][(step - 1) * tiles + tile]
+
+
+def call(kernel, plan, outs, scratch, flops, bytes_moved, args, spaces=None):
     in_vmem = pl.BlockSpec(memory_space=pltpu.VMEM)
     return pl.pallas_call(
         functools.partial(kernel, plan),
         out_shape=[jax.ShapeDtypeStruct(shape, jnp.float32) for shape in outs],
-        in_specs=[in_vmem] * len(args),
+        in_specs=spaces or [in_vmem] * len(args),
         out_specs=[in_vmem] * len(outs),
-        scratch_shapes=[pltpu.VMEM(shape, jnp.float32) for shape in scratch],
+        scratch_shapes=scratch,
         compiler_params=pltpu.CompilerParams(vmem_limit_bytes=24 * 2**20),
         cost_estimate=pl.CostEstimate(flops=flops, bytes_accessed=bytes_moved, transcendentals=0),
     )(*args)
@@ -309,76 +334,74 @@
 
 def shards(plan, potential, density, anchor, extent, center, charge, place):
     ring, depth, slots, chunks = plan.ring, plan.total_z, plan.slots, plan.chunks
-    rows = plan.cells_r
+    rows, width, block = plan.cells_r, plan.cells_z, potential.shape
     swap = [(0, 1), (1, 0)]
     potential_other = lax.ppermute(potential, "ax", swap)
     density_other = lax.ppermute(density, "ax", swap)
-    factors = call(
+    tables = (anchor, extent, center, charge.reshape(1, -1), place.reshape(1, -1))
+    *factors, potential, density = call(
         factors_kernel,
         plan,
-        [(chunks, depth, 2 * LANES), (chunks, 2, ring, LANES), (chunks, 3, slots, LANES)],
-        [],
+        [(chunks, depth, 2 * LANES), (chunks, 2, ring, LANES), (chunks, 3, slots, LANES)] + [block] * 2,
+        [pltpu.VMEM(table.shape, table.dtype) for table in tables] + [pltpu.SemaphoreType.DMA((7,))],
         10**6,
         10**6,
-        (anchor, extent, center, charge.reshape(1, -1), place.reshape(1, -1)),
+        (*tables, potential, density),
+        [pl.BlockSpec(memory_space=pl.ANY)] * 7,
     )
-    outs = [(rows, plan.cells_a, plan.cells_z), (rows, 8, depth)]
-    outs += [(max(1, SWEEPS * plan.sides), ring, depth), (chunks, 8, LANES)]
     tall = rows + 2 * plan.guard
     scratch = [(tall, ring, depth)] * 2 + [(slots, ring, depth), (4, tall, depth)]
-    own, hal, side_rows, force = call(
+    own, hal, sides = call(
         sweeps_kernel,
         plan,
-        outs,
-        scratch,
+        [block, (rows, 8, width), (plan.side_tiles + chunks, 8, LANES)],
+        [pltpu.VMEM(shape, jnp.float32) for shape in scratch],
         10**9,
         10**7,
         (potential, potential_other, density, density_other, *factors),
     )
 
-    core, messenger = 0, plan.n_ax - 1
-
-    def send(value, perm):
-        return lax.ppermute(value, AXES, perm)
-
-    landed = []
+    def send(value, move):
+        return lax.ppermute(value, AXES, plan.moves(move))
+
+    per_side = plan.side_tiles // max(1, plan.sides)
     if plan.sides == 1:
-        landed.append(send(side_rows, plan.pairs(core, lambda r, a: (1 - r, a))))
-    elif plan.sides == 2:
-        down = plan.pairs(core, lambda r, a: (r - 1, a) if r > 0 else None)
-        up = plan.pairs(core, lambda r, a: (r + 1, a) if r + 1 < plan.n_rad else None)
-        landed.append(send(side_rows[SWEEPS:], down))
-        landed.append(send(side_rows[:SWEEPS], up))
-    packed = (rows // 2, 8, depth)
+        landed = [send(sides, lambda r, a: (1 - r, a))]
+        forces = [sides, landed[0]]
+    else:
+        landed = []
+        force = sides[plan.side_tiles :]
+        if plan.sides == 2:
+            landed.append(send(sides[per_side : 2 * per_side], lambda r, a: (r - 1, a) if r else None))
+            last = plan.n_rad - 1
+            landed.append(send(sides[:per_side], lambda r, a: (r + 1, a) if r < last else None))
+        step = 1
+        while step < plan.n_rad:
+            force = force + send(force, lambda r, a: (r ^ step, a))
+            step *= 2
+        forces = [force]
+    pairs = rows // 2
     even, odd = call(
-        turn_kernel, plan, [packed] * 2, [(rows, 8, depth)], 10**5, 10**6, (hal, *landed)
-    )
-    landed.append(send(even, plan.pairs(core, lambda r, a: (r, a ^ 1))))
-    landed.append(send(odd, plan.pairs(core, lambda r, a: (r, (a + 1 - 2 * (1 - a % 2)) % plan.n_ang))))
-
-    for axis, count in ((0, plan.n_rad), (1, plan.n_ang)):
-        step = 1
-        while step < count:
-            moved = lambda r, a, step=step: (r ^ step, a) if axis == 0 else (r, a ^ step)
-            force = force + send(force, plan.pairs(messenger, moved))
-            step *= 2
-
-    hand_on = [(0, messenger)]
-    handed = [lax.ppermute(value, "ax", hand_on) for value in landed]
-    force = force + lax.ppermute(force, "ax", [(messenger, 0)])
-    (final,) = call(
-        final_kernel,
+        turn_kernel,
         plan,
-        [(rows, plan.cells_a, plan.cells_z)],
-        [],
+        [(pairs + chunks, 8, width), (pairs, 8, width)],
+        [pltpu.VMEM((rows, 8, width), jnp.float32)],
         10**5,
         10**6,
-        (own, *landed, *handed),
+        (hal, *landed, *forces),
     )
-    devices = plan.n_rad * plan.n_ang * plan.n_ax
-    share = plan.atoms // devices
-    rank = plan.device(*(lax.axis_index(name) for name in AXES))
-    first = rank * share
+    odd_in = send(odd, lambda r, a: (r, (a + 1 - 2 * (1 - a % 2)) % plan.n_ang))
+    even_in = send(even, lambda r, a: (r, a ^ 1))
+    force = even[pairs:] + even_in[pairs:]
+    step = 2
+    while step < plan.n_ang:
+        force = force + send(force, lambda r, a: (r, a ^ step))
+        step *= 2
+    (final,) = call(
+        final_kernel, plan, [block], [], 10**5, 10**6, (own, *landed, even_in, odd_in)
+    )
+    share = plan.atoms // (plan.n_rad * plan.n_ang * plan.n_ax)
+    first = plan.device(*(lax.axis_index(name) for name in AXES)) * share
     mine = lax.dynamic_slice(force, (first // LANES, 0, first % LANES), (1, 3, share))
     return final, mine.reshape(3, share)
 

time: 40.1 us -> 28.3 us (0.71)
  starting transfers between devices: 23.4 us -> 9.85 us
  Pallas kernels: 3.58 us -> 4.9 us
  waiting for transfers between devices: 7.06 us -> 7.95 us
    ppermute x11 -> x5, starting transfers between devices: 22.8 us -> 9.25 us  [send(): return lax.ppermute(value, AXES, plan.moves(move))]
    pallas_call x4, Pallas kernels: 3.58 us -> 4.9 us  [call(): pl.pallas_call(functools.partial(kernel, plan), out_shape=[jax.ShapeDtype...]
    ppermute x11 -> x5, waiting for transfers between devices: 7.06 us -> 7.94 us  [send(): return lax.ppermute(value, AXES, plan.moves(move))]
  transfers between devices with their start and end apart: 13 -> 7, of which waited for: 3 -> 3; matrix products, arithmetic and copies ran while one was open for 2% -> 0% of each run, Pallas kernels for 1% -> 6%
where the time goes in v2:
time: 28.3 us; the launch traced here: 28.1 us
  starting transfers between devices  9.85 us (35%)
  waiting for transfers between devices  7.95 us (28%)
  Pallas kernels  4.9 us (17%)
  local copies, waits for them, and re-layouts  4.68 us (17%)
  between operations  0.69 us (2%)
    ppermute x5, starting transfers between devices, send(): return lax.ppermute(value, AXES, plan.moves(move))  9.25 us
    ppermute x5, waiting for transfers between devices, send(): return lax.ppermute(value, AXES, plan.moves(move))  7.94 us
    pallas_call x4, Pallas kernels, call(): pl.pallas_call(functools.partial(kernel, plan), out_shape=[jax.ShapeDtype...  4.9 us
    unnamed x14, local copies, waits for them, and re-layouts  4.02 us
    reshape x1, local copies, waits for them, and re-layouts, shards(): return (final, mine.reshape(3, share))  0.65 us
  transfers between devices with their start and end apart: 7, of which 3 were waited for; matrix products, arithmetic and copies ran while one was open for 0% of the time, Pallas kernels for 6%

profile of v2, /device:TPU:0, one launch (start us, length us, event | category | flops | bytes accessed | tf_op | source)
XLA Modules:
  0.0 28.1 jit_solution(3089487740041101299)
XLA Ops:
  0.6 0.5 %collective-permute-start = (f32[16,48,128]{2,1,0:T(8,128)}, f32[16,48,128]{2,1,0:T(8,128)S(1)}, u32[]{:S(2)}, u32[]{:S(2)}) collective-permute-start(f32[16,48,128]{2,1,0:T(8,128)} %refs_5_.1), channel_id=1, source_target_pairs={{0,1},{1,0},{2,3},{3,2},{4,5},{5,4},{6,7},{7,6},{8,9},{9,8},{10,11... | collective-permute-start | bytes 1179656 | tf_op jit(solution)/shard_map/ppermute | solution.py:339
  1.2 0.1 collective-permute-start.1
  1.2 0.1 copy-done.2
  1.3 0.6 %copy-done.5 = f32[128]{0:T(128)S(1)} copy-done((f32[128]{0:T(128)S(1)}, f32[128]{0:T(128)}, u32[]{:S(2)}) %copy-start.5) | copy-done | bytes 536
  1.9 0.0 copy-done.6
  1.9 1.0 %copy-done = f32[16,48,128]{2,1,0:T(8,128)S(1)} copy-done((f32[16,48,128]{2,1,0:T(8,128)S(1)}, f32[16,48,128]{2,1,0:T(8,128)}, u32[]{:S(2)}) %copy-start) | copy-done | bytes 393240
  2.9 1.0 %copy-done.1 = f32[16,48,128]{2,1,0:T(8,128)S(1)} copy-done((f32[16,48,128]{2,1,0:T(8,128)S(1)}, f32[16,48,128]{2,1,0:T(8,128)}, u32[]{:S(2)}) %copy-start.1) | copy-done | bytes 393240
  3.9 0.7 %copy-done.3 = s32[3,128]{1,0:T(4,128)S(1)} copy-done((s32[3,128]{1,0:T(4,128)S(1)}, s32[3,128]{1,0:T(4,128)}, u32[]{:S(2)}) %copy-start.3) | copy-done | bytes 1560
  4.6 0.7 %copy-done.4 = f32[3,128]{1,0:T(4,128)S(1)} copy-done((f32[3,128]{1,0:T(4,128)S(1)}, f32[3,128]{1,0:T(4,128)}, u32[]{:S(2)}) %copy-start.4) | copy-done | bytes 1560
  5.3 0.8 %shard_map.86 = (f32[1,256,256]{2,1,0:T(8,128)S(1)}, f32[1,2,56,128]{3,2,1,0:T(8,128)S(1)}, f32[1,3,19,128]{3,2,1,0:T(8,128)S(1)}, f32[16,48,128]{2,1,0:T(8,128)S(1)}, f32[16,48,128]{2,1,0:T(8,128)S(1)}) custom-call(s32[3,128]{1,0:T(4,128)S(1)} %copy-done.2, s32[3,128]{1,0:T(4,128)S(1)} %copy-done.3, f32[3,128]{1,0:T(4,128)S(1)} %copy-done.4, ...), custom_call_target="tpu_custom_call" | custom-call | flops 1000000 | bytes 1000000 | tf_op jit(solution)/shard_map/pallas_call | solution.py:324
  6.1 0.0 collective-permute-done.1.rho_other
  6.1 3.3 %shard_map.87 = (f32[16,48,128]{2,1,0:T(8,128)S(1)}, f32[16,8,128]{2,1,0:T(8,128)S(1)}, f32[22,8,128]{2,1,0:T(8,128)S(1)}) custom-call(f32[16,48,128]{2,1,0:T(8,128)S(1)} %get-tuple-element.12.pot_own, f32[16,48,128]{2,1,0:T(8,128)S(1)} %collective-permute-done.pot_other, f32[16,48,128]{2,1,0:T(8,128)S(1)} %get-tuple-element.13.rho_own, ...), custom_call_target="tpu_custom_call" | custom-call | flops 1000000000 | bytes 10000000 | tf_op jit(solution)/shard_map/pallas_call | solution.py:324
  9.4 2.7 %collective-permute-start.2 = (f32[22,8,128]{2,1,0:T(8,128)S(1)}, f32[22,8,128]{2,1,0:T(8,128)S(1)}, u32[]{:S(2)}, u32[]{:S(2)}) collective-permute-start(f32[22,8,128]{2,1,0:T(8,128)S(1)} %get-tuple-element.18.refs_2_), channel_id=1, source_target_pairs={{0,17},{1,16},{2,19},{3,18},{4,21},{5,20},{6,23},{7,22},{8,25},{9,... | collective-permute-start | bytes 270344 | tf_op jit(solution)/shard_map/ppermute | solution.py:365
  12.0 2.8 %collective-permute-done.2.refs_1_.refs_3_ = f32[22,8,128]{2,1,0:T(8,128)S(1)} collective-permute-done((f32[22,8,128]{2,1,0:T(8,128)S(1)}, f32[22,8,128]{2,1,0:T(8,128)S(1)}, u32[]{:S(2)}, u32[]{:S(2)}) %collective-permute-start.2) | collective-permute-done | bytes 90144 | tf_op jit(solution)/shard_map/ppermute | solution.py:365
  14.8 2.0 %collective-permute-start.3 = (f32[9,8,128]{2,1,0:T(8,128)S(1)}, f32[9,8,128]{2,1,0:T(8,128)S(1)}, u32[]{:S(2)}, u32[]{:S(2)}) collective-permute-start(f32[9,8,128]{2,1,0:T(8,128)S(1)} %get-tuple-element.20), channel_id=1, source_target_pairs={{0,3},{1,2},{2,1},{3,0},{4,7},{5,6},{6,5},{7,4},{8,11},{9,10},{10,... | collective-permute-start | bytes 110600 | tf_op jit(solution)/shard_map/ppermute | solution.py:365
  16.9 3.6 %collective-permute-start.4 = (f32[8,8,128]{2,1,0:T(8,128)S(1)}, f32[8,8,128]{2,1,0:T(8,128)S(1)}, u32[]{:S(2)}, u32[]{:S(2)}) collective-permute-start(f32[8,8,128]{2,1,0:T(8,128)S(1)} %get-tuple-element.21), channel_id=1, source_target_pairs={{0,15},{1,14},{2,5},{3,4},{4,3},{5,2},{6,9},{7,8},{8,7},{9,6},{10,... | collective-permute-start | bytes 98312 | tf_op jit(solution)/shard_map/ppermute | solution.py:365
  20.4 0.0 collective-permute-done.3.refs_2_
  20.4 0.0 collective-permute-start.5
  20.5 3.0 %collective-permute-done.5 = f32[1,8,128]{2,1,0:T(8,128)S(1)} collective-permute-done((f32[1,8,128]{2,1,0:T(8,128)S(1)}, f32[1,8,128]{2,1,0:T(8,128)S(1)}, u32[]{:S(2)}, u32[]{:S(2)}) %collective-permute-start.5) | collective-permute-done | bytes 4128 | tf_op jit(solution)/shard_map/ppermute | solution.py:365
  23.5 1.0 %collective-permute-start.6 = (f32[1,8,128]{2,1,0:T(8,128)S(1)}, f32[1,8,128]{2,1,0:T(8,128)S(1)}, u32[]{:S(2)}, u32[]{:S(2)}) collective-permute-start(f32[1,8,128]{2,1,0:T(8,128)S(1)} %add.25), channel_id=1, source_target_pairs={{0,9},{1,8},{2,11},{3,10},{4,13},{5,12},{6,15},{7,14},{8,1},{9,0},... | collective-permute-start | bytes 12296 | tf_op jit(solution)/shard_map/ppermute | solution.py:365
  24.5 0.0 collective-permute-done.4.refs_3_
  24.5 0.8 %shard_map.89 = f32[16,48,128]{2,1,0:T(8,128)} custom-call(f32[16,48,128]{2,1,0:T(8,128)S(1)} %get-tuple-element.17.refs_0_, f32[22,8,128]{2,1,0:T(8,128)S(1)} %collective-permute-done.2.refs_1_.refs_3_, f32[9,8,128]{2,1,0:T(8,128)S(1)} %collective-permute-done.3.refs_2_, f32[8,8,128]{2,1,0:T(8,128)S(1)} %collective-permute-done.4.refs_3_), custom_call_target="tpu_custom_call" | custom-call | flops 100000 | bytes 1000000 | tf_op jit(solution)/shard_map/pallas_call | solution.py:324
  25.3 2.2 %collective-permute-done.6 = f32[1,8,128]{2,1,0:T(8,128)S(1)} collective-permute-done((f32[1,8,128]{2,1,0:T(8,128)S(1)}, f32[1,8,128]{2,1,0:T(8,128)S(1)}, u32[]{:S(2)}, u32[]{:S(2)}) %collective-permute-start.6) | collective-permute-done | bytes 4128 | tf_op jit(solution)/shard_map/ppermute | solution.py:365
  27.4 0.7 %dynamic-slice_bitcast_fusion = f32[3,4]{1,0:T(4,128)} fusion(f32[1,8,128]{2,1,0:T(8,128)S(1)} %add.26, s32[]{:T(128)S(6)} %select_n.14), kind=kLoop, calls=%fused_computation.1 | loop fusion | bytes 100 | tf_op jit(solution)/shard_map/reshape | solution.py:406
  (12 shorter events, 0.1 us)
Async XLA Ops:
  0.6 0.7 %copy-start.2 = (s32[3,128]{1,0:T(4,128)S(1)}, s32[3,128]{1,0:T(4,128)}, u32[]{:S(2)}) copy-start(s32[3,128]{1,0:T(4,128)} %refs_0_.1) | copy-start | bytes 4612
  0.6 5.4 %collective-permute-start = (f32[16,48,128]{2,1,0:T(8,128)}, f32[16,48,128]{2,1,0:T(8,128)S(1)}, u32[]{:S(2)}, u32[]{:S(2)}) collective-permute-start(f32[16,48,128]{2,1,0:T(8,128)} %refs_5_.1), channel_id=1, source_target_pairs={{0,1},{1,0},{2,3},{3,2},{4,5},{5,4},{6,7},{7,6},{8,9},{9,8},{10,11... | collective-permute-start | bytes 1179656 | tf_op jit(solution)/shard_map/ppermute | solution.py:339
  1.2 4.9 %collective-permute-start.1 = (f32[16,48,128]{2,1,0:T(8,128)}, f32[16,48,128]{2,1,0:T(8,128)S(1)}, u32[]{:S(2)}, u32[]{:S(2)}) collective-permute-start(f32[16,48,128]{2,1,0:T(8,128)} %refs_6_.1), channel_id=1, source_target_pairs={{0,1},{1,0},{2,3},{3,2},{4,5},{5,4},{6,7},{7,6},{8,9},{9,8},{10,11... | collective-permute-start | bytes 1179656 | tf_op jit(solution)/shard_map/ppermute | solution.py:340
  1.2 0.7 %copy-start.5 = (f32[128]{0:T(128)S(1)}, f32[128]{0:T(128)}, u32[]{:S(2)}) copy-start(f32[128]{0:T(128)} %param.12) | copy-start | bytes 1540
  1.2 0.7 %copy-start.6 = (s32[128]{0:T(128)S(1)}, s32[128]{0:T(128)}, u32[]{:S(2)}) copy-start(s32[128]{0:T(128)} %param.13) | copy-start | bytes 1540
  1.9 1.0 %copy-start = (f32[16,48,128]{2,1,0:T(8,128)S(1)}, f32[16,48,128]{2,1,0:T(8,128)}, u32[]{:S(2)}) copy-start(f32[16,48,128]{2,1,0:T(8,128)} %refs_5_.1) | copy-start | bytes 1179652
  2.9 1.0 %copy-start.1 = (f32[16,48,128]{2,1,0:T(8,128)S(1)}, f32[16,48,128]{2,1,0:T(8,128)}, u32[]{:S(2)}) copy-start(f32[16,48,128]{2,1,0:T(8,128)} %refs_6_.1) | copy-start | bytes 1179652
  3.9 0.7 %copy-start.3 = (s32[3,128]{1,0:T(4,128)S(1)}, s32[3,128]{1,0:T(4,128)}, u32[]{:S(2)}) copy-start(s32[3,128]{1,0:T(4,128)} %refs_1_.1) | copy-start | bytes 4612
  4.6 0.7 %copy-start.4 = (f32[3,128]{1,0:T(4,128)S(1)}, f32[3,128]{1,0:T(4,128)}, u32[]{:S(2)}) copy-start(f32[3,128]{1,0:T(4,128)} %refs_2_.1) | copy-start | bytes 4612
  9.4 5.4 %collective-permute-start.2 = (f32[22,8,128]{2,1,0:T(8,128)S(1)}, f32[22,8,128]{2,1,0:T(8,128)S(1)}, u32[]{:S(2)}, u32[]{:S(2)}) collective-permute-start(f32[22,8,128]{2,1,0:T(8,128)S(1)} %get-tuple-element.18.refs_2_), channel_id=1, source_target_pairs={{0,17},{1,16},{2,19},{3,18},{4,21},{5,20},{6,23},{7,22},{8,25},{9,... | collective-permute-start | bytes 270344 | tf_op jit(solution)/shard_map/ppermute | solution.py:365
  14.8 5.6 %collective-permute-start.3 = (f32[9,8,128]{2,1,0:T(8,128)S(1)}, f32[9,8,128]{2,1,0:T(8,128)S(1)}, u32[]{:S(2)}, u32[]{:S(2)}) collective-permute-start(f32[9,8,128]{2,1,0:T(8,128)S(1)} %get-tuple-element.20), channel_id=1, source_target_pairs={{0,3},{1,2},{2,1},{3,0},{4,7},{5,6},{6,5},{7,4},{8,11},{9,10},{10,... | collective-permute-start | bytes 110600 | tf_op jit(solution)/shard_map/ppermute | solution.py:365
  16.9 7.6 %collective-permute-start.4 = (f32[8,8,128]{2,1,0:T(8,128)S(1)}, f32[8,8,128]{2,1,0:T(8,128)S(1)}, u32[]{:S(2)}, u32[]{:S(2)}) collective-permute-start(f32[8,8,128]{2,1,0:T(8,128)S(1)} %get-tuple-element.21), channel_id=1, source_target_pairs={{0,15},{1,14},{2,5},{3,4},{4,3},{5,2},{6,9},{7,8},{8,7},{9,6},{10,... | collective-permute-start | bytes 98312 | tf_op jit(solution)/shard_map/ppermute | solution.py:365
  20.4 3.0 %collective-permute-start.5 = (f32[1,8,128]{2,1,0:T(8,128)S(1)}, f32[1,8,128]{2,1,0:T(8,128)S(1)}, u32[]{:S(2)}, u32[]{:S(2)}) collective-permute-start(f32[1,8,128]{2,1,0:T(8,128)S(1)} %slice_add_fusion), channel_id=1, source_target_pairs={{0,5},{1,4},{2,7},{3,6},{4,1},{5,0},{6,3},{7,2},{8,13},{9,12},{10,... | collective-permute-start | bytes 12296 | tf_op jit(solution)/shard_map/ppermute | solution.py:365
  23.5 3.9 %collective-permute-start.6 = (f32[1,8,128]{2,1,0:T(8,128)S(1)}, f32[1,8,128]{2,1,0:T(8,128)S(1)}, u32[]{:S(2)}, u32[]{:S(2)}) collective-permute-start(f32[1,8,128]{2,1,0:T(8,128)S(1)} %add.25), channel_id=1, source_target_pairs={{0,9},{1,8},{2,11},{3,10},{4,13},{5,12},{6,15},{7,14},{8,1},{9,0},... | collective-permute-start | bytes 12296 | tf_op jit(solution)/shard_map/ppermute | solution.py:365

commit v3 on v2

--- a/solution.py
+++ b/solution.py
@@ -319,7 +319,7 @@
                 out[row, 8 * tile : 8 * tile + 8, :] += landed[side][(step - 1) * tiles + tile]
 
 
-def call(kernel, plan, outs, scratch, flops, bytes_moved, args, spaces=None):
+def call(kernel, plan, outs, scratch, flops, bytes_moved, args, spaces=None, megabytes=24):
     in_vmem = pl.BlockSpec(memory_space=pltpu.VMEM)
     return pl.pallas_call(
         functools.partial(kernel, plan),
@@ -327,7 +327,7 @@
         in_specs=spaces or [in_vmem] * len(args),
         out_specs=[in_vmem] * len(outs),
         scratch_shapes=scratch,
-        compiler_params=pltpu.CompilerParams(vmem_limit_bytes=24 * 2**20),
+        compiler_params=pltpu.CompilerParams(vmem_limit_bytes=megabytes * 2**20),
         cost_estimate=pl.CostEstimate(flops=flops, bytes_accessed=bytes_moved, transcendentals=0),
     )(*args)
 
@@ -346,7 +346,7 @@
         [pltpu.VMEM(table.shape, table.dtype) for table in tables] + [pltpu.SemaphoreType.DMA((7,))],
         10**6,
         10**6,
-        (*tables, potential, density),
+        [pltpu.with_memory_space_constraint(value, pltpu.HBM) for value in (*tables, potential, density)],
         [pl.BlockSpec(memory_space=pl.ANY)] * 7,
     )
     tall = rows + 2 * plan.guard

time: 28.3 us -> 25.3 us (0.89)
  local copies, waits for them, and re-layouts: 4.68 us -> 0.65 us
  waiting for transfers between devices: 7.95 us -> 8.64 us
  Pallas kernels: 4.9 us -> 5.36 us
    unnamed x14 -> x0, local copies, waits for them, and re-layouts: 4.02 us -> none
    ppermute x1, waiting for transfers between devices: 0.01 us -> 0.56 us  [shards(): density_other = lax.ppermute(density, 'ax', swap)]
    pallas_call x4, Pallas kernels: 4.9 us -> 5.36 us  [call(): pl.pallas_call(functools.partial(kernel, plan), out_shape=[jax.ShapeDtype...]
  transfers between devices with their start and end apart: 7 -> 7, of which waited for: 3 -> 5; matrix products, arithmetic and copies ran while one was open for 0% -> 0% of each run, Pallas kernels for 6% -> 8%
where the time goes in v3:
time: 25.3 us; the launch traced here: 25.1 us
  starting transfers between devices  9.79 us (39%)
  waiting for transfers between devices  8.64 us (34%)
  Pallas kernels  5.36 us (21%)
  between operations  0.66 us (3%)
  local copies, waits for them, and re-layouts  0.65 us (3%)
    ppermute x5, starting transfers between devices, send(): return lax.ppermute(value, AXES, plan.moves(move))  9.19 us
    ppermute x5, waiting for transfers between devices, send(): return lax.ppermute(value, AXES, plan.moves(move))  7.86 us
    pallas_call x4, Pallas kernels, call(): pl.pallas_call(functools.partial(kernel, plan), out_shape=[jax.ShapeDtype...  5.36 us
    reshape x1, local copies, waits for them, and re-layouts, shards(): return (final, mine.reshape(3, share))  0.65 us
    ppermute x1, waiting for transfers between devices, shards(): density_other = lax.ppermute(density, 'ax', swap)  0.56 us
    ppermute x1, starting transfers between devices, shards(): potential_other = lax.ppermute(potential, 'ax', swap)  0.52 us
  transfers between devices with their start and end apart: 7, of which 5 were waited for; matrix products, arithmetic and copies ran while one was open for 0% of the time, Pallas kernels for 8%

profile of v3, /device:TPU:0, one launch (start us, length us, event | category | flops | bytes accessed | tf_op | source)
XLA Modules:
  0.0 25.1 jit_solution(278022048401698701)
XLA Ops:
  0.6 0.5 %collective-permute-start = (f32[16,48,128]{2,1,0:T(8,128)}, f32[16,48,128]{2,1,0:T(8,128)S(1)}, u32[]{:S(2)}, u32[]{:S(2)}) collective-permute-start(f32[16,48,128]{2,1,0:T(8,128)} %refs_5_.1), channel_id=1, source_target_pairs={{0,1},{1,0},{2,3},{3,2},{4,5},{5,4},{6,7},{7,6},{8,9},{9,8},{10,11... | collective-permute-start | bytes 1179656 | tf_op jit(solution)/shard_map/ppermute | solution.py:339
  1.1 0.1 collective-permute-start.1
  1.2 1.3 %shard_map.86 = (f32[1,256,256]{2,1,0:T(8,128)S(1)}, f32[1,2,56,128]{3,2,1,0:T(8,128)S(1)}, f32[1,3,19,128]{3,2,1,0:T(8,128)S(1)}, f32[16,48,128]{2,1,0:T(8,128)S(1)}, f32[16,48,128]{2,1,0:T(8,128)S(1)}) custom-call(s32[3,128]{1,0:T(4,128)} %refs_0_.1, s32[3,128]{1,0:T(4,128)} %refs_1_.1, f32[3,128]{1,0:T(4,128)} %refs_2_.1, f32[1,128]{1,0:T(1,128)} %bitcast.4, ...), custom_call_target="tpu_custom_call" | custom-call | flops 1000000 | bytes 1000000 | tf_op jit(solution)/shard_map/pallas_call | solution.py:324
  2.5 0.2 collective-permute-done.pot_other
  2.7 0.6 %collective-permute-done.1.rho_other = f32[16,48,128]{2,1,0:T(8,128)S(1)} collective-permute-done((f32[16,48,128]{2,1,0:T(8,128)}, f32[16,48,128]{2,1,0:T(8,128)S(1)}, u32[]{:S(2)}, u32[]{:S(2)}) %collective-permute-start.1) | collective-permute-done | bytes 393248 | tf_op jit(solution)/shard_map/ppermute | solution.py:340
  3.3 3.3 %shard_map.87 = (f32[16,48,128]{2,1,0:T(8,128)S(1)}, f32[16,8,128]{2,1,0:T(8,128)S(1)}, f32[22,8,128]{2,1,0:T(8,128)S(1)}) custom-call(f32[16,48,128]{2,1,0:T(8,128)S(1)} %get-tuple-element.12.pot_own, f32[16,48,128]{2,1,0:T(8,128)S(1)} %collective-permute-done.pot_other, f32[16,48,128]{2,1,0:T(8,128)S(1)} %get-tuple-element.13.rho_own, ...), custom_call_target="tpu_custom_call" | custom-call | flops 1000000000 | bytes 10000000 | tf_op jit(solution)/shard_map/pallas_call | solution.py:324
  6.6 2.7 %collective-permute-start.2 = (f32[22,8,128]{2,1,0:T(8,128)S(1)}, f32[22,8,128]{2,1,0:T(8,128)S(1)}, u32[]{:S(2)}, u32[]{:S(2)}) collective-permute-start(f32[22,8,128]{2,1,0:T(8,128)S(1)} %get-tuple-element.18.refs_2_), channel_id=1, source_target_pairs={{0,17},{1,16},{2,19},{3,18},{4,21},{5,20},{6,23},{7,22},{8,25},{9,... | collective-permute-start | bytes 270344 | tf_op jit(solution)/shard_map/ppermute | solution.py:365
  9.2 2.7 %collective-permute-done.2.refs_1_.refs_3_ = f32[22,8,128]{2,1,0:T(8,128)S(1)} collective-permute-done((f32[22,8,128]{2,1,0:T(8,128)S(1)}, f32[22,8,128]{2,1,0:T(8,128)S(1)}, u32[]{:S(2)}, u32[]{:S(2)}) %collective-permute-start.2) | collective-permute-done | bytes 90144 | tf_op jit(solution)/shard_map/ppermute | solution.py:365
  12.0 2.0 %collective-permute-start.3 = (f32[9,8,128]{2,1,0:T(8,128)S(1)}, f32[9,8,128]{2,1,0:T(8,128)S(1)}, u32[]{:S(2)}, u32[]{:S(2)}) collective-permute-start(f32[9,8,128]{2,1,0:T(8,128)S(1)} %get-tuple-element.20), channel_id=1, source_target_pairs={{0,3},{1,2},{2,1},{3,0},{4,7},{5,6},{6,5},{7,4},{8,11},{9,10},{10,... | collective-permute-start | bytes 110600 | tf_op jit(solution)/shard_map/ppermute | solution.py:365
  14.0 3.5 %collective-permute-start.4 = (f32[8,8,128]{2,1,0:T(8,128)S(1)}, f32[8,8,128]{2,1,0:T(8,128)S(1)}, u32[]{:S(2)}, u32[]{:S(2)}) collective-permute-start(f32[8,8,128]{2,1,0:T(8,128)S(1)} %get-tuple-element.21), channel_id=1, source_target_pairs={{0,15},{1,14},{2,5},{3,4},{4,3},{5,2},{6,9},{7,8},{8,7},{9,6},{10,... | collective-permute-start | bytes 98312 | tf_op jit(solution)/shard_map/ppermute | solution.py:365
  17.5 0.0 collective-permute-done.3.refs_2_
  17.5 0.0 collective-permute-start.5
  17.5 3.0 %collective-permute-done.5 = f32[1,8,128]{2,1,0:T(8,128)S(1)} collective-permute-done((f32[1,8,128]{2,1,0:T(8,128)S(1)}, f32[1,8,128]{2,1,0:T(8,128)S(1)}, u32[]{:S(2)}, u32[]{:S(2)}) %collective-permute-start.5) | collective-permute-done | bytes 4128 | tf_op jit(solution)/shard_map/ppermute | solution.py:365
  20.5 1.0 %collective-permute-start.6 = (f32[1,8,128]{2,1,0:T(8,128)S(1)}, f32[1,8,128]{2,1,0:T(8,128)S(1)}, u32[]{:S(2)}, u32[]{:S(2)}) collective-permute-start(f32[1,8,128]{2,1,0:T(8,128)S(1)} %add.25), channel_id=1, source_target_pairs={{0,9},{1,8},{2,11},{3,10},{4,13},{5,12},{6,15},{7,14},{8,1},{9,0},... | collective-permute-start | bytes 12296 | tf_op jit(solution)/shard_map/ppermute | solution.py:365
  21.5 0.0 collective-permute-done.4.refs_3_
  21.5 0.8 %shard_map.89 = f32[16,48,128]{2,1,0:T(8,128)} custom-call(f32[16,48,128]{2,1,0:T(8,128)S(1)} %get-tuple-element.17.refs_0_, f32[22,8,128]{2,1,0:T(8,128)S(1)} %collective-permute-done.2.refs_1_.refs_3_, f32[9,8,128]{2,1,0:T(8,128)S(1)} %collective-permute-done.3.refs_2_, f32[8,8,128]{2,1,0:T(8,128)S(1)} %collective-permute-done.4.refs_3_), custom_call_target="tpu_custom_call" | custom-call | flops 100000 | bytes 1000000 | tf_op jit(solution)/shard_map/pallas_call | solution.py:324
  22.3 2.1 %collective-permute-done.6 = f32[1,8,128]{2,1,0:T(8,128)S(1)} collective-permute-done((f32[1,8,128]{2,1,0:T(8,128)S(1)}, f32[1,8,128]{2,1,0:T(8,128)S(1)}, u32[]{:S(2)}, u32[]{:S(2)}) %collective-permute-start.6) | collective-permute-done | bytes 4128 | tf_op jit(solution)/shard_map/ppermute | solution.py:365
  24.5 0.7 %dynamic-slice_bitcast_fusion = f32[3,4]{1,0:T(4,128)} fusion(f32[1,8,128]{2,1,0:T(8,128)S(1)} %add.26, s32[]{:T(128)S(6)} %select_n.14), kind=kLoop, calls=%fused_computation.1 | loop fusion | bytes 100 | tf_op jit(solution)/shard_map/reshape | solution.py:406
  (4 shorter events, 0.0 us)
Async XLA Ops:
  0.6 2.1 %collective-permute-start = (f32[16,48,128]{2,1,0:T(8,128)}, f32[16,48,128]{2,1,0:T(8,128)S(1)}, u32[]{:S(2)}, u32[]{:S(2)}) collective-permute-start(f32[16,48,128]{2,1,0:T(8,128)} %refs_5_.1), channel_id=1, source_target_pairs={{0,1},{1,0},{2,3},{3,2},{4,5},{5,4},{6,7},{7,6},{8,9},{9,8},{10,11... | collective-permute-start | bytes 1179656 | tf_op jit(solution)/shard_map/ppermute | solution.py:339
  1.1 2.1 %collective-permute-start.1 = (f32[16,48,128]{2,1,0:T(8,128)}, f32[16,48,128]{2,1,0:T(8,128)S(1)}, u32[]{:S(2)}, u32[]{:S(2)}) collective-permute-start(f32[16,48,128]{2,1,0:T(8,128)} %refs_6_.1), channel_id=1, source_target_pairs={{0,1},{1,0},{2,3},{3,2},{4,5},{5,4},{6,7},{7,6},{8,9},{9,8},{10,11... | collective-permute-start | bytes 1179656 | tf_op jit(solution)/shard_map/ppermute | solution.py:340
  6.6 5.4 %collective-permute-start.2 = (f32[22,8,128]{2,1,0:T(8,128)S(1)}, f32[22,8,128]{2,1,0:T(8,128)S(1)}, u32[]{:S(2)}, u32[]{:S(2)}) collective-permute-start(f32[22,8,128]{2,1,0:T(8,128)S(1)} %get-tuple-element.18.refs_2_), channel_id=1, source_target_pairs={{0,17},{1,16},{2,19},{3,18},{4,21},{5,20},{6,23},{7,22},{8,25},{9,... | collective-permute-start | bytes 270344 | tf_op jit(solution)/shard_map/ppermute | solution.py:365
  12.0 5.5 %collective-permute-start.3 = (f32[9,8,128]{2,1,0:T(8,128)S(1)}, f32[9,8,128]{2,1,0:T(8,128)S(1)}, u32[]{:S(2)}, u32[]{:S(2)}) collective-permute-start(f32[9,8,128]{2,1,0:T(8,128)S(1)} %get-tuple-element.20), channel_id=1, source_target_pairs={{0,3},{1,2},{2,1},{3,0},{4,7},{5,6},{6,5},{7,4},{8,11},{9,10},{10,... | collective-permute-start | bytes 110600 | tf_op jit(solution)/shard_map/ppermute | solution.py:365
  14.0 7.6 %collective-permute-start.4 = (f32[8,8,128]{2,1,0:T(8,128)S(1)}, f32[8,8,128]{2,1,0:T(8,128)S(1)}, u32[]{:S(2)}, u32[]{:S(2)}) collective-permute-start(f32[8,8,128]{2,1,0:T(8,128)S(1)} %get-tuple-element.21), channel_id=1, source_target_pairs={{0,15},{1,14},{2,5},{3,4},{4,3},{5,2},{6,9},{7,8},{8,7},{9,6},{10,... | collective-permute-start | bytes 98312 | tf_op jit(solution)/shard_map/ppermute | solution.py:365
  17.5 3.0 %collective-permute-start.5 = (f32[1,8,128]{2,1,0:T(8,128)S(1)}, f32[1,8,128]{2,1,0:T(8,128)S(1)}, u32[]{:S(2)}, u32[]{:S(2)}) collective-permute-start(f32[1,8,128]{2,1,0:T(8,128)S(1)} %slice_add_fusion), channel_id=1, source_target_pairs={{0,5},{1,4},{2,7},{3,6},{4,1},{5,0},{6,3},{7,2},{8,13},{9,12},{10,... | collective-permute-start | bytes 12296 | tf_op jit(solution)/shard_map/ppermute | solution.py:365
  20.5 3.9 %collective-permute-start.6 = (f32[1,8,128]{2,1,0:T(8,128)S(1)}, f32[1,8,128]{2,1,0:T(8,128)S(1)}, u32[]{:S(2)}, u32[]{:S(2)}) collective-permute-start(f32[1,8,128]{2,1,0:T(8,128)S(1)} %add.25), channel_id=1, source_target_pairs={{0,9},{1,8},{2,11},{3,10},{4,13},{5,12},{6,15},{7,14},{8,1},{9,0},... | collective-permute-start | bytes 12296 | tf_op jit(solution)/shard_map/ppermute | solution.py:365

commit v4 on v3

--- a/solution.py
+++ b/solution.py
@@ -40,7 +40,9 @@
         self.sides = 0 if self.n_rad == 1 else 1 if self.n_rad == 2 else 2
         self.slots = self.cells_r + SWEEPS * self.sides
         self.guard = SWEEPS + 1
-        self.side_tiles = self.sides * SWEEPS * (self.ring // 8)
+        self.beyond = SWEEPS * self.sides
+        self.face = SWEEPS * (self.cells_a // 8)
+        self.halo = (self.slots + 1) // 2
 
     def sign(self, side, rad):
         if self.sides == 1:
@@ -67,6 +69,25 @@
                     for ax in range(self.n_ax):
                         found.append((self.device(rad, ang, ax), self.device(*target, 1 - ax)))
         return found
+
+
+def even_sector(ang):
+    return (lax.broadcasted_iota(jnp.int32, (8, LANES), 0) * 0 + ang) % 2 == 0
+
+
+def pack(front, back, is_even):
+    low_half = lax.broadcasted_iota(jnp.int32, front.shape, 0) < 4
+    above = jnp.where(low_half, front, pltpu.roll(back, 4, 0))
+    below = jnp.where(low_half, pltpu.roll(front, 4, 0), back)
+    return jnp.where(is_even, above, below), jnp.where(is_even, below, above)
+
+
+def unpack(even, odd, half, is_even):
+    low_half = lax.broadcasted_iota(jnp.int32, even.shape, 0) < 4
+    above, below = jnp.where(is_even, even, odd), jnp.where(is_even, odd, even)
+    first = below if half == 0 else pltpu.roll(below, 4, 0)
+    last = above if half == 1 else pltpu.roll(above, 4, 0)
+    return jnp.where(low_half, first, 0.0), jnp.where(low_half, 0.0, last)
 
 
 def factors_kernel(plan, *refs):
@@ -164,8 +185,10 @@
     a_fac,
     r_fac,
     own_out,
-    hal_out,
-    rad_out,
+    even_out,
+    odd_out,
+    face_out,
+    force_out,
     first,
     second,
     grown,
@@ -211,10 +234,9 @@
         return (1.0 - weight) * center + (weight * inverse) * total
 
     def send_row(slot, fresh):
-        tiles = ring // 8
-        for tile in range(tiles - 1):
-            rad_out[slot * tiles + tile] = fresh[8 * tile : 8 * tile + 8, plan.cells_z :]
-        rad_out[slot * tiles + tiles - 1] = fresh[plan.cells_a :, : plan.cells_z]
+        tiles = plan.cells_a // 8
+        for tile in range(tiles):
+            face_out[slot * tiles + tile] = fresh[8 * tile : 8 * tile + 8, plan.cells_z :]
 
     source, target = first, second
     for sweep in range(SWEEPS):
@@ -224,7 +246,6 @@
             if last:
                 grown[row] = fresh
                 own_out[row] = fresh[: plan.cells_a, : plan.cells_z]
-                hal_out[row] = fresh[plan.cells_a :, plan.cells_z :]
             else:
                 target[guard + row] = fresh
         for side in range(plan.sides):
@@ -239,7 +260,12 @@
                     target[place] = fresh
         source, target = target, source
 
-    force_base = plan.side_tiles
+    is_even = even_sector(lax.axis_index("ang"))
+    halo = [grown[slot, plan.cells_a :, plan.cells_z :] for slot in range(rows)]
+    halo += [grown[slot, plan.cells_a :, : plan.cells_z] for slot in range(rows, plan.slots)]
+    halo += [jnp.zeros_like(halo[0])] * (2 * plan.halo - plan.slots)
+    for tile in range(plan.halo):
+        even_out[tile], odd_out[tile] = pack(halo[2 * tile], halo[2 * tile + 1], is_even)
 
     def chunk(number, carry):
         spread = jnp.dot(
@@ -258,7 +284,7 @@
             for k, turn in enumerate((0, 1, 0))
         ]
         total.append(jnp.zeros((5, LANES), jnp.float32))
-        rad_out[force_base + number] = jnp.concatenate(total, axis=0)
+        force_out[number] = jnp.concatenate(total, axis=0)
         return carry
 
     if plan.chunks == 1:
@@ -267,55 +293,48 @@
         lax.fori_loop(0, plan.chunks, chunk, 0)
 
 
-def turn_kernel(plan, *refs):
-    hal, landed, forces = refs[0], refs[1 : 1 + plan.sides], refs[1 + plan.sides : -3]
-    even_out, odd_out, held = refs[-3:]
-    rad, ang = lax.axis_index("rad"), lax.axis_index("ang")
-    width = plan.cells_z
-    held[...] = hal[...]
-    tiles = plan.ring // 8
+def join_kernel(plan, even, *refs):
+    forces, out = refs[:-1], refs[-1]
+    out[: plan.halo] = even[...]
+    out[plan.halo :] = forces[0][...] if len(forces) == 1 else forces[0][...] + forces[1][...]
+
+
+def fold_kernel(plan, face, even, even_in, odd_in, face_out, force_out):
+    is_even = even_sector(lax.axis_index("ang"))
+    face_out[...] = face[...]
+    tiles = plan.cells_a // 8
+    for slot in range(plan.beyond):
+        tile, half = divmod(plan.cells_r + slot, 2)
+        first, last = unpack(even_in[tile], odd_in[tile], half, is_even)
+        face_out[slot * tiles] = face_out[slot * tiles] + first
+        face_out[slot * tiles + tiles - 1] = face_out[slot * tiles + tiles - 1] + last
+    force_out[...] = even[plan.halo :] + even_in[plan.halo :]
+
+
+def add_kernel(plan, first, second, out):
+    out[...] = first[...] + second[...]
+
+
+def copy_kernel(plan, value, after, out):
+    out[...] = value[...]
+
+
+def final_kernel(plan, *refs):
+    own, landed, even_in, odd_in, force, out, force_out = refs[0], refs[1 : 1 + plan.sides], *refs[-5:]
+    force_out[...] = force[...]
+    rad = lax.axis_index("rad")
+    is_even = even_sector(lax.axis_index("ang"))
+    top = plan.cells_a - 8
+    tiles = plan.cells_a // 8
+    for row in range(plan.cells_r):
+        first, last = unpack(even_in[row // 2], odd_in[row // 2], row % 2, is_even)
+        out[row] = own[row]
+        out[row, 0:8, :] += first
+        out[row, top:, :] += last
     for side in range(plan.sides):
         for step in range(1, SWEEPS + 1):
             row = plan.landing_row(side, rad, step)
-            held[row] = held[row] + landed[side][step * tiles - 1]
-    low_half = lax.broadcasted_iota(jnp.int32, (8, width), 0) < 4
-    is_even = (lax.broadcasted_iota(jnp.int32, (8, width), 0) * 0 + ang) % 2 == 0
-    pairs = plan.cells_r // 2
-    for tile in range(pairs):
-        front, back = held[2 * tile], held[2 * tile + 1]
-        above = jnp.where(low_half, front, pltpu.roll(back, 4, 0))
-        below = jnp.where(low_half, pltpu.roll(front, 4, 0), back)
-        even_out[tile] = jnp.where(is_even, above, below)
-        odd_out[tile] = jnp.where(is_even, below, above)
-    for number in range(plan.chunks):
-        total = forces[0][number - plan.chunks + forces[0].shape[0]]
-        if len(forces) > 1:
-            total = total + forces[1][number - plan.chunks + forces[1].shape[0]]
-        even_out[pairs + number] = total
-
-
-def final_kernel(plan, *refs):
-    own, landed, even_in, odd_in, out = refs[0], refs[1 : 1 + plan.sides], *refs[-3:]
-    rad, ang = lax.axis_index("rad"), lax.axis_index("ang")
-    width = plan.cells_z
-    low_half = lax.broadcasted_iota(jnp.int32, (8, width), 0) < 4
-    is_even = (lax.broadcasted_iota(jnp.int32, (8, width), 0) * 0 + ang) % 2 == 0
-    top = plan.cells_a - 8
-    tiles = plan.ring // 8
-    for tile in range(plan.cells_r // 2):
-        even, odd = even_in[tile], odd_in[tile]
-        above, below = jnp.where(is_even, even, odd), jnp.where(is_even, odd, even)
-        for half in range(2):
-            row = 2 * tile + half
-            from_below = below if half == 0 else pltpu.roll(below, 4, 0)
-            from_above = above if half == 1 else pltpu.roll(above, 4, 0)
-            out[row] = own[row]
-            out[row, 0:8, :] += jnp.where(low_half, from_below, 0.0)
-            out[row, top:, :] += jnp.where(low_half, 0.0, from_above)
-    for side in range(plan.sides):
-        for step in range(1, SWEEPS + 1):
-            row = plan.landing_row(side, rad, step)
-            for tile in range(tiles - 1):
+            for tile in range(tiles):
                 out[row, 8 * tile : 8 * tile + 8, :] += landed[side][(step - 1) * tiles + tile]
 
 
@@ -351,10 +370,11 @@
     )
     tall = rows + 2 * plan.guard
     scratch = [(tall, ring, depth)] * 2 + [(slots, ring, depth), (4, tall, depth)]
-    own, hal, sides = call(
+    own, even, odd, face, force = call(
         sweeps_kernel,
         plan,
-        [block, (rows, 8, width), (plan.side_tiles + chunks, 8, LANES)],
+        [block, (plan.halo, 8, width), (plan.halo, 8, width)]
+        + [(max(1, plan.face * plan.sides), 8, width), (chunks, 8, LANES)],
         [pltpu.VMEM(shape, jnp.float32) for shape in scratch],
         10**9,
         10**7,
@@ -364,42 +384,60 @@
     def send(value, move):
         return lax.ppermute(value, AXES, plan.moves(move))
 
-    per_side = plan.side_tiles // max(1, plan.sides)
-    if plan.sides == 1:
-        landed = [send(sides, lambda r, a: (1 - r, a))]
-        forces = [sides, landed[0]]
-    else:
-        landed = []
-        force = sides[plan.side_tiles :]
-        if plan.sides == 2:
-            landed.append(send(sides[per_side : 2 * per_side], lambda r, a: (r - 1, a) if r else None))
-            last = plan.n_rad - 1
-            landed.append(send(sides[:per_side], lambda r, a: (r + 1, a) if r < last else None))
-        step = 1
-        while step < plan.n_rad:
-            force = force + send(force, lambda r, a: (r ^ step, a))
-            step *= 2
-        forces = [force]
-    pairs = rows // 2
-    even, odd = call(
-        turn_kernel,
+    def send_radial(value, length):
+        if plan.sides == 0:
+            return []
+        if plan.sides == 1:
+            return [send(value, lambda r, a: (1 - r, a))]
+        last = plan.n_rad - 1
+        return [
+            send(value[length : 2 * length], lambda r, a: (r - 1, a) if r else None),
+            send(value[:length], lambda r, a: (r + 1, a) if r < last else None),
+        ]
+
+    def send_angular(value, step):
+        return send(value, lambda r, a: (r, a ^ step))
+
+    (odd,) = call(copy_kernel, plan, [odd.shape], [], 10**6, 10**6, (odd, force))
+    odd_in = send(odd, lambda r, a: (r, (a + 1 - 2 * (1 - a % 2)) % plan.n_ang))
+    parts = [force]
+    step = plan.n_ang // 2
+    while step > 2:
+        force = sum(parts)
+        parts = [force, send_angular(force, step)]
+        step //= 2
+    (even,) = call(
+        join_kernel, plan, [(plan.halo + chunks, 8, width)], [], 10**9, 10**9, (even, *parts)
+    )
+    even_in = send_angular(even, 1)
+    (odd_in,) = call(copy_kernel, plan, [odd.shape], [], 10**9, 10**9, (odd_in, odd))
+    face, force = call(
+        fold_kernel,
         plan,
-        [(pairs + chunks, 8, width), (pairs, 8, width)],
-        [pltpu.VMEM((rows, 8, width), jnp.float32)],
+        [face.shape, (chunks, 8, LANES)],
+        [],
+        10**5,
+        10**5,
+        (face, even, even_in, odd_in),
+    )
+    (face,) = call(copy_kernel, plan, [face.shape], [], 10**6, 10**6, (face, force))
+    faces = send_radial(face, plan.face)
+    step = 1
+    while step < plan.n_rad:
+        part = send(force, lambda r, a: (r ^ step, a))
+        (force,) = call(add_kernel, plan, [force.shape], [], 10**9, 10**9, (force, part))
+        step *= 2
+    last_part = send_angular(force, 2) if plan.n_ang > 2 else jnp.zeros_like(force)
+    final, force = call(
+        final_kernel,
+        plan,
+        [block, force.shape],
+        [],
         10**5,
         10**6,
-        (hal, *landed, *forces),
-    )
-    odd_in = send(odd, lambda r, a: (r, (a + 1 - 2 * (1 - a % 2)) % plan.n_ang))
-    even_in = send(even, lambda r, a: (r, a ^ 1))
-    force = even[pairs:] + even_in[pairs:]
-    step = 2
-    while step < plan.n_ang:
-        force = force + send(force, lambda r, a: (r, a ^ step))
-        step *= 2
-    (final,) = call(
-        final_kernel, plan, [block], [], 10**5, 10**6, (own, *landed, even_in, odd_in)
-    )
+        (own, *faces, even_in, odd_in, force),
+    )
+    force = force + last_part
     share = plan.atoms // (plan.n_rad * plan.n_ang * plan.n_ax)
     first = plan.device(*(lax.axis_index(name) for name in AXES)) * share
     mine = lax.dynamic_slice(force, (first // LANES, 0, first % LANES), (1, 3, share))

time: 25.3 us -> 24.3 us (0.960)
  waiting for transfers between devices: 8.64 us -> 8.12 us
  starting transfers between devices: 9.79 us -> 9.28 us
    ppermute x5 -> x6, waiting for transfers between devices: 7.86 us -> 7.34 us  [send(): return lax.ppermute(value, AXES, plan.moves(move))]
    ppermute x5 -> x6, starting transfers between devices: 9.19 us -> 8.68 us  [send(): return lax.ppermute(value, AXES, plan.moves(move))]
    pallas_call x4 -> x9, Pallas kernels: 5.36 us -> 5.38 us  [call(): pl.pallas_call(functools.partial(kernel, plan), out_shape=[jax.ShapeDtype...]
  transfers between devices with their start and end apart: 7 -> 8, of which waited for: 5 -> 6; matrix products, arithmetic and copies ran while one was open for 0% -> 0% of each run, Pallas kernels for 8% -> 9%
where the time goes in v4:
time: 24.3 us; the launch traced here: 24.1 us
  starting transfers between devices  9.28 us (38%)
  waiting for transfers between devices  8.12 us (33%)
  Pallas kernels  5.38 us (22%)
  between operations  0.66 us (3%)
  local copies, waits for them, and re-layouts  0.65 us (3%)
    ppermute x6, starting transfers between devices, send(): return lax.ppermute(value, AXES, plan.moves(move))  8.68 us
    ppermute x6, waiting for transfers between devices, send(): return lax.ppermute(value, AXES, plan.moves(move))  7.34 us
    pallas_call x9, Pallas kernels, call(): pl.pallas_call(functools.partial(kernel, plan), out_shape=[jax.ShapeDtype...  5.38 us
    reshape x1, local copies, waits for them, and re-layouts, shards(): return (final, mine.reshape(3, share))  0.65 us
    ppermute x1, waiting for transfers between devices, shards(): density_other = lax.ppermute(density, 'ax', swap)  0.56 us
    ppermute x1, starting transfers between devices, shards(): potential_other = lax.ppermute(potential, 'ax', swap)  0.52 us
  transfers between devices with their start and end apart: 8, of which 6 were waited for; matrix products, arithmetic and copies ran while one was open for 0% of the time, Pallas kernels for 9%

profile of v4, /device:TPU:0, one launch (start us, length us, event | category | flops | bytes accessed | tf_op | source)
XLA Modules:
  0.0 24.1 jit_solution(13581393049712191941)
XLA Ops:
  0.6 0.5 %collective-permute-start = (f32[16,48,128]{2,1,0:T(8,128)}, f32[16,48,128]{2,1,0:T(8,128)S(1)}, u32[]{:S(2)}, u32[]{:S(2)}) collective-permute-start(f32[16,48,128]{2,1,0:T(8,128)} %refs_5_.1), channel_id=1, source_target_pairs={{0,1},{1,0},{2,3},{3,2},{4,5},{5,4},{6,7},{7,6},{8,9},{9,8},{10,11... | collective-permute-start | bytes 1179656 | tf_op jit(solution)/shard_map/ppermute | solution.py:358
  1.2 0.1 collective-permute-start.1
  1.2 1.3 %shard_map.86 = (f32[1,256,256]{2,1,0:T(8,128)S(1)}, f32[1,2,56,128]{3,2,1,0:T(8,128)S(1)}, f32[1,3,19,128]{3,2,1,0:T(8,128)S(1)}, f32[16,48,128]{2,1,0:T(8,128)S(1)}, f32[16,48,128]{2,1,0:T(8,128)S(1)}) custom-call(s32[3,128]{1,0:T(4,128)} %refs_0_.1, s32[3,128]{1,0:T(4,128)} %refs_1_.1, f32[3,128]{1,0:T(4,128)} %refs_2_.1, f32[1,128]{1,0:T(1,128)} %bitcast.4, ...), custom_call_target="tpu_custom_call" | custom-call | flops 1000000 | bytes 1000000 | tf_op jit(solution)/shard_map/pallas_call | solution.py:343
  2.5 0.2 collective-permute-done.pot_other
  2.7 0.6 %collective-permute-done.1.rho_other = f32[16,48,128]{2,1,0:T(8,128)S(1)} collective-permute-done((f32[16,48,128]{2,1,0:T(8,128)}, f32[16,48,128]{2,1,0:T(8,128)S(1)}, u32[]{:S(2)}, u32[]{:S(2)}) %collective-permute-start.1) | collective-permute-done | bytes 393248 | tf_op jit(solution)/shard_map/ppermute | solution.py:359
  3.3 3.3 %shard_map.87 = (f32[16,48,128]{2,1,0:T(8,128)S(1)}, f32[10,8,128]{2,1,0:T(8,128)S(1)}, f32[10,8,128]{2,1,0:T(8,128)S(1)}, f32[18,8,128]{2,1,0:T(8,128)S(1)}, f32[1,8,128]{2,1,0:T(8,128)S(1)}) custom-call(f32[16,48,128]{2,1,0:T(8,128)S(1)} %get-tuple-element.16.pot_own, f32[16,48,128]{2,1,0:T(8,128)S(1)} %collective-permute-done.pot_other, ...), custom_call_target="tpu_custom_call" | custom-call | flops 1000000000 | bytes 10000000 | tf_op jit(solution)/shard_map/pallas_call | solution.py:343
  6.6 3.8 %collective-permute-start.2 = (f32[1,8,128]{2,1,0:T(8,128)S(1)}, f32[1,8,128]{2,1,0:T(8,128)S(1)}, u32[]{:S(2)}, u32[]{:S(2)}) collective-permute-start(f32[1,8,128]{2,1,0:T(8,128)S(1)} %get-tuple-element.24.refs_0_.after), channel_id=1, source_target_pairs={{0,9},{1,8},{2,11},{3,10},{4,13},{5,12},{6,15},{7,14},{8,1},{9,0},... | collective-permute-start | bytes 12296 | tf_op jit(solution)/shard_map/ppermute | solution.py:385
  10.3 2.3 %collective-permute-start.4 = (f32[10,8,128]{2,1,0:T(8,128)S(1)}, f32[10,8,128]{2,1,0:T(8,128)S(1)}, u32[]{:S(2)}, u32[]{:S(2)}) collective-permute-start(f32[10,8,128]{2,1,0:T(8,128)S(1)} %shard_map.89.after), channel_id=1, source_target_pairs={{0,15},{1,14},{2,5},{3,4},{4,3},{5,2},{6,9},{7,8},{8,7},{9,6},{10,... | collective-permute-start | bytes 122888 | tf_op jit(solution)/shard_map/ppermute | solution.py:385
  12.6 0.0 collective-permute-done.2.refs_1_
  12.6 0.6 %collective-permute-start.3 = (f32[11,8,128]{2,1,0:T(8,128)S(1)}, f32[11,8,128]{2,1,0:T(8,128)S(1)}, u32[]{:S(2)}, u32[]{:S(2)}) collective-permute-start(f32[11,8,128]{2,1,0:T(8,128)S(1)} %shard_map.88.even), channel_id=1, source_target_pairs={{0,3},{1,2},{2,1},{3,0},{4,7},{5,6},{6,5},{7,4},{8,11},{9,10},{10,... | collective-permute-start | bytes 135176 | tf_op jit(solution)/shard_map/ppermute | solution.py:385
  13.2 3.4 %collective-permute-done.4.value = f32[10,8,128]{2,1,0:T(8,128)S(1)} collective-permute-done((f32[10,8,128]{2,1,0:T(8,128)S(1)}, f32[10,8,128]{2,1,0:T(8,128)S(1)}, u32[]{:S(2)}, u32[]{:S(2)}) %collective-permute-start.4) | collective-permute-done | bytes 40992 | tf_op jit(solution)/shard_map/ppermute | solution.py:385
  16.6 0.6 %collective-permute-done.3.even_in.refs_2_ = f32[11,8,128]{2,1,0:T(8,128)S(1)} collective-permute-done((f32[11,8,128]{2,1,0:T(8,128)S(1)}, f32[11,8,128]{2,1,0:T(8,128)S(1)}, u32[]{:S(2)}, u32[]{:S(2)}) %collective-permute-start.3) | collective-permute-done | bytes 45088 | tf_op jit(solution)/shard_map/ppermute | solution.py:385
  17.2 1.3 %collective-permute-start.6 = (f32[1,8,128]{2,1,0:T(8,128)S(1)}, f32[1,8,128]{2,1,0:T(8,128)S(1)}, u32[]{:S(2)}, u32[]{:S(2)}) collective-permute-start(f32[1,8,128]{2,1,0:T(8,128)S(1)} %get-tuple-element.27.after.first), channel_id=1, source_target_pairs={{0,17},{1,16},{2,19},{3,18},{4,21},{5,20},{6,23},{7,22},{8,25},{9,... | collective-permute-start | bytes 12296 | tf_op jit(solution)/shard_map/ppermute | solution.py:385
  18.6 0.5 %collective-permute-start.5 = (f32[18,8,128]{2,1,0:T(8,128)S(1)}, f32[18,8,128]{2,1,0:T(8,128)S(1)}, u32[]{:S(2)}, u32[]{:S(2)}) collective-permute-start(f32[18,8,128]{2,1,0:T(8,128)S(1)} %shard_map.92), channel_id=1, source_target_pairs={{0,17},{1,16},{2,19},{3,18},{4,21},{5,20},{6,23},{7,22},{8,25},{9,... | collective-permute-start | bytes 221192 | tf_op jit(solution)/shard_map/ppermute | solution.py:385
  19.0 1.3 %collective-permute-done.6.second = f32[1,8,128]{2,1,0:T(8,128)S(1)} collective-permute-done((f32[1,8,128]{2,1,0:T(8,128)S(1)}, f32[1,8,128]{2,1,0:T(8,128)S(1)}, u32[]{:S(2)}, u32[]{:S(2)}) %collective-permute-start.6) | collective-permute-done | bytes 4128 | tf_op jit(solution)/shard_map/ppermute | solution.py:385
  20.3 0.3 %collective-permute-start.7 = (f32[1,8,128]{2,1,0:T(8,128)S(1)}, f32[1,8,128]{2,1,0:T(8,128)S(1)}, u32[]{:S(2)}, u32[]{:S(2)}) collective-permute-start(f32[1,8,128]{2,1,0:T(8,128)S(1)} %shard_map.93.refs_4_), channel_id=1, source_target_pairs={{0,5},{1,4},{2,7},{3,6},{4,1},{5,0},{6,3},{7,2},{8,13},{9,12},{10,... | collective-permute-start | bytes 12296 | tf_op jit(solution)/shard_map/ppermute | solution.py:385
  20.6 2.1 %collective-permute-done.5.refs_1_ = f32[18,8,128]{2,1,0:T(8,128)S(1)} collective-permute-done((f32[18,8,128]{2,1,0:T(8,128)S(1)}, f32[18,8,128]{2,1,0:T(8,128)S(1)}, u32[]{:S(2)}, u32[]{:S(2)}) %collective-permute-start.5) | collective-permute-done | bytes 73760 | tf_op jit(solution)/shard_map/ppermute | solution.py:385
  22.7 0.8 %shard_map.94 = (f32[16,48,128]{2,1,0:T(8,128)}, f32[1,8,128]{2,1,0:T(8,128)S(1)}) custom-call(f32[16,48,128]{2,1,0:T(8,128)S(1)} %get-tuple-element.21.refs_0_, f32[18,8,128]{2,1,0:T(8,128)S(1)} %collective-permute-done.5.refs_1_, f32[11,8,128]{2,1,0:T(8,128)S(1)} %collective-permute-done.3.even_in.refs_2_, f32[10,8,128]{2,1,0:T(8,128)S(1)} %shard_map.90.odd_in.refs_3_, ...), custom_call_target="tpu_custom_call" | custom-call | flops 100000 | bytes 1000000 | tf_op jit(solution)/shard_map/pallas_call | solution.py:343
  23.4 0.0 collective-permute-done.7
  23.5 0.7 %dynamic-slice_bitcast_fusion = f32[3,4]{1,0:T(4,128)} fusion(f32[1,8,128]{2,1,0:T(8,128)S(1)} %add.18, s32[]{:T(128)S(6)} %select_n.14), kind=kLoop, calls=%fused_computation | loop fusion | bytes 100 | tf_op jit(solution)/shard_map/reshape | solution.py:444
  (7 shorter events, 0.0 us)
Async XLA Ops:
  0.6 2.1 %collective-permute-start = (f32[16,48,128]{2,1,0:T(8,128)}, f32[16,48,128]{2,1,0:T(8,128)S(1)}, u32[]{:S(2)}, u32[]{:S(2)}) collective-permute-start(f32[16,48,128]{2,1,0:T(8,128)} %refs_5_.1), channel_id=1, source_target_pairs={{0,1},{1,0},{2,3},{3,2},{4,5},{5,4},{6,7},{7,6},{8,9},{9,8},{10,11... | collective-permute-start | bytes 1179656 | tf_op jit(solution)/shard_map/ppermute | solution.py:358
  1.2 2.1 %collective-permute-start.1 = (f32[16,48,128]{2,1,0:T(8,128)}, f32[16,48,128]{2,1,0:T(8,128)S(1)}, u32[]{:S(2)}, u32[]{:S(2)}) collective-permute-start(f32[16,48,128]{2,1,0:T(8,128)} %refs_6_.1), channel_id=1, source_target_pairs={{0,1},{1,0},{2,3},{3,2},{4,5},{5,4},{6,7},{7,6},{8,9},{9,8},{10,11... | collective-permute-start | bytes 1179656 | tf_op jit(solution)/shard_map/ppermute | solution.py:359
  6.6 6.1 %collective-permute-start.2 = (f32[1,8,128]{2,1,0:T(8,128)S(1)}, f32[1,8,128]{2,1,0:T(8,128)S(1)}, u32[]{:S(2)}, u32[]{:S(2)}) collective-permute-start(f32[1,8,128]{2,1,0:T(8,128)S(1)} %get-tuple-element.24.refs_0_.after), channel_id=1, source_target_pairs={{0,9},{1,8},{2,11},{3,10},{4,13},{5,12},{6,15},{7,14},{8,1},{9,0},... | collective-permute-start | bytes 12296 | tf_op jit(solution)/shard_map/ppermute | solution.py:385
  10.3 6.2 %collective-permute-start.4 = (f32[10,8,128]{2,1,0:T(8,128)S(1)}, f32[10,8,128]{2,1,0:T(8,128)S(1)}, u32[]{:S(2)}, u32[]{:S(2)}) collective-permute-start(f32[10,8,128]{2,1,0:T(8,128)S(1)} %shard_map.89.after), channel_id=1, source_target_pairs={{0,15},{1,14},{2,5},{3,4},{4,3},{5,2},{6,9},{7,8},{8,7},{9,6},{10,... | collective-permute-start | bytes 122888 | tf_op jit(solution)/shard_map/ppermute | solution.py:385
  12.6 4.6 %collective-permute-start.3 = (f32[11,8,128]{2,1,0:T(8,128)S(1)}, f32[11,8,128]{2,1,0:T(8,128)S(1)}, u32[]{:S(2)}, u32[]{:S(2)}) collective-permute-start(f32[11,8,128]{2,1,0:T(8,128)S(1)} %shard_map.88.even), channel_id=1, source_target_pairs={{0,3},{1,2},{2,1},{3,0},{4,7},{5,6},{6,5},{7,4},{8,11},{9,10},{10,... | collective-permute-start | bytes 135176 | tf_op jit(solution)/shard_map/ppermute | solution.py:385
  17.2 3.1 %collective-permute-start.6 = (f32[1,8,128]{2,1,0:T(8,128)S(1)}, f32[1,8,128]{2,1,0:T(8,128)S(1)}, u32[]{:S(2)}, u32[]{:S(2)}) collective-permute-start(f32[1,8,128]{2,1,0:T(8,128)S(1)} %get-tuple-element.27.after.first), channel_id=1, source_target_pairs={{0,17},{1,16},{2,19},{3,18},{4,21},{5,20},{6,23},{7,22},{8,25},{9,... | collective-permute-start | bytes 12296 | tf_op jit(solution)/shard_map/ppermute | solution.py:385
  18.6 4.1 %collective-permute-start.5 = (f32[18,8,128]{2,1,0:T(8,128)S(1)}, f32[18,8,128]{2,1,0:T(8,128)S(1)}, u32[]{:S(2)}, u32[]{:S(2)}) collective-permute-start(f32[18,8,128]{2,1,0:T(8,128)S(1)} %shard_map.92), channel_id=1, source_target_pairs={{0,17},{1,16},{2,19},{3,18},{4,21},{5,20},{6,23},{7,22},{8,25},{9,... | collective-permute-start | bytes 221192 | tf_op jit(solution)/shard_map/ppermute | solution.py:385
  20.3 3.1 %collective-permute-start.7 = (f32[1,8,128]{2,1,0:T(8,128)S(1)}, f32[1,8,128]{2,1,0:T(8,128)S(1)}, u32[]{:S(2)}, u32[]{:S(2)}) collective-permute-start(f32[1,8,128]{2,1,0:T(8,128)S(1)} %shard_map.93.refs_4_), channel_id=1, source_target_pairs={{0,5},{1,4},{2,7},{3,6},{4,1},{5,0},{6,3},{7,2},{8,13},{9,12},{10,... | collective-permute-start | bytes 12296 | tf_op jit(solution)/shard_map/ppermute | solution.py:385

commit v5 on v4

--- a/solution.py
+++ b/solution.py
@@ -41,7 +41,7 @@
         self.slots = self.cells_r + SWEEPS * self.sides
         self.guard = SWEEPS + 1
         self.beyond = SWEEPS * self.sides
-        self.face = SWEEPS * (self.cells_a // 8)
+        self.tiles = self.cells_a // 8
         self.halo = (self.slots + 1) // 2
 
     def sign(self, side, rad):
@@ -91,17 +91,30 @@
 
 
 def factors_kernel(plan, *refs):
-    sources, (z_out, a_out, r_out, pot_out, rho_out), held = refs[:7], refs[7:12], refs[12:17]
+    sources, outs, held = refs[:7], refs[7:14], refs[14:19]
+    z_high, z_low, a_out, r_out, coef, pot_out, rho_out = outs
     copies = [
-        pltpu.make_async_copy(source, target, refs[17].at[k])
+        pltpu.make_async_copy(source, target, refs[19].at[k])
         for k, (source, target) in enumerate(zip(sources, (*held, pot_out, rho_out)))
     ]
     for copy in copies:
         copy.start()
+    rad, ang, ax = (lax.axis_index(name) for name in AXES)
+    level = lax.broadcasted_iota(jnp.int32, coef.shape[1:], 0) - plan.guard + rad * plan.cells_r
+    valid = (level >= 0) & (level < plan.total_r)
+    radius = 0.5 * plan.total_r + level.astype(jnp.float32) + 0.5
+    upper, lower = (radius + 0.5) / radius, (radius - 0.5) / radius
+    angular = 1.0 / (radius * radius * (plan.angle_step * plan.angle_step))
+    diagonal = upper + lower + 2.0 * angular + 2.0
+    inverse = jnp.where(valid, 1.0 / diagonal, 0.0)
+    coef[0] = upper
+    coef[1] = lower
+    coef[2] = angular
+    coef[3] = inverse
+
     for copy in copies[:5]:
         copy.wait()
     anchor, extent, center, charge, place = held
-    rad, ang, ax = (lax.axis_index(name) for name in AXES)
     width_r, width_a, width_z = plan.cells_r / 3.0, plan.cells_a / 3.0, plan.cells_z / 3.0
     amplitude = 1.0 / math.sqrt(width_a * width_z / width_r)
     table = jnp.concatenate(
@@ -140,8 +153,10 @@
         profile, slope = pair(
             depth, row[2] * plan.cells_z, row[5] * plan.cells_z, row[8], width_z, plan.total_z
         )
-        z_out[number, :, :LANES] = profile
-        z_out[number, :, LANES:] = slope
+        factor = jnp.concatenate([profile, slope], axis=1)
+        high = factor.astype(jnp.bfloat16)
+        z_high[number] = high
+        z_low[number] = (factor - high.astype(jnp.float32)).astype(jnp.bfloat16)
         spot = lax.broadcasted_iota(jnp.int32, (plan.ring, LANES), 0)
         spot = jnp.where(spot < plan.cells_a + 4, spot, spot - plan.ring) + ang * plan.cells_a
         spot = jnp.where(spot < 0, spot + plan.total_a, spot)
@@ -175,74 +190,94 @@
         copy.wait()
 
 
+def whole(plan, own, other, row):
+    blank = jnp.zeros((plan.ring - plan.cells_a, plan.total_z), jnp.float32)
+    return jnp.concatenate([jnp.concatenate([own[row], other[row]], axis=1), blank], axis=0)
+
+
+def around(plan, center, turn):
+    total = pltpu.roll(center, 1, 1) + pltpu.roll(center, plan.total_z - 1, 1)
+    return total + turn * (pltpu.roll(center, 1, 0) + pltpu.roll(center, plan.ring - 1, 0))
+
+
+def start_kernel(plan, pot_own, pot_other, coef, out):
+    rad = lax.axis_index("rad")
+    rows, weight = plan.cells_r, sweep_weights(SWEEPS)[0]
+    plane = functools.partial(whole, plan, pot_own, pot_other)
+    for row in range(rows):
+        up, down, turn, inverse = (coef[k, pl.ds(plan.guard + row, 1), :] for k in range(4))
+        center = plane(row)
+        total = around(plan, center, turn)
+        if row + 1 < rows:
+            total += up * plane(row + 1)
+        if row > 0:
+            total += down * plane(row - 1)
+        out[row] = (1.0 - weight) * center + (weight * inverse) * total
+    for side in range(plan.sides):
+        place = plan.guard + plan.side_row(side, rad, 1)
+        up, down, _, inverse = (coef[k, pl.ds(place, 1), :] for k in range(4))
+        factor = jnp.where(plan.sign(side, rad) > 0, down, up)
+        out[rows + side] = (weight * inverse * factor) * plane(plan.side_row(side, rad, 0))
+
+
 def sweeps_kernel(
     plan,
-    pot_own,
-    pot_other,
+    begun,
     rho_own,
     rho_other,
-    z_fac,
+    coef,
+    z_high,
+    z_low,
     a_fac,
     r_fac,
     own_out,
     even_out,
     odd_out,
-    face_out,
+    mid_out,
+    edge_out,
     force_out,
     first,
     second,
     grown,
-    coef,
 ):
     rad = lax.axis_index("rad")
     guard, rows, ring, depth = plan.guard, plan.cells_r, plan.ring, plan.total_z
     weights = sweep_weights(SWEEPS)
-
-    level = lax.broadcasted_iota(jnp.int32, (coef.shape[1], depth), 0) - guard + rad * rows
-    valid = (level >= 0) & (level < plan.total_r)
-    radius = 0.5 * plan.total_r + level.astype(jnp.float32) + 0.5
-    upper, lower = (radius + 0.5) / radius, (radius - 0.5) / radius
-    angular = 1.0 / (radius * radius * (plan.angle_step * plan.angle_step))
-    diagonal = upper + lower + 2.0 * angular + 2.0
-    inverse = jnp.where(valid, 1.0 / diagonal, 0.0)
-    coef[0] = upper
-    coef[1] = lower
-    coef[2] = angular
-    coef[3] = inverse
 
     blank = jnp.zeros((ring, depth), jnp.float32)
     for buffer in (first, second):
         for row in range(guard):
             buffer[row] = blank
             buffer[guard + rows + row] = blank
-    tail = jnp.zeros((ring - plan.cells_a, depth), jnp.float32)
-
-    def whole(own, other, row):
-        return jnp.concatenate([jnp.concatenate([own[row], other[row]], axis=1), tail], axis=0)
-
     for row in range(rows):
-        first[guard + row] = whole(pot_own, pot_other, row)
+        inverse = coef[3, pl.ds(guard + row, 1), :]
+        charge = whole(plan, rho_own, rho_other, row)
+        first[guard + row] = begun[row] + (weights[0] * inverse) * charge
+    for side in range(plan.sides):
+        first[guard + plan.side_row(side, rad, 1)] = begun[rows + side]
+    for slot in range(plan.slots, grown.shape[0]):
+        grown[slot] = blank
 
     def relaxed(source, row, weight, charge):
         center = source[row]
         up, down, turn, inverse = (coef[k, pl.ds(row, 1), :] for k in range(4))
-        total = pltpu.roll(center, 1, 1) + pltpu.roll(center, depth - 1, 1)
-        total += turn * (pltpu.roll(center, 1, 0) + pltpu.roll(center, ring - 1, 0))
+        total = around(plan, center, turn)
         total += up * source[row + 1] + down * source[row - 1]
         if charge is not None:
             total += charge
         return (1.0 - weight) * center + (weight * inverse) * total
 
     def send_row(slot, fresh):
-        tiles = plan.cells_a // 8
-        for tile in range(tiles):
-            face_out[slot * tiles + tile] = fresh[8 * tile : 8 * tile + 8, plan.cells_z :]
+        part = [fresh[8 * tile : 8 * tile + 8, plan.cells_z :] for tile in range(plan.tiles)]
+        edge_out[2 * slot], edge_out[2 * slot + 1] = part[0], part[-1]
+        for tile in range(1, plan.tiles - 1):
+            mid_out[slot * (plan.tiles - 2) + tile - 1] = part[tile]
 
     source, target = first, second
-    for sweep in range(SWEEPS):
+    for sweep in range(1, SWEEPS):
         last = sweep == SWEEPS - 1
         for row in range(rows):
-            fresh = relaxed(source, guard + row, weights[sweep], whole(rho_own, rho_other, row))
+            fresh = relaxed(source, guard + row, weights[sweep], whole(plan, rho_own, rho_other, row))
             if last:
                 grown[row] = fresh
                 own_out[row] = fresh[: plan.cells_a, : plan.cells_z]
@@ -267,12 +302,14 @@
     for tile in range(plan.halo):
         even_out[tile], odd_out[tile] = pack(halo[2 * tile], halo[2 * tile + 1], is_even)
 
+    flat = grown[...].reshape(grown.shape[0] * ring, depth)
+    high = flat.astype(jnp.bfloat16)
+    low = (flat - high.astype(jnp.float32)).astype(jnp.bfloat16)
+    product = functools.partial(jnp.dot, preferred_element_type=jnp.float32)
+
     def chunk(number, carry):
-        spread = jnp.dot(
-            grown[...].reshape(plan.slots * ring, depth),
-            z_fac[number],
-            precision=highest,
-            preferred_element_type=jnp.float32,
+        spread = product(high, z_high[number]) + (
+            product(high, z_low[number]) + product(low, z_high[number])
         )
         sums = [jnp.zeros((ring, LANES), jnp.float32) for _ in range(3)]
         for slot in range(plan.slots):
@@ -299,20 +336,21 @@
     out[plan.halo :] = forces[0][...] if len(forces) == 1 else forces[0][...] + forces[1][...]
 
 
-def fold_kernel(plan, face, even, even_in, odd_in, face_out, force_out):
+def fold_kernel(plan, edge, even, even_in, odd_in, edge_out, force_out):
     is_even = even_sector(lax.axis_index("ang"))
-    face_out[...] = face[...]
-    tiles = plan.cells_a // 8
     for slot in range(plan.beyond):
         tile, half = divmod(plan.cells_r + slot, 2)
         first, last = unpack(even_in[tile], odd_in[tile], half, is_even)
-        face_out[slot * tiles] = face_out[slot * tiles] + first
-        face_out[slot * tiles + tiles - 1] = face_out[slot * tiles + tiles - 1] + last
+        edge_out[2 * slot] = edge[2 * slot] + first
+        edge_out[2 * slot + 1] = edge[2 * slot + 1] + last
     force_out[...] = even[plan.halo :] + even_in[plan.halo :]
 
 
-def add_kernel(plan, first, second, out):
-    out[...] = first[...] + second[...]
+def meet_kernel(plan, first, second, *refs):
+    half = len(refs) // 2
+    refs[half][...] = first[...] + second[...]
+    for mid, out in zip(refs[:half], refs[half + 1 :]):
+        out[...] = mid[...]
 
 
 def copy_kernel(plan, value, after, out):
@@ -320,12 +358,12 @@
 
 
 def final_kernel(plan, *refs):
-    own, landed, even_in, odd_in, force, out, force_out = refs[0], refs[1 : 1 + plan.sides], *refs[-5:]
+    own, mids, edges = refs[0], refs[1 : 1 + plan.sides], refs[1 + plan.sides : 1 + 2 * plan.sides]
+    even_in, odd_in, force, out, force_out = refs[-5:]
     force_out[...] = force[...]
     rad = lax.axis_index("rad")
     is_even = even_sector(lax.axis_index("ang"))
-    top = plan.cells_a - 8
-    tiles = plan.cells_a // 8
+    top, inner = plan.cells_a - 8, plan.tiles - 2
     for row in range(plan.cells_r):
         first, last = unpack(even_in[row // 2], odd_in[row // 2], row % 2, is_even)
         out[row] = own[row]
@@ -334,15 +372,19 @@
     for side in range(plan.sides):
         for step in range(1, SWEEPS + 1):
             row = plan.landing_row(side, rad, step)
-            for tile in range(tiles):
-                out[row, 8 * tile : 8 * tile + 8, :] += landed[side][(step - 1) * tiles + tile]
+            out[row, 0:8, :] += edges[side][2 * step - 2]
+            out[row, top:, :] += edges[side][2 * step - 1]
+            for tile in range(inner):
+                out[row, 8 * tile + 8 : 8 * tile + 16, :] += mids[side][(step - 1) * inner + tile]
 
 
 def call(kernel, plan, outs, scratch, flops, bytes_moved, args, spaces=None, megabytes=24):
     in_vmem = pl.BlockSpec(memory_space=pltpu.VMEM)
     return pl.pallas_call(
         functools.partial(kernel, plan),
-        out_shape=[jax.ShapeDtypeStruct(shape, jnp.float32) for shape in outs],
+        out_shape=[
+            out if hasattr(out, "dtype") else jax.ShapeDtypeStruct(out, jnp.float32) for out in outs
+        ],
         in_specs=spaces or [in_vmem] * len(args),
         out_specs=[in_vmem] * len(outs),
         scratch_shapes=scratch,
@@ -358,27 +400,40 @@
     potential_other = lax.ppermute(potential, "ax", swap)
     density_other = lax.ppermute(density, "ax", swap)
     tables = (anchor, extent, center, charge.reshape(1, -1), place.reshape(1, -1))
-    *factors, potential, density = call(
+    tall = rows + 2 * plan.guard
+    axial = jax.ShapeDtypeStruct((chunks, depth, 2 * LANES), jnp.bfloat16)
+    *factors, coef, potential, density = call(
         factors_kernel,
         plan,
-        [(chunks, depth, 2 * LANES), (chunks, 2, ring, LANES), (chunks, 3, slots, LANES)] + [block] * 2,
+        [axial, axial, (chunks, 2, ring, LANES), (chunks, 3, slots, LANES)]
+        + [(4, tall, depth), block, block],
         [pltpu.VMEM(table.shape, table.dtype) for table in tables] + [pltpu.SemaphoreType.DMA((7,))],
         10**6,
         10**6,
         [pltpu.with_memory_space_constraint(value, pltpu.HBM) for value in (*tables, potential, density)],
         [pl.BlockSpec(memory_space=pl.ANY)] * 7,
     )
-    tall = rows + 2 * plan.guard
-    scratch = [(tall, ring, depth)] * 2 + [(slots, ring, depth), (4, tall, depth)]
-    own, even, odd, face, force = call(
+    (begun,) = call(
+        start_kernel,
+        plan,
+        [(rows + plan.sides, ring, depth)],
+        [],
+        10**7,
+        10**7,
+        (potential, potential_other, coef),
+    )
+    scratch = [(tall, ring, depth)] * 2 + [(2 * plan.halo, ring, depth)]
+    inner = SWEEPS * (plan.tiles - 2)
+    own, even, odd, mid, edge, force = call(
         sweeps_kernel,
         plan,
         [block, (plan.halo, 8, width), (plan.halo, 8, width)]
-        + [(max(1, plan.face * plan.sides), 8, width), (chunks, 8, LANES)],
+        + [(max(1, inner * plan.sides), 8, width), (max(1, 2 * plan.beyond), 8, width)]
+        + [(chunks, 8, LANES)],
         [pltpu.VMEM(shape, jnp.float32) for shape in scratch],
         10**9,
         10**7,
-        (potential, potential_other, density, density_other, *factors),
+        (begun, density, density_other, coef, *factors),
     )
 
     def send(value, move):
@@ -410,23 +465,29 @@
         join_kernel, plan, [(plan.halo + chunks, 8, width)], [], 10**9, 10**9, (even, *parts)
     )
     even_in = send_angular(even, 1)
+    (mid,) = call(copy_kernel, plan, [mid.shape], [], 10**6, 10**6, (mid, even))
+    mids = send_radial(mid, inner)
     (odd_in,) = call(copy_kernel, plan, [odd.shape], [], 10**9, 10**9, (odd_in, odd))
-    face, force = call(
+    edge, force = call(
         fold_kernel,
         plan,
-        [face.shape, (chunks, 8, LANES)],
+        [edge.shape, (chunks, 8, LANES)],
         [],
         10**5,
         10**5,
-        (face, even, even_in, odd_in),
-    )
-    (face,) = call(copy_kernel, plan, [face.shape], [], 10**6, 10**6, (face, force))
-    faces = send_radial(face, plan.face)
+        (edge, even, even_in, odd_in),
+    )
+    (edge,) = call(copy_kernel, plan, [edge.shape], [], 10**6, 10**6, (edge, force))
+    edges = send_radial(edge, 2 * SWEEPS)
     step = 1
     while step < plan.n_rad:
         part = send(force, lambda r, a: (r ^ step, a))
-        (force,) = call(add_kernel, plan, [force.shape], [], 10**9, 10**9, (force, part))
         step *= 2
+        if step < plan.n_rad:
+            force = force + part
+        else:
+            shapes = [value.shape for value in (force, *mids)]
+            force, *mids = call(meet_kernel, plan, shapes, [], 10**9, 10**9, (force, part, *mids))
     last_part = send_angular(force, 2) if plan.n_ang > 2 else jnp.zeros_like(force)
     final, force = call(
         final_kernel,
@@ -435,7 +496,7 @@
         [],
         10**5,
         10**6,
-        (own, *faces, even_in, odd_in, force),
+        (own, *mids, *edges, even_in, odd_in, force),
     )
     force = force + last_part
     share = plan.atoms // (plan.n_rad * plan.n_ang * plan.n_ax)

time: 24.3 us -> 23.2 us (0.955)
  waiting for transfers between devices: 8.12 us -> 5.98 us
  starting transfers between devices: 9.28 us -> 10.8 us
  Pallas kernels: 5.38 us -> 4.97 us
    ppermute x6 -> x7, waiting for transfers between devices: 7.34 us -> 5.76 us  [send(): return lax.ppermute(value, AXES, plan.moves(move))]
    ppermute x6 -> x7, starting transfers between devices: 8.68 us -> 10.2 us  [send(): return lax.ppermute(value, AXES, plan.moves(move))]
    ppermute x1, waiting for transfers between devices: 0.56 us -> 0.01 us  [shards(): density_other = lax.ppermute(density, 'ax', swap)]
    pallas_call x9 -> x11, Pallas kernels: 5.38 us -> 4.97 us  [call(): pl.pallas_call(functools.partial(kernel, plan), out_shape=[out if hasattr...]
  transfers between devices with their start and end apart: 8 -> 9, of which waited for: 6 -> 6; matrix products, arithmetic and copies ran while one was open for 0% -> 0% of each run, Pallas kernels for 9% -> 12%
where the time goes in v5:
time: 23.2 us; the launch traced here: 23 us
  starting transfers between devices  10.8 us (47%)
  waiting for transfers between devices  5.98 us (26%)
  Pallas kernels  4.97 us (21%)
  between operations  0.68 us (3%)
  local copies, waits for them, and re-layouts  0.65 us (3%)
    ppermute x7, starting transfers between devices, send(): return lax.ppermute(value, AXES, plan.moves(move))  10.2 us
    ppermute x7, waiting for transfers between devices, send(): return lax.ppermute(value, AXES, plan.moves(move))  5.76 us
    pallas_call x11, Pallas kernels, call(): pl.pallas_call(functools.partial(kernel, plan), out_shape=[out if hasattr...  4.97 us
    reshape x1, local copies, waits for them, and re-layouts, shards(): return (final, mine.reshape(3, share))  0.65 us
    ppermute x1, starting transfers between devices, shards(): potential_other = lax.ppermute(potential, 'ax', swap)  0.52 us
  transfers between devices with their start and end apart: 9, of which 6 were waited for; matrix products, arithmetic and copies ran while one was open for 0% of the time, Pallas kernels for 12%

profile of v5, /device:TPU:0, one launch (start us, length us, event | category | flops | bytes accessed | tf_op | source)
XLA Modules:
  0.0 23.0 jit_solution(11401934310872037045)
XLA Ops:
  0.6 0.5 %collective-permute-start = (f32[16,48,128]{2,1,0:T(8,128)}, f32[16,48,128]{2,1,0:T(8,128)S(1)}, u32[]{:S(2)}, u32[]{:S(2)}) collective-permute-start(f32[16,48,128]{2,1,0:T(8,128)} %refs_5_.1), channel_id=1, source_target_pairs={{0,1},{1,0},{2,3},{3,2},{4,5},{5,4},{6,7},{7,6},{8,9},{9,8},{10,11... | collective-permute-start | bytes 1179656 | tf_op jit(solution)/shard_map/ppermute | solution.py:400
  1.1 0.1 collective-permute-start.1
  1.2 1.3 %shard_map.86 = (bf16[1,256,256]{2,1,0:T(8,128)(2,1)S(1)}, bf16[1,256,256]{2,1,0:T(8,128)(2,1)S(1)}, f32[1,2,56,128]{3,2,1,0:T(8,128)S(1)}, f32[1,3,19,128]{3,2,...) custom-call(s32[3,128]{1,0:T(4,128)} %refs_0_.1, ...), custom_call_target="tpu_custom_call" | custom-call | flops 1000000 | bytes 1000000 | tf_op jit(solution)/shard_map/pallas_call | solution.py:383
  2.5 0.2 collective-permute-done.pot_other
  2.7 0.6 %shard_map.87.begun = f32[17,56,256]{2,1,0:T(8,128)S(1)} custom-call(f32[16,48,128]{2,1,0:T(8,128)S(1)} %get-tuple-element.21.pot_own, f32[16,48,128]{2,1,0:T(8,128)S(1)} %collective-permute-done.pot_other, f32[4,24,256]{2,1,0:T(8,128)S(1)} %get-tuple-element.22.coef), custom_call_target="tpu_custom_call" | custom-call | flops 10000000 | bytes 10000000 | tf_op jit(solution)/shard_map/pallas_call | solution.py:383
  3.4 0.0 collective-permute-done.1.rho_other
  3.4 2.2 %shard_map.88 = (f32[16,48,128]{2,1,0:T(8,128)S(1)}, f32[10,8,128]{2,1,0:T(8,128)S(1)}, f32[10,8,128]{2,1,0:T(8,128)S(1)}, f32[12,8,128]{2,1,0:T(8,128)S(1)}, f3...) custom-call(f32[17,56,256]{2,1,0:T(8,128)S(1)} %shard_map.87.begun, f32[16,48,128]{2,1,0:T(8,128)S(1)} %get-tuple-element.23.rho_own, ...), custom_call_target="tpu_custom_call" | custom-call | flops 1000000000 | bytes 10000000 | tf_op jit(solution)/shard_map/pallas_call | solution.py:383
  5.6 3.8 %collective-permute-start.2 = (f32[1,8,128]{2,1,0:T(8,128)S(1)}, f32[1,8,128]{2,1,0:T(8,128)S(1)}, u32[]{:S(2)}, u32[]{:S(2)}) collective-permute-start(f32[1,8,128]{2,1,0:T(8,128)S(1)} %get-tuple-element.31.refs_0_.after), channel_id=1, source_target_pairs={{0,9},{1,8},{2,11},{3,10},{4,13},{5,12},{6,15},{7,14},{8,1},{9,0},... | collective-permute-start | bytes 12296 | tf_op jit(solution)/shard_map/ppermute | solution.py:440
  9.4 2.3 %collective-permute-start.4 = (f32[10,8,128]{2,1,0:T(8,128)S(1)}, f32[10,8,128]{2,1,0:T(8,128)S(1)}, u32[]{:S(2)}, u32[]{:S(2)}) collective-permute-start(f32[10,8,128]{2,1,0:T(8,128)S(1)} %shard_map.90.after), channel_id=1, source_target_pairs={{0,15},{1,14},{2,5},{3,4},{4,3},{5,2},{6,9},{7,8},{8,7},{9,6},{10,... | collective-permute-start | bytes 122888 | tf_op jit(solution)/shard_map/ppermute | solution.py:440
  11.7 0.0 collective-permute-done.2.refs_1_
  11.7 0.6 %collective-permute-start.3 = (f32[11,8,128]{2,1,0:T(8,128)S(1)}, f32[11,8,128]{2,1,0:T(8,128)S(1)}, u32[]{:S(2)}, u32[]{:S(2)}) collective-permute-start(f32[11,8,128]{2,1,0:T(8,128)S(1)} %shard_map.89.even.after), channel_id=1, source_target_pairs={{0,3},{1,2},{2,1},{3,0},{4,7},{5,6},{6,5},{7,4},{8,11},{9,10},{10,... | collective-permute-start | bytes 135176 | tf_op jit(solution)/shard_map/ppermute | solution.py:440
  12.3 1.5 %collective-permute-start.6 = (f32[12,8,128]{2,1,0:T(8,128)S(1)}, f32[12,8,128]{2,1,0:T(8,128)S(1)}, u32[]{:S(2)}, u32[]{:S(2)}) collective-permute-start(f32[12,8,128]{2,1,0:T(8,128)S(1)} %shard_map.93), channel_id=1, source_target_pairs={{0,17},{1,16},{2,19},{3,18},{4,21},{5,20},{6,23},{7,22},{8,25},{9,... | collective-permute-start | bytes 147464 | tf_op jit(solution)/shard_map/ppermute | solution.py:440
  13.7 1.9 %collective-permute-done.4.value = f32[10,8,128]{2,1,0:T(8,128)S(1)} collective-permute-done((f32[10,8,128]{2,1,0:T(8,128)S(1)}, f32[10,8,128]{2,1,0:T(8,128)S(1)}, u32[]{:S(2)}, u32[]{:S(2)}) %collective-permute-start.4) | collective-permute-done | bytes 40992 | tf_op jit(solution)/shard_map/ppermute | solution.py:440
  15.6 0.6 %collective-permute-done.3.even_in.refs_3_ = f32[11,8,128]{2,1,0:T(8,128)S(1)} collective-permute-done((f32[11,8,128]{2,1,0:T(8,128)S(1)}, f32[11,8,128]{2,1,0:T(8,128)S(1)}, u32[]{:S(2)}, u32[]{:S(2)}) %collective-permute-start.3) | collective-permute-done | bytes 45088 | tf_op jit(solution)/shard_map/ppermute | solution.py:440
  16.3 1.3 %collective-permute-start.5 = (f32[1,8,128]{2,1,0:T(8,128)S(1)}, f32[1,8,128]{2,1,0:T(8,128)S(1)}, u32[]{:S(2)}, u32[]{:S(2)}) collective-permute-start(f32[1,8,128]{2,1,0:T(8,128)S(1)} %get-tuple-element.33.first.after), channel_id=1, source_target_pairs={{0,17},{1,16},{2,19},{3,18},{4,21},{5,20},{6,23},{7,22},{8,25},{9,... | collective-permute-start | bytes 12296 | tf_op jit(solution)/shard_map/ppermute | solution.py:440
  17.6 0.5 %collective-permute-start.7 = (f32[6,8,128]{2,1,0:T(8,128)S(1)}, f32[6,8,128]{2,1,0:T(8,128)S(1)}, u32[]{:S(2)}, u32[]{:S(2)}) collective-permute-start(f32[6,8,128]{2,1,0:T(8,128)S(1)} %shard_map.95), channel_id=1, source_target_pairs={{0,17},{1,16},{2,19},{3,18},{4,21},{5,20},{6,23},{7,22},{8,25},{9,... | collective-permute-start | bytes 73736 | tf_op jit(solution)/shard_map/ppermute | solution.py:440
  18.1 0.0 collective-permute-done.6.refs_0_
  18.1 1.3 %collective-permute-done.5.second = f32[1,8,128]{2,1,0:T(8,128)S(1)} collective-permute-done((f32[1,8,128]{2,1,0:T(8,128)S(1)}, f32[1,8,128]{2,1,0:T(8,128)S(1)}, u32[]{:S(2)}, u32[]{:S(2)}) %collective-permute-start.5) | collective-permute-done | bytes 4128 | tf_op jit(solution)/shard_map/ppermute | solution.py:440
  19.4 0.3 %collective-permute-start.8 = (f32[1,8,128]{2,1,0:T(8,128)S(1)}, f32[1,8,128]{2,1,0:T(8,128)S(1)}, u32[]{:S(2)}, u32[]{:S(2)}) collective-permute-start(f32[1,8,128]{2,1,0:T(8,128)S(1)} %get-tuple-element.37.refs_5_), channel_id=1, source_target_pairs={{0,5},{1,4},{2,7},{3,6},{4,1},{5,0},{6,3},{7,2},{8,13},{9,12},{10,... | collective-permute-start | bytes 12296 | tf_op jit(solution)/shard_map/ppermute | solution.py:440
  19.6 1.2 %collective-permute-done.7.refs_2_ = f32[6,8,128]{2,1,0:T(8,128)S(1)} collective-permute-done((f32[6,8,128]{2,1,0:T(8,128)S(1)}, f32[6,8,128]{2,1,0:T(8,128)S(1)}, u32[]{:S(2)}, u32[]{:S(2)}) %collective-permute-start.7) | collective-permute-done | bytes 24608 | tf_op jit(solution)/shard_map/ppermute | solution.py:440
  20.8 0.8 %shard_map.96 = (f32[16,48,128]{2,1,0:T(8,128)}, f32[1,8,128]{2,1,0:T(8,128)S(1)}) custom-call(f32[16,48,128]{2,1,0:T(8,128)S(1)} %get-tuple-element.28.refs_0_, f32[12,8,128]{2,1,0:T(8,128)S(1)} %get-tuple-element.35.refs_1_, f32[6,8,128]{2,1,0:T(8,128)S(1)} %collective-permute-done.7.refs_2_, f32[11,8,128]{2,1,0:T(8,128)S(1)} %collective-permute-done.3.even_in.refs_3_, ...), custom_call_target="tpu_custom_call" | custom-call | flops 100000 | bytes 1000000 | tf_op jit(solution)/shard_map/pallas_call | solution.py:383
  21.6 0.8 %collective-permute-done.8 = f32[1,8,128]{2,1,0:T(8,128)S(1)} collective-permute-done((f32[1,8,128]{2,1,0:T(8,128)S(1)}, f32[1,8,128]{2,1,0:T(8,128)S(1)}, u32[]{:S(2)}, u32[]{:S(2)}) %collective-permute-start.8) | collective-permute-done | bytes 4128 | tf_op jit(solution)/shard_map/ppermute | solution.py:440
  22.4 0.7 %dynamic-slice_bitcast_fusion = f32[3,4]{1,0:T(4,128)} fusion(f32[1,8,128]{2,1,0:T(8,128)S(1)} %add.18, s32[]{:T(128)S(6)} %select_n.14), kind=kLoop, calls=%fused_computation | loop fusion | bytes 100 | tf_op jit(solution)/shard_map/reshape | solution.py:505
  (8 shorter events, 0.0 us)
Async XLA Ops:
  0.6 2.1 %collective-permute-start = (f32[16,48,128]{2,1,0:T(8,128)}, f32[16,48,128]{2,1,0:T(8,128)S(1)}, u32[]{:S(2)}, u32[]{:S(2)}) collective-permute-start(f32[16,48,128]{2,1,0:T(8,128)} %refs_5_.1), channel_id=1, source_target_pairs={{0,1},{1,0},{2,3},{3,2},{4,5},{5,4},{6,7},{7,6},{8,9},{9,8},{10,11... | collective-permute-start | bytes 1179656 | tf_op jit(solution)/shard_map/ppermute | solution.py:400
  1.1 2.2 %collective-permute-start.1 = (f32[16,48,128]{2,1,0:T(8,128)}, f32[16,48,128]{2,1,0:T(8,128)S(1)}, u32[]{:S(2)}, u32[]{:S(2)}) collective-permute-start(f32[16,48,128]{2,1,0:T(8,128)} %refs_6_.1), channel_id=1, source_target_pairs={{0,1},{1,0},{2,3},{3,2},{4,5},{5,4},{6,7},{7,6},{8,9},{9,8},{10,11... | collective-permute-start | bytes 1179656 | tf_op jit(solution)/shard_map/ppermute | solution.py:401
  5.6 6.1 %collective-permute-start.2 = (f32[1,8,128]{2,1,0:T(8,128)S(1)}, f32[1,8,128]{2,1,0:T(8,128)S(1)}, u32[]{:S(2)}, u32[]{:S(2)}) collective-permute-start(f32[1,8,128]{2,1,0:T(8,128)S(1)} %get-tuple-element.31.refs_0_.after), channel_id=1, source_target_pairs={{0,9},{1,8},{2,11},{3,10},{4,13},{5,12},{6,15},{7,14},{8,1},{9,0},... | collective-permute-start | bytes 12296 | tf_op jit(solution)/shard_map/ppermute | solution.py:440
  9.4 6.2 %collective-permute-start.4 = (f32[10,8,128]{2,1,0:T(8,128)S(1)}, f32[10,8,128]{2,1,0:T(8,128)S(1)}, u32[]{:S(2)}, u32[]{:S(2)}) collective-permute-start(f32[10,8,128]{2,1,0:T(8,128)S(1)} %shard_map.90.after), channel_id=1, source_target_pairs={{0,15},{1,14},{2,5},{3,4},{4,3},{5,2},{6,9},{7,8},{8,7},{9,6},{10,... | collective-permute-start | bytes 122888 | tf_op jit(solution)/shard_map/ppermute | solution.py:440
  11.7 4.6 %collective-permute-start.3 = (f32[11,8,128]{2,1,0:T(8,128)S(1)}, f32[11,8,128]{2,1,0:T(8,128)S(1)}, u32[]{:S(2)}, u32[]{:S(2)}) collective-permute-start(f32[11,8,128]{2,1,0:T(8,128)S(1)} %shard_map.89.even.after), channel_id=1, source_target_pairs={{0,3},{1,2},{2,1},{3,0},{4,7},{5,6},{6,5},{7,4},{8,11},{9,10},{10,... | collective-permute-start | bytes 135176 | tf_op jit(solution)/shard_map/ppermute | solution.py:440
  12.3 5.8 %collective-permute-start.6 = (f32[12,8,128]{2,1,0:T(8,128)S(1)}, f32[12,8,128]{2,1,0:T(8,128)S(1)}, u32[]{:S(2)}, u32[]{:S(2)}) collective-permute-start(f32[12,8,128]{2,1,0:T(8,128)S(1)} %shard_map.93), channel_id=1, source_target_pairs={{0,17},{1,16},{2,19},{3,18},{4,21},{5,20},{6,23},{7,22},{8,25},{9,... | collective-permute-start | bytes 147464 | tf_op jit(solution)/shard_map/ppermute | solution.py:440
  16.3 3.1 %collective-permute-start.5 = (f32[1,8,128]{2,1,0:T(8,128)S(1)}, f32[1,8,128]{2,1,0:T(8,128)S(1)}, u32[]{:S(2)}, u32[]{:S(2)}) collective-permute-start(f32[1,8,128]{2,1,0:T(8,128)S(1)} %get-tuple-element.33.first.after), channel_id=1, source_target_pairs={{0,17},{1,16},{2,19},{3,18},{4,21},{5,20},{6,23},{7,22},{8,25},{9,... | collective-permute-start | bytes 12296 | tf_op jit(solution)/shard_map/ppermute | solution.py:440
  17.6 3.3 %collective-permute-start.7 = (f32[6,8,128]{2,1,0:T(8,128)S(1)}, f32[6,8,128]{2,1,0:T(8,128)S(1)}, u32[]{:S(2)}, u32[]{:S(2)}) collective-permute-start(f32[6,8,128]{2,1,0:T(8,128)S(1)} %shard_map.95), channel_id=1, source_target_pairs={{0,17},{1,16},{2,19},{3,18},{4,21},{5,20},{6,23},{7,22},{8,25},{9,... | collective-permute-start | bytes 73736 | tf_op jit(solution)/shard_map/ppermute | solution.py:440
  19.4 3.0 %collective-permute-start.8 = (f32[1,8,128]{2,1,0:T(8,128)S(1)}, f32[1,8,128]{2,1,0:T(8,128)S(1)}, u32[]{:S(2)}, u32[]{:S(2)}) collective-permute-start(f32[1,8,128]{2,1,0:T(8,128)S(1)} %get-tuple-element.37.refs_5_), channel_id=1, source_target_pairs={{0,5},{1,4},{2,7},{3,6},{4,1},{5,0},{6,3},{7,2},{8,13},{9,12},{10,... | collective-permute-start | bytes 12296 | tf_op jit(solution)/shard_map/ppermute | solution.py:440

commit v6 on v5

--- a/solution.py
+++ b/solution.py
@@ -336,14 +336,19 @@
     out[plan.halo :] = forces[0][...] if len(forces) == 1 else forces[0][...] + forces[1][...]
 
 
-def fold_kernel(plan, edge, even, even_in, odd_in, edge_out, force_out):
+def sum_kernel(plan, even, even_in, out):
+    out[...] = even[plan.halo :] + even_in[plan.halo :]
+
+
+def fold_kernel(plan, edge, even_in, odd_in, *refs):
+    forces, edge_out, force_out = refs[:-2], refs[-2], refs[-1]
     is_even = even_sector(lax.axis_index("ang"))
     for slot in range(plan.beyond):
         tile, half = divmod(plan.cells_r + slot, 2)
         first, last = unpack(even_in[tile], odd_in[tile], half, is_even)
         edge_out[2 * slot] = edge[2 * slot] + first
         edge_out[2 * slot + 1] = edge[2 * slot + 1] + last
-    force_out[...] = even[plan.halo :] + even_in[plan.halo :]
+    force_out[...] = forces[0][...] if len(forces) == 1 else forces[0][...] + forces[1][...]
 
 
 def meet_kernel(plan, first, second, *refs):
@@ -453,20 +458,21 @@
     def send_angular(value, step):
         return send(value, lambda r, a: (r, a ^ step))
 
-    (odd,) = call(copy_kernel, plan, [odd.shape], [], 10**6, 10**6, (odd, force))
+    (even,) = call(
+        join_kernel, plan, [(plan.halo + chunks, 8, width)], [], 10**5, 10**5, (even, force)
+    )
+    even_in = send_angular(even, 1)
+    (odd,) = call(copy_kernel, plan, [odd.shape], [], 10**6, 10**6, (odd, even))
     odd_in = send(odd, lambda r, a: (r, (a + 1 - 2 * (1 - a % 2)) % plan.n_ang))
+    (force,) = call(sum_kernel, plan, [force.shape], [], 10**9, 10**9, (even, even_in))
+    (mid,) = call(copy_kernel, plan, [mid.shape], [], 10**6, 10**6, (mid, force))
+    mids = send_radial(mid, inner)
     parts = [force]
     step = plan.n_ang // 2
     while step > 2:
         force = sum(parts)
         parts = [force, send_angular(force, step)]
         step //= 2
-    (even,) = call(
-        join_kernel, plan, [(plan.halo + chunks, 8, width)], [], 10**9, 10**9, (even, *parts)
-    )
-    even_in = send_angular(even, 1)
-    (mid,) = call(copy_kernel, plan, [mid.shape], [], 10**6, 10**6, (mid, even))
-    mids = send_radial(mid, inner)
     (odd_in,) = call(copy_kernel, plan, [odd.shape], [], 10**9, 10**9, (odd_in, odd))
     edge, force = call(
         fold_kernel,
@@ -475,7 +481,7 @@
         [],
         10**5,
         10**5,
-        (edge, even, even_in, odd_in),
+        (edge, even_in, odd_in, *parts),
     )
     (edge,) = call(copy_kernel, plan, [edge.shape], [], 10**6, 10**6, (edge, force))
     edges = send_radial(edge, 2 * SWEEPS)

time: 23.2 us -> 22.8 us (0.983)
  waiting for transfers between devices: 5.98 us -> 4.86 us
  starting transfers between devices: 10.8 us -> 11.5 us
    ppermute x7, waiting for transfers between devices: 5.76 us -> 4.64 us  [send(): return lax.ppermute(value, AXES, plan.moves(move))]
    ppermute x7, starting transfers between devices: 10.2 us -> 10.9 us  [send(): return lax.ppermute(value, AXES, plan.moves(move))]
    pallas_call x11 -> x12, Pallas kernels: 4.97 us -> 4.98 us  [call(): pl.pallas_call(functools.partial(kernel, plan), out_shape=[out if hasattr...]
  transfers between devices with their start and end apart: 9 -> 9, of which waited for: 6 -> 5; matrix products, arithmetic and copies ran while one was open for 0% -> 0% of each run, Pallas kernels for 12% -> 12%
where the time goes in v6:
time: 22.8 us; the launch traced here: 22.7 us
  starting transfers between devices  11.5 us (50%)
  Pallas kernels  4.98 us (22%)
  waiting for transfers between devices  4.86 us (21%)
  between operations  0.69 us (3%)
  local copies, waits for them, and re-layouts  0.65 us (3%)
    ppermute x7, starting transfers between devices, send(): return lax.ppermute(value, AXES, plan.moves(move))  10.9 us
    pallas_call x12, Pallas kernels, call(): pl.pallas_call(functools.partial(kernel, plan), out_shape=[out if hasattr...  4.98 us
    ppermute x7, waiting for transfers between devices, send(): return lax.ppermute(value, AXES, plan.moves(move))  4.64 us
    reshape x1, local copies, waits for them, and re-layouts, shards(): return (final, mine.reshape(3, share))  0.65 us
    ppermute x1, starting transfers between devices, shards(): potential_other = lax.ppermute(potential, 'ax', swap)  0.52 us
  transfers between devices with their start and end apart: 9, of which 5 were waited for; matrix products, arithmetic and copies ran while one was open for 0% of the time, Pallas kernels for 12%

profile of v6, /device:TPU:0, one launch (start us, length us, event | category | flops | bytes accessed | tf_op | source)
XLA Modules:
  0.0 22.7 jit_solution(860339201972462896)
XLA Ops:
  0.6 0.5 %collective-permute-start = (f32[16,48,128]{2,1,0:T(8,128)}, f32[16,48,128]{2,1,0:T(8,128)S(1)}, u32[]{:S(2)}, u32[]{:S(2)}) collective-permute-start(f32[16,48,128]{2,1,0:T(8,128)} %refs_5_.1), channel_id=1, source_target_pairs={{0,1},{1,0},{2,3},{3,2},{4,5},{5,4},{6,7},{7,6},{8,9},{9,8},{10,11... | collective-permute-start | bytes 1179656 | tf_op jit(solution)/shard_map/ppermute | solution.py:405
  1.1 0.1 collective-permute-start.1
  1.2 1.3 %shard_map.86 = (bf16[1,256,256]{2,1,0:T(8,128)(2,1)S(1)}, bf16[1,256,256]{2,1,0:T(8,128)(2,1)S(1)}, f32[1,2,56,128]{3,2,1,0:T(8,128)S(1)}, f32[1,3,19,128]{3,2,...) custom-call(s32[3,128]{1,0:T(4,128)} %refs_0_.1, ...), custom_call_target="tpu_custom_call" | custom-call | flops 1000000 | bytes 1000000 | tf_op jit(solution)/shard_map/pallas_call | solution.py:388
  2.5 0.2 collective-permute-done.pot_other
  2.7 0.6 %shard_map.87.begun = f32[17,56,256]{2,1,0:T(8,128)S(1)} custom-call(f32[16,48,128]{2,1,0:T(8,128)S(1)} %get-tuple-element.21.pot_own, f32[16,48,128]{2,1,0:T(8,128)S(1)} %collective-permute-done.pot_other, f32[4,24,256]{2,1,0:T(8,128)S(1)} %get-tuple-element.22.coef), custom_call_target="tpu_custom_call" | custom-call | flops 10000000 | bytes 10000000 | tf_op jit(solution)/shard_map/pallas_call | solution.py:388
  3.4 0.0 collective-permute-done.1.rho_other
  3.4 2.2 %shard_map.88 = (f32[16,48,128]{2,1,0:T(8,128)S(1)}, f32[10,8,128]{2,1,0:T(8,128)S(1)}, f32[10,8,128]{2,1,0:T(8,128)S(1)}, f32[12,8,128]{2,1,0:T(8,128)S(1)}, f3...) custom-call(f32[17,56,256]{2,1,0:T(8,128)S(1)} %shard_map.87.begun, f32[16,48,128]{2,1,0:T(8,128)S(1)} %get-tuple-element.23.rho_own, ...), custom_call_target="tpu_custom_call" | custom-call | flops 1000000000 | bytes 10000000 | tf_op jit(solution)/shard_map/pallas_call | solution.py:388
  5.6 2.7 %collective-permute-start.2 = (f32[11,8,128]{2,1,0:T(8,128)S(1)}, f32[11,8,128]{2,1,0:T(8,128)S(1)}, u32[]{:S(2)}, u32[]{:S(2)}) collective-permute-start(f32[11,8,128]{2,1,0:T(8,128)S(1)} %shard_map.89.after.even), channel_id=1, source_target_pairs={{0,3},{1,2},{2,1},{3,0},{4,7},{5,6},{6,5},{7,4},{8,11},{9,10},{10,... | collective-permute-start | bytes 135176 | tf_op jit(solution)/shard_map/ppermute | solution.py:445
  8.3 3.5 %collective-permute-start.3 = (f32[10,8,128]{2,1,0:T(8,128)S(1)}, f32[10,8,128]{2,1,0:T(8,128)S(1)}, u32[]{:S(2)}, u32[]{:S(2)}) collective-permute-start(f32[10,8,128]{2,1,0:T(8,128)S(1)} %shard_map.90.after), channel_id=1, source_target_pairs={{0,15},{1,14},{2,5},{3,4},{4,3},{5,2},{6,9},{7,8},{8,7},{9,6},{10,... | collective-permute-start | bytes 122888 | tf_op jit(solution)/shard_map/ppermute | solution.py:445
  11.9 0.0 collective-permute-done.2.even_in.refs_3_
  11.9 1.2 %collective-permute-start.4 = (f32[1,8,128]{2,1,0:T(8,128)S(1)}, f32[1,8,128]{2,1,0:T(8,128)S(1)}, u32[]{:S(2)}, u32[]{:S(2)}) collective-permute-start(f32[1,8,128]{2,1,0:T(8,128)S(1)} %shard_map.92.refs_0_.after), channel_id=1, source_target_pairs={{0,9},{1,8},{2,11},{3,10},{4,13},{5,12},{6,15},{7,14},{8,1},{9,0},... | collective-permute-start | bytes 12296 | tf_op jit(solution)/shard_map/ppermute | solution.py:445
  13.0 1.5 %collective-permute-start.6 = (f32[12,8,128]{2,1,0:T(8,128)S(1)}, f32[12,8,128]{2,1,0:T(8,128)S(1)}, u32[]{:S(2)}, u32[]{:S(2)}) collective-permute-start(f32[12,8,128]{2,1,0:T(8,128)S(1)} %shard_map.94), channel_id=1, source_target_pairs={{0,17},{1,16},{2,19},{3,18},{4,21},{5,20},{6,23},{7,22},{8,25},{9,... | collective-permute-start | bytes 147464 | tf_op jit(solution)/shard_map/ppermute | solution.py:445
  14.5 0.0 collective-permute-done.3.value
  14.5 1.3 %collective-permute-done.4.refs_1_ = f32[1,8,128]{2,1,0:T(8,128)S(1)} collective-permute-done((f32[1,8,128]{2,1,0:T(8,128)S(1)}, f32[1,8,128]{2,1,0:T(8,128)S(1)}, u32[]{:S(2)}, u32[]{:S(2)}) %collective-permute-start.4) | collective-permute-done | bytes 4128 | tf_op jit(solution)/shard_map/ppermute | solution.py:445
  15.8 1.3 %collective-permute-start.5 = (f32[1,8,128]{2,1,0:T(8,128)S(1)}, f32[1,8,128]{2,1,0:T(8,128)S(1)}, u32[]{:S(2)}, u32[]{:S(2)}) collective-permute-start(f32[1,8,128]{2,1,0:T(8,128)S(1)} %get-tuple-element.33.first.after), channel_id=1, source_target_pairs={{0,17},{1,16},{2,19},{3,18},{4,21},{5,20},{6,23},{7,22},{8,25},{9,... | collective-permute-start | bytes 12296 | tf_op jit(solution)/shard_map/ppermute | solution.py:445
  17.1 0.5 %collective-permute-start.7 = (f32[6,8,128]{2,1,0:T(8,128)S(1)}, f32[6,8,128]{2,1,0:T(8,128)S(1)}, u32[]{:S(2)}, u32[]{:S(2)}) collective-permute-start(f32[6,8,128]{2,1,0:T(8,128)S(1)} %shard_map.96), channel_id=1, source_target_pairs={{0,17},{1,16},{2,19},{3,18},{4,21},{5,20},{6,23},{7,22},{8,25},{9,... | collective-permute-start | bytes 73736 | tf_op jit(solution)/shard_map/ppermute | solution.py:445
  17.6 1.3 %collective-permute-done.5.second = f32[1,8,128]{2,1,0:T(8,128)S(1)} collective-permute-done((f32[1,8,128]{2,1,0:T(8,128)S(1)}, f32[1,8,128]{2,1,0:T(8,128)S(1)}, u32[]{:S(2)}, u32[]{:S(2)}) %collective-permute-start.5) | collective-permute-done | bytes 4128 | tf_op jit(solution)/shard_map/ppermute | solution.py:445
  18.9 0.0 collective-permute-done.6.refs_0_
  18.9 0.2 %collective-permute-start.8 = (f32[1,8,128]{2,1,0:T(8,128)S(1)}, f32[1,8,128]{2,1,0:T(8,128)S(1)}, u32[]{:S(2)}, u32[]{:S(2)}) collective-permute-start(f32[1,8,128]{2,1,0:T(8,128)S(1)} %get-tuple-element.37.refs_5_), channel_id=1, source_target_pairs={{0,5},{1,4},{2,7},{3,6},{4,1},{5,0},{6,3},{7,2},{8,13},{9,12},{10,... | collective-permute-start | bytes 12296 | tf_op jit(solution)/shard_map/ppermute | solution.py:445
  19.1 1.2 %collective-permute-done.7.refs_2_ = f32[6,8,128]{2,1,0:T(8,128)S(1)} collective-permute-done((f32[6,8,128]{2,1,0:T(8,128)S(1)}, f32[6,8,128]{2,1,0:T(8,128)S(1)}, u32[]{:S(2)}, u32[]{:S(2)}) %collective-permute-start.7) | collective-permute-done | bytes 24608 | tf_op jit(solution)/shard_map/ppermute | solution.py:445
  20.4 0.8 %shard_map.97 = (f32[16,48,128]{2,1,0:T(8,128)}, f32[1,8,128]{2,1,0:T(8,128)S(1)}) custom-call(f32[16,48,128]{2,1,0:T(8,128)S(1)} %get-tuple-element.28.refs_0_, f32[12,8,128]{2,1,0:T(8,128)S(1)} %get-tuple-element.35.refs_1_, f32[6,8,128]{2,1,0:T(8,128)S(1)} %collective-permute-done.7.refs_2_, f32[11,8,128]{2,1,0:T(8,128)S(1)} %collective-permute-done.2.even_in.refs_3_, ...), custom_call_target="tpu_custom_call" | custom-call | flops 100000 | bytes 1000000 | tf_op jit(solution)/shard_map/pallas_call | solution.py:388
  21.2 0.8 %collective-permute-done.8 = f32[1,8,128]{2,1,0:T(8,128)S(1)} collective-permute-done((f32[1,8,128]{2,1,0:T(8,128)S(1)}, f32[1,8,128]{2,1,0:T(8,128)S(1)}, u32[]{:S(2)}, u32[]{:S(2)}) %collective-permute-start.8) | collective-permute-done | bytes 4128 | tf_op jit(solution)/shard_map/ppermute | solution.py:445
  22.0 0.7 %dynamic-slice_bitcast_fusion = f32[3,4]{1,0:T(4,128)} fusion(f32[1,8,128]{2,1,0:T(8,128)S(1)} %add.18, s32[]{:T(128)S(6)} %select_n.14), kind=kLoop, calls=%fused_computation | loop fusion | bytes 100 | tf_op jit(solution)/shard_map/reshape | solution.py:511
  (9 shorter events, 0.0 us)
Async XLA Ops:
  0.6 2.1 %collective-permute-start = (f32[16,48,128]{2,1,0:T(8,128)}, f32[16,48,128]{2,1,0:T(8,128)S(1)}, u32[]{:S(2)}, u32[]{:S(2)}) collective-permute-start(f32[16,48,128]{2,1,0:T(8,128)} %refs_5_.1), channel_id=1, source_target_pairs={{0,1},{1,0},{2,3},{3,2},{4,5},{5,4},{6,7},{7,6},{8,9},{9,8},{10,11... | collective-permute-start | bytes 1179656 | tf_op jit(solution)/shard_map/ppermute | solution.py:405
  1.1 2.2 %collective-permute-start.1 = (f32[16,48,128]{2,1,0:T(8,128)}, f32[16,48,128]{2,1,0:T(8,128)S(1)}, u32[]{:S(2)}, u32[]{:S(2)}) collective-permute-start(f32[16,48,128]{2,1,0:T(8,128)} %refs_6_.1), channel_id=1, source_target_pairs={{0,1},{1,0},{2,3},{3,2},{4,5},{5,4},{6,7},{7,6},{8,9},{9,8},{10,11... | collective-permute-start | bytes 1179656 | tf_op jit(solution)/shard_map/ppermute | solution.py:406
  5.6 6.2 %collective-permute-start.2 = (f32[11,8,128]{2,1,0:T(8,128)S(1)}, f32[11,8,128]{2,1,0:T(8,128)S(1)}, u32[]{:S(2)}, u32[]{:S(2)}) collective-permute-start(f32[11,8,128]{2,1,0:T(8,128)S(1)} %shard_map.89.after.even), channel_id=1, source_target_pairs={{0,3},{1,2},{2,1},{3,0},{4,7},{5,6},{6,5},{7,4},{8,11},{9,10},{10,... | collective-permute-start | bytes 135176 | tf_op jit(solution)/shard_map/ppermute | solution.py:445
  8.3 6.2 %collective-permute-start.3 = (f32[10,8,128]{2,1,0:T(8,128)S(1)}, f32[10,8,128]{2,1,0:T(8,128)S(1)}, u32[]{:S(2)}, u32[]{:S(2)}) collective-permute-start(f32[10,8,128]{2,1,0:T(8,128)S(1)} %shard_map.90.after), channel_id=1, source_target_pairs={{0,15},{1,14},{2,5},{3,4},{4,3},{5,2},{6,9},{7,8},{8,7},{9,6},{10,... | collective-permute-start | bytes 122888 | tf_op jit(solution)/shard_map/ppermute | solution.py:445
  11.9 3.9 %collective-permute-start.4 = (f32[1,8,128]{2,1,0:T(8,128)S(1)}, f32[1,8,128]{2,1,0:T(8,128)S(1)}, u32[]{:S(2)}, u32[]{:S(2)}) collective-permute-start(f32[1,8,128]{2,1,0:T(8,128)S(1)} %shard_map.92.refs_0_.after), channel_id=1, source_target_pairs={{0,9},{1,8},{2,11},{3,10},{4,13},{5,12},{6,15},{7,14},{8,1},{9,0},... | collective-permute-start | bytes 12296 | tf_op jit(solution)/shard_map/ppermute | solution.py:445
  13.0 5.9 %collective-permute-start.6 = (f32[12,8,128]{2,1,0:T(8,128)S(1)}, f32[12,8,128]{2,1,0:T(8,128)S(1)}, u32[]{:S(2)}, u32[]{:S(2)}) collective-permute-start(f32[12,8,128]{2,1,0:T(8,128)S(1)} %shard_map.94), channel_id=1, source_target_pairs={{0,17},{1,16},{2,19},{3,18},{4,21},{5,20},{6,23},{7,22},{8,25},{9,... | collective-permute-start | bytes 147464 | tf_op jit(solution)/shard_map/ppermute | solution.py:445
  15.8 3.1 %collective-permute-start.5 = (f32[1,8,128]{2,1,0:T(8,128)S(1)}, f32[1,8,128]{2,1,0:T(8,128)S(1)}, u32[]{:S(2)}, u32[]{:S(2)}) collective-permute-start(f32[1,8,128]{2,1,0:T(8,128)S(1)} %get-tuple-element.33.first.after), channel_id=1, source_target_pairs={{0,17},{1,16},{2,19},{3,18},{4,21},{5,20},{6,23},{7,22},{8,25},{9,... | collective-permute-start | bytes 12296 | tf_op jit(solution)/shard_map/ppermute | solution.py:445
  17.1 3.3 %collective-permute-start.7 = (f32[6,8,128]{2,1,0:T(8,128)S(1)}, f32[6,8,128]{2,1,0:T(8,128)S(1)}, u32[]{:S(2)}, u32[]{:S(2)}) collective-permute-start(f32[6,8,128]{2,1,0:T(8,128)S(1)} %shard_map.96), channel_id=1, source_target_pairs={{0,17},{1,16},{2,19},{3,18},{4,21},{5,20},{6,23},{7,22},{8,25},{9,... | collective-permute-start | bytes 73736 | tf_op jit(solution)/shard_map/ppermute | solution.py:445
  18.9 3.1 %collective-permute-start.8 = (f32[1,8,128]{2,1,0:T(8,128)S(1)}, f32[1,8,128]{2,1,0:T(8,128)S(1)}, u32[]{:S(2)}, u32[]{:S(2)}) collective-permute-start(f32[1,8,128]{2,1,0:T(8,128)S(1)} %get-tuple-element.37.refs_5_), channel_id=1, source_target_pairs={{0,5},{1,4},{2,7},{3,6},{4,1},{5,0},{6,3},{7,2},{8,13},{9,12},{10,... | collective-permute-start | bytes 12296 | tf_op jit(solution)/shard_map/ppermute | solution.py:445

commit v7 on v6

--- a/solution.py
+++ b/solution.py
@@ -43,6 +43,8 @@
         self.beyond = SWEEPS * self.sides
         self.tiles = self.cells_a // 8
         self.halo = (self.slots + 1) // 2
+        self.pairs = self.cells_r // 2
+        self.corners = self.halo - self.pairs
 
     def sign(self, side, rad):
         if self.sides == 1:
@@ -230,25 +232,22 @@
     z_low,
     a_fac,
     r_fac,
-    own_out,
-    even_out,
-    odd_out,
-    mid_out,
-    edge_out,
+    grown,
     force_out,
     first,
     second,
-    grown,
 ):
     rad = lax.axis_index("rad")
     guard, rows, ring, depth = plan.guard, plan.cells_r, plan.ring, plan.total_z
     weights = sweep_weights(SWEEPS)
 
     blank = jnp.zeros((ring, depth), jnp.float32)
-    for buffer in (first, second):
-        for row in range(guard):
-            buffer[row] = blank
-            buffer[guard + rows + row] = blank
+    for away in range(1, guard + 1):
+        for row in (guard - away, guard + rows - 1 + away):
+            if away < guard:
+                first[row] = blank
+            if away != 2:
+                second[row] = blank
     for row in range(rows):
         inverse = coef[3, pl.ds(guard + row, 1), :]
         charge = whole(plan, rho_own, rho_other, row)
@@ -267,12 +266,6 @@
             total += charge
         return (1.0 - weight) * center + (weight * inverse) * total
 
-    def send_row(slot, fresh):
-        part = [fresh[8 * tile : 8 * tile + 8, plan.cells_z :] for tile in range(plan.tiles)]
-        edge_out[2 * slot], edge_out[2 * slot + 1] = part[0], part[-1]
-        for tile in range(1, plan.tiles - 1):
-            mid_out[slot * (plan.tiles - 2) + tile - 1] = part[tile]
-
     source, target = first, second
     for sweep in range(1, SWEEPS):
         last = sweep == SWEEPS - 1
@@ -280,7 +273,6 @@
             fresh = relaxed(source, guard + row, weights[sweep], whole(plan, rho_own, rho_other, row))
             if last:
                 grown[row] = fresh
-                own_out[row] = fresh[: plan.cells_a, : plan.cells_z]
             else:
                 target[guard + row] = fresh
         for side in range(plan.sides):
@@ -290,17 +282,9 @@
                 if last:
                     slot = SWEEPS * side + step - 1
                     grown[rows + slot] = fresh
-                    send_row(slot, fresh)
                 else:
                     target[place] = fresh
         source, target = target, source
-
-    is_even = even_sector(lax.axis_index("ang"))
-    halo = [grown[slot, plan.cells_a :, plan.cells_z :] for slot in range(rows)]
-    halo += [grown[slot, plan.cells_a :, : plan.cells_z] for slot in range(rows, plan.slots)]
-    halo += [jnp.zeros_like(halo[0])] * (2 * plan.halo - plan.slots)
-    for tile in range(plan.halo):
-        even_out[tile], odd_out[tile] = pack(halo[2 * tile], halo[2 * tile + 1], is_even)
 
     flat = grown[...].reshape(grown.shape[0] * ring, depth)
     high = flat.astype(jnp.bfloat16)
@@ -330,24 +314,54 @@
         lax.fori_loop(0, plan.chunks, chunk, 0)
 
 
-def join_kernel(plan, even, *refs):
-    forces, out = refs[:-1], refs[-1]
-    out[: plan.halo] = even[...]
-    out[plan.halo :] = forces[0][...] if len(forces) == 1 else forces[0][...] + forces[1][...]
+def halo_tile(plan, grown, tile, is_even):
+    planes = []
+    for slot in (2 * tile, 2 * tile + 1):
+        half = slice(plan.cells_z, None) if slot < plan.cells_r else slice(plan.cells_z)
+        planes.append(grown[slot, plan.cells_a :, half])
+    return pack(*planes, is_even)
+
+
+def join_kernel(plan, grown, force, out):
+    is_even = even_sector(lax.axis_index("ang"))
+    for tile in range(plan.corners):
+        out[tile] = halo_tile(plan, grown, plan.pairs + tile, is_even)[0]
+    out[plan.corners :] = force[...]
+
+
+def main_kernel(plan, grown, after, out):
+    is_even = even_sector(lax.axis_index("ang"))
+    for tile in range(plan.pairs):
+        out[tile] = halo_tile(plan, grown, tile, is_even)[0]
+
+
+def odd_kernel(plan, grown, after, out):
+    is_even = even_sector(lax.axis_index("ang"))
+    for tile in range(plan.halo):
+        out[tile] = halo_tile(plan, grown, tile, is_even)[1]
+
+
+def mid_kernel(plan, grown, after, out):
+    inner = plan.tiles - 2
+    for slot in range(plan.beyond):
+        for tile in range(inner):
+            first = 8 * (tile + 1)
+            out[slot * inner + tile] = grown[plan.cells_r + slot, first : first + 8, plan.cells_z :]
 
 
 def sum_kernel(plan, even, even_in, out):
-    out[...] = even[plan.halo :] + even_in[plan.halo :]
-
-
-def fold_kernel(plan, edge, even_in, odd_in, *refs):
+    out[...] = even[plan.corners :] + even_in[plan.corners :]
+
+
+def fold_kernel(plan, grown, even_in, odd_in, *refs):
     forces, edge_out, force_out = refs[:-2], refs[-2], refs[-1]
     is_even = even_sector(lax.axis_index("ang"))
     for slot in range(plan.beyond):
         tile, half = divmod(plan.cells_r + slot, 2)
-        first, last = unpack(even_in[tile], odd_in[tile], half, is_even)
-        edge_out[2 * slot] = edge[2 * slot] + first
-        edge_out[2 * slot + 1] = edge[2 * slot + 1] + last
+        first, last = unpack(even_in[tile - plan.pairs], odd_in[tile], half, is_even)
+        plane, top = plan.cells_r + slot, plan.cells_a - 8
+        edge_out[2 * slot] = grown[plane, :8, plan.cells_z :] + first
+        edge_out[2 * slot + 1] = grown[plane, top : plan.cells_a, plan.cells_z :] + last
     force_out[...] = forces[0][...] if len(forces) == 1 else forces[0][...] + forces[1][...]
 
 
@@ -371,7 +385,7 @@
     top, inner = plan.cells_a - 8, plan.tiles - 2
     for row in range(plan.cells_r):
         first, last = unpack(even_in[row // 2], odd_in[row // 2], row % 2, is_even)
-        out[row] = own[row]
+        out[row] = own[row, : plan.cells_a, : plan.cells_z]
         out[row, 0:8, :] += first
         out[row, top:, :] += last
     for side in range(plan.sides):
@@ -381,6 +395,14 @@
             out[row, top:, :] += edges[side][2 * step - 1]
             for tile in range(inner):
                 out[row, 8 * tile + 8 : 8 * tile + 16, :] += mids[side][(step - 1) * inner + tile]
+
+
+def share_kernel(plan, force, part, out):
+    share = out.shape[1]
+    start = plan.device(*(lax.axis_index(name) for name in AXES)) * share
+    total = force[start // LANES] + part[start // LANES]
+    turned = pltpu.roll(total, lax.rem(LANES - lax.rem(start, LANES), LANES), 1)
+    out[...] = turned[:3, :share]
 
 
 def call(kernel, plan, outs, scratch, flops, bytes_moved, args, spaces=None, megabytes=24):
@@ -427,14 +449,12 @@
         10**7,
         (potential, potential_other, coef),
     )
-    scratch = [(tall, ring, depth)] * 2 + [(2 * plan.halo, ring, depth)]
+    scratch = [(tall, ring, depth)] * 2
     inner = SWEEPS * (plan.tiles - 2)
-    own, even, odd, mid, edge, force = call(
+    grown, force = call(
         sweeps_kernel,
         plan,
-        [block, (plan.halo, 8, width), (plan.halo, 8, width)]
-        + [(max(1, inner * plan.sides), 8, width), (max(1, 2 * plan.beyond), 8, width)]
-        + [(chunks, 8, LANES)],
+        [(2 * plan.halo, ring, depth), (chunks, 8, LANES)],
         [pltpu.VMEM(shape, jnp.float32) for shape in scratch],
         10**9,
         10**7,
@@ -458,15 +478,20 @@
     def send_angular(value, step):
         return send(value, lambda r, a: (r, a ^ step))
 
+    (join,) = call(
+        join_kernel, plan, [(plan.corners + chunks, 8, width)], [], 10**5, 10**5, (grown, force)
+    )
+    join_in = send_angular(join, 1)
+    odd_shape = (plan.halo, 8, width)
+    (odd,) = call(odd_kernel, plan, [odd_shape], [], 10**6, 10**6, (grown, join))
+    odd_in = send(odd, lambda r, a: (r, (a + 1 - 2 * (1 - a % 2)) % plan.n_ang))
+    (force,) = call(sum_kernel, plan, [force.shape], [], 10**9, 10**9, (join, join_in))
+    mid_shape = (max(1, inner * plan.sides), 8, width)
+    (mid,) = call(mid_kernel, plan, [mid_shape], [], 10**6, 10**6, (grown, force))
     (even,) = call(
-        join_kernel, plan, [(plan.halo + chunks, 8, width)], [], 10**5, 10**5, (even, force)
-    )
-    even_in = send_angular(even, 1)
-    (odd,) = call(copy_kernel, plan, [odd.shape], [], 10**6, 10**6, (odd, even))
-    odd_in = send(odd, lambda r, a: (r, (a + 1 - 2 * (1 - a % 2)) % plan.n_ang))
-    (force,) = call(sum_kernel, plan, [force.shape], [], 10**9, 10**9, (even, even_in))
-    (mid,) = call(copy_kernel, plan, [mid.shape], [], 10**6, 10**6, (mid, force))
-    mids = send_radial(mid, inner)
+        main_kernel, plan, [(plan.pairs, 8, width)], [], 10**6, 10**6, (grown, force)
+    )
+    mids = send_radial(mid, inner) + [send_angular(even, 1)]
     parts = [force]
     step = plan.n_ang // 2
     while step > 2:
@@ -477,11 +502,11 @@
     edge, force = call(
         fold_kernel,
         plan,
-        [edge.shape, (chunks, 8, LANES)],
+        [(max(1, 2 * plan.beyond), 8, width), (chunks, 8, LANES)],
         [],
         10**5,
         10**5,
-        (edge, even_in, odd_in, *parts),
+        (grown, join_in, odd_in, *parts),
     )
     (edge,) = call(copy_kernel, plan, [edge.shape], [], 10**6, 10**6, (edge, force))
     edges = send_radial(edge, 2 * SWEEPS)
@@ -494,6 +519,7 @@
         else:
             shapes = [value.shape for value in (force, *mids)]
             force, *mids = call(meet_kernel, plan, shapes, [], 10**9, 10**9, (force, part, *mids))
+    *mids, even_in = mids
     last_part = send_angular(force, 2) if plan.n_ang > 2 else jnp.zeros_like(force)
     final, force = call(
         final_kernel,
@@ -502,13 +528,11 @@
         [],
         10**5,
         10**6,
-        (own, *mids, *edges, even_in, odd_in, force),
-    )
-    force = force + last_part
+        (grown, *mids, *edges, even_in, odd_in, force),
+    )
     share = plan.atoms // (plan.n_rad * plan.n_ang * plan.n_ax)
-    first = plan.device(*(lax.axis_index(name) for name in AXES)) * share
-    mine = lax.dynamic_slice(force, (first // LANES, 0, first % LANES), (1, 3, share))
-    return final, mine.reshape(3, share)
+    (mine,) = call(share_kernel, plan, [(3, share)], [], 10**5, 10**5, (force, last_part))
+    return final, mine
 
 
 def solution(mesh):

time: 22.8 us -> 22.9 us (level)
  waiting for transfers between devices: 4.86 us -> 2.86 us
  starting transfers between devices: 11.5 us -> 13.5 us
  local copies, waits for them, and re-layouts: 0.65 us -> 0 us
  Pallas kernels: 4.98 us -> 5.61 us
    ppermute x7 -> x8, starting transfers between devices: 10.9 us -> 12.9 us  [send(): return lax.ppermute(value, AXES, plan.moves(move))]
    ppermute x7 -> x8, waiting for transfers between devices: 4.64 us -> 2.64 us  [send(): return lax.ppermute(value, AXES, plan.moves(move))]
    reshape x1 -> x0, local copies, waits for them, and re-layouts: 0.65 us -> none  [shards(): return (final, mine.reshape(3, share))]
    pallas_call x12 -> x14, Pallas kernels: 4.98 us -> 5.61 us  [call(): pl.pallas_call(functools.partial(kernel, plan), out_shape=[out if hasattr...]
  transfers between devices with their start and end apart: 9 -> 10, of which waited for: 5 -> 4; matrix products, arithmetic and copies ran while one was open for 0% -> 0% of each run, Pallas kernels for 12% -> 12%
where the time goes in v7:
time: 22.9 us; the launch traced here: 22.7 us
  starting transfers between devices  13.5 us (59%)
  Pallas kernels  5.61 us (24%)
  waiting for transfers between devices  2.86 us (12%)
  between operations  0.68 us (3%)
    ppermute x8, starting transfers between devices, send(): return lax.ppermute(value, AXES, plan.moves(move))  12.9 us
    pallas_call x14, Pallas kernels, call(): pl.pallas_call(functools.partial(kernel, plan), out_shape=[out if hasattr...  5.61 us
    ppermute x8, waiting for transfers between devices, send(): return lax.ppermute(value, AXES, plan.moves(move))  2.64 us
    ppermute x1, starting transfers between devices, shards(): potential_other = lax.ppermute(potential, 'ax', swap)  0.52 us
  transfers between devices with their start and end apart: 10, of which 4 were waited for; matrix products, arithmetic and copies ran while one was open for 0% of the time, Pallas kernels for 12%

profile of v7, /device:TPU:0, one launch (start us, length us, event | category | flops | bytes accessed | tf_op | source)
XLA Modules:
  0.0 22.7 jit_solution(10233604561011409506)
XLA Ops:
  0.6 0.5 %collective-permute-start = (f32[16,48,128]{2,1,0:T(8,128)}, f32[16,48,128]{2,1,0:T(8,128)S(1)}, u32[]{:S(2)}, u32[]{:S(2)}) collective-permute-start(f32[16,48,128]{2,1,0:T(8,128)} %refs_5_.1), channel_id=1, source_target_pairs={{0,1},{1,0},{2,3},{3,2},{4,5},{5,4},{6,7},{7,6},{8,9},{9,8},{10,11... | collective-permute-start | bytes 1179656 | tf_op jit(solution)/shard_map/ppermute | solution.py:427
  1.1 0.1 collective-permute-start.1
  1.2 1.3 %shard_map.86 = (bf16[1,256,256]{2,1,0:T(8,128)(2,1)S(1)}, bf16[1,256,256]{2,1,0:T(8,128)(2,1)S(1)}, f32[1,2,56,128]{3,2,1,0:T(8,128)S(1)}, f32[1,3,19,128]{3,2,...) custom-call(s32[3,128]{1,0:T(4,128)} %refs_0_.1, ...), custom_call_target="tpu_custom_call" | custom-call | flops 1000000 | bytes 1000000 | tf_op jit(solution)/shard_map/pallas_call | solution.py:410
  2.5 0.2 collective-permute-done.pot_other
  2.7 0.6 %shard_map.87.begun = f32[17,56,256]{2,1,0:T(8,128)S(1)} custom-call(f32[16,48,128]{2,1,0:T(8,128)S(1)} %get-tuple-element.18.pot_own, f32[16,48,128]{2,1,0:T(8,128)S(1)} %collective-permute-done.pot_other, f32[4,24,256]{2,1,0:T(8,128)S(1)} %get-tuple-element.19.coef), custom_call_target="tpu_custom_call" | custom-call | flops 10000000 | bytes 10000000 | tf_op jit(solution)/shard_map/pallas_call | solution.py:410
  3.4 0.0 collective-permute-done.1.rho_other
  3.4 2.2 %shard_map.88 = (f32[20,56,256]{2,1,0:T(8,128)S(1)}, f32[1,8,128]{2,1,0:T(8,128)S(1)}) custom-call(f32[17,56,256]{2,1,0:T(8,128)S(1)} %shard_map.87.begun, f32[16,48,128]{2,1,0:T(8,128)S(1)} %get-tuple-element.20.rho_own, f32[16,48,128]{2,1,0:T(8,128)S(1)} %collective-permute-done.1.rho_other, f32[4,24,256]{2,1,0:T(8,128)S(1)} %get-tuple-element.19.coef, ...), custom_call_target="tpu_custom_call" | custom-call | flops 1000000000 | bytes 10000000 | tf_op jit(solution)/shard_map/pallas_call | solution.py:410
  5.6 2.7 %collective-permute-start.2 = (f32[3,8,128]{2,1,0:T(8,128)S(1)}, f32[3,8,128]{2,1,0:T(8,128)S(1)}, u32[]{:S(2)}, u32[]{:S(2)}) collective-permute-start(f32[3,8,128]{2,1,0:T(8,128)S(1)} %shard_map.89.after.even), channel_id=1, source_target_pairs={{0,3},{1,2},{2,1},{3,0},{4,7},{5,6},{6,5},{7,4},{8,11},{9,10},{10,... | collective-permute-start | bytes 36872 | tf_op jit(solution)/shard_map/ppermute | solution.py:465
  8.3 3.6 %collective-permute-start.3 = (f32[10,8,128]{2,1,0:T(8,128)S(1)}, f32[10,8,128]{2,1,0:T(8,128)S(1)}, u32[]{:S(2)}, u32[]{:S(2)}) collective-permute-start(f32[10,8,128]{2,1,0:T(8,128)S(1)} %shard_map.90.after), channel_id=1, source_target_pairs={{0,15},{1,14},{2,5},{3,4},{4,3},{5,2},{6,9},{7,8},{8,7},{9,6},{10,... | collective-permute-start | bytes 122888 | tf_op jit(solution)/shard_map/ppermute | solution.py:465
  11.9 0.0 collective-permute-done.2.even_in
  11.9 0.6 %collective-permute-start.4 = (f32[1,8,128]{2,1,0:T(8,128)S(1)}, f32[1,8,128]{2,1,0:T(8,128)S(1)}, u32[]{:S(2)}, u32[]{:S(2)}) collective-permute-start(f32[1,8,128]{2,1,0:T(8,128)S(1)} %shard_map.92.refs_0_.after), channel_id=1, source_target_pairs={{0,9},{1,8},{2,11},{3,10},{4,13},{5,12},{6,15},{7,14},{8,1},{9,0},... | collective-permute-start | bytes 12296 | tf_op jit(solution)/shard_map/ppermute | solution.py:465
  12.5 1.6 %collective-permute-start.7 = (f32[8,8,128]{2,1,0:T(8,128)S(1)}, f32[8,8,128]{2,1,0:T(8,128)S(1)}, u32[]{:S(2)}, u32[]{:S(2)}) collective-permute-start(f32[8,8,128]{2,1,0:T(8,128)S(1)} %shard_map.95), channel_id=1, source_target_pairs={{0,3},{1,2},{2,1},{3,0},{4,7},{5,6},{6,5},{7,4},{8,11},{9,10},{10,... | collective-permute-start | bytes 98312 | tf_op jit(solution)/shard_map/ppermute | solution.py:465
  14.1 1.3 %collective-permute-start.6 = (f32[12,8,128]{2,1,0:T(8,128)S(1)}, f32[12,8,128]{2,1,0:T(8,128)S(1)}, u32[]{:S(2)}, u32[]{:S(2)}) collective-permute-start(f32[12,8,128]{2,1,0:T(8,128)S(1)} %shard_map.94), channel_id=1, source_target_pairs={{0,17},{1,16},{2,19},{3,18},{4,21},{5,20},{6,23},{7,22},{8,25},{9,... | collective-permute-start | bytes 147464 | tf_op jit(solution)/shard_map/ppermute | solution.py:465
  15.3 0.0 collective-permute-done.3.value
  15.3 0.5 %collective-permute-done.4.refs_1_ = f32[1,8,128]{2,1,0:T(8,128)S(1)} collective-permute-done((f32[1,8,128]{2,1,0:T(8,128)S(1)}, f32[1,8,128]{2,1,0:T(8,128)S(1)}, u32[]{:S(2)}, u32[]{:S(2)}) %collective-permute-start.4) | collective-permute-done | bytes 4128 | tf_op jit(solution)/shard_map/ppermute | solution.py:465
  15.8 1.3 %collective-permute-start.5 = (f32[1,8,128]{2,1,0:T(8,128)S(1)}, f32[1,8,128]{2,1,0:T(8,128)S(1)}, u32[]{:S(2)}, u32[]{:S(2)}) collective-permute-start(f32[1,8,128]{2,1,0:T(8,128)S(1)} %get-tuple-element.27.first.after), channel_id=1, source_target_pairs={{0,17},{1,16},{2,19},{3,18},{4,21},{5,20},{6,23},{7,22},{8,25},{9,... | collective-permute-start | bytes 12296 | tf_op jit(solution)/shard_map/ppermute | solution.py:465
  17.2 0.5 %collective-permute-start.8 = (f32[6,8,128]{2,1,0:T(8,128)S(1)}, f32[6,8,128]{2,1,0:T(8,128)S(1)}, u32[]{:S(2)}, u32[]{:S(2)}) collective-permute-start(f32[6,8,128]{2,1,0:T(8,128)S(1)} %shard_map.97), channel_id=1, source_target_pairs={{0,17},{1,16},{2,19},{3,18},{4,21},{5,20},{6,23},{7,22},{8,25},{9,... | collective-permute-start | bytes 73736 | tf_op jit(solution)/shard_map/ppermute | solution.py:465
  17.7 0.0 collective-permute-done.7.refs_1_
  17.7 1.3 %collective-permute-done.5.second = f32[1,8,128]{2,1,0:T(8,128)S(1)} collective-permute-done((f32[1,8,128]{2,1,0:T(8,128)S(1)}, f32[1,8,128]{2,1,0:T(8,128)S(1)}, u32[]{:S(2)}, u32[]{:S(2)}) %collective-permute-start.5) | collective-permute-done | bytes 4128 | tf_op jit(solution)/shard_map/ppermute | solution.py:465
  18.9 1.5 %collective-permute-start.9 = (f32[1,8,128]{2,1,0:T(8,128)S(1)}, f32[1,8,128]{2,1,0:T(8,128)S(1)}, u32[]{:S(2)}, u32[]{:S(2)}) collective-permute-start(f32[1,8,128]{2,1,0:T(8,128)S(1)} %get-tuple-element.31.refs_5_), channel_id=1, source_target_pairs={{0,5},{1,4},{2,7},{3,6},{4,1},{5,0},{6,3},{7,2},{8,13},{9,12},{10,... | collective-permute-start | bytes 12296 | tf_op jit(solution)/shard_map/ppermute | solution.py:465
  20.4 0.0 collective-permute-done.8.refs_2_
  20.4 0.8 %shard_map.98 = (f32[16,48,128]{2,1,0:T(8,128)}, f32[1,8,128]{2,1,0:T(8,128)S(1)}) custom-call(f32[20,56,256]{2,1,0:T(8,128)S(1)} %get-tuple-element.25.grown.refs_0_, f32[12,8,128]{2,1,0:T(8,128)S(1)} %get-tuple-element.28.refs_1_, f32[6,8,128]{2,1,0:T(8,128)S(1)} %collective-permute-done.8.refs_2_, f32[8,8,128]{2,1,0:T(8,128)S(1)} %get-tuple-element.30.refs_3_, ...), custom_call_target="tpu_custom_call" | custom-call | flops 100000 | bytes 1000000 | tf_op jit(solution)/shard_map/pallas_call | solution.py:410
  21.2 0.8 %collective-permute-done.9.part = f32[1,8,128]{2,1,0:T(8,128)S(1)} collective-permute-done((f32[1,8,128]{2,1,0:T(8,128)S(1)}, f32[1,8,128]{2,1,0:T(8,128)S(1)}, u32[]{:S(2)}, u32[]{:S(2)}) %collective-permute-start.9) | collective-permute-done | bytes 4128 | tf_op jit(solution)/shard_map/ppermute | solution.py:465
  22.0 0.6 %shard_map.99 = f32[3,4]{1,0:T(4,128)} custom-call(f32[1,8,128]{2,1,0:T(8,128)S(1)} %get-tuple-element.33.force, f32[1,8,128]{2,1,0:T(8,128)S(1)} %collective-permute-done.9.part), custom_call_target="tpu_custom_call" | custom-call | flops 100000 | bytes 100000 | tf_op jit(solution)/shard_map/pallas_call | solution.py:410
  (10 shorter events, 0.1 us)
Async XLA Ops:
  0.6 2.1 %collective-permute-start = (f32[16,48,128]{2,1,0:T(8,128)}, f32[16,48,128]{2,1,0:T(8,128)S(1)}, u32[]{:S(2)}, u32[]{:S(2)}) collective-permute-start(f32[16,48,128]{2,1,0:T(8,128)} %refs_5_.1), channel_id=1, source_target_pairs={{0,1},{1,0},{2,3},{3,2},{4,5},{5,4},{6,7},{7,6},{8,9},{9,8},{10,11... | collective-permute-start | bytes 1179656 | tf_op jit(solution)/shard_map/ppermute | solution.py:427
  1.1 2.2 %collective-permute-start.1 = (f32[16,48,128]{2,1,0:T(8,128)}, f32[16,48,128]{2,1,0:T(8,128)S(1)}, u32[]{:S(2)}, u32[]{:S(2)}) collective-permute-start(f32[16,48,128]{2,1,0:T(8,128)} %refs_6_.1), channel_id=1, source_target_pairs={{0,1},{1,0},{2,3},{3,2},{4,5},{5,4},{6,7},{7,6},{8,9},{9,8},{10,11... | collective-permute-start | bytes 1179656 | tf_op jit(solution)/shard_map/ppermute | solution.py:428
  5.6 6.3 %collective-permute-start.2 = (f32[3,8,128]{2,1,0:T(8,128)S(1)}, f32[3,8,128]{2,1,0:T(8,128)S(1)}, u32[]{:S(2)}, u32[]{:S(2)}) collective-permute-start(f32[3,8,128]{2,1,0:T(8,128)S(1)} %shard_map.89.after.even), channel_id=1, source_target_pairs={{0,3},{1,2},{2,1},{3,0},{4,7},{5,6},{6,5},{7,4},{8,11},{9,10},{10,... | collective-permute-start | bytes 36872 | tf_op jit(solution)/shard_map/ppermute | solution.py:465
  8.3 7.0 %collective-permute-start.3 = (f32[10,8,128]{2,1,0:T(8,128)S(1)}, f32[10,8,128]{2,1,0:T(8,128)S(1)}, u32[]{:S(2)}, u32[]{:S(2)}) collective-permute-start(f32[10,8,128]{2,1,0:T(8,128)S(1)} %shard_map.90.after), channel_id=1, source_target_pairs={{0,15},{1,14},{2,5},{3,4},{4,3},{5,2},{6,9},{7,8},{8,7},{9,6},{10,... | collective-permute-start | bytes 122888 | tf_op jit(solution)/shard_map/ppermute | solution.py:465
  11.9 3.9 %collective-permute-start.4 = (f32[1,8,128]{2,1,0:T(8,128)S(1)}, f32[1,8,128]{2,1,0:T(8,128)S(1)}, u32[]{:S(2)}, u32[]{:S(2)}) collective-permute-start(f32[1,8,128]{2,1,0:T(8,128)S(1)} %shard_map.92.refs_0_.after), channel_id=1, source_target_pairs={{0,9},{1,8},{2,11},{3,10},{4,13},{5,12},{6,15},{7,14},{8,1},{9,0},... | collective-permute-start | bytes 12296 | tf_op jit(solution)/shard_map/ppermute | solution.py:465
  12.5 5.2 %collective-permute-start.7 = (f32[8,8,128]{2,1,0:T(8,128)S(1)}, f32[8,8,128]{2,1,0:T(8,128)S(1)}, u32[]{:S(2)}, u32[]{:S(2)}) collective-permute-start(f32[8,8,128]{2,1,0:T(8,128)S(1)} %shard_map.95), channel_id=1, source_target_pairs={{0,3},{1,2},{2,1},{3,0},{4,7},{5,6},{6,5},{7,4},{8,11},{9,10},{10,... | collective-permute-start | bytes 98312 | tf_op jit(solution)/shard_map/ppermute | solution.py:465
  14.1 4.9 %collective-permute-start.6 = (f32[12,8,128]{2,1,0:T(8,128)S(1)}, f32[12,8,128]{2,1,0:T(8,128)S(1)}, u32[]{:S(2)}, u32[]{:S(2)}) collective-permute-start(f32[12,8,128]{2,1,0:T(8,128)S(1)} %shard_map.94), channel_id=1, source_target_pairs={{0,17},{1,16},{2,19},{3,18},{4,21},{5,20},{6,23},{7,22},{8,25},{9,... | collective-permute-start | bytes 147464 | tf_op jit(solution)/shard_map/ppermute | solution.py:465
  15.8 3.1 %collective-permute-start.5 = (f32[1,8,128]{2,1,0:T(8,128)S(1)}, f32[1,8,128]{2,1,0:T(8,128)S(1)}, u32[]{:S(2)}, u32[]{:S(2)}) collective-permute-start(f32[1,8,128]{2,1,0:T(8,128)S(1)} %get-tuple-element.27.first.after), channel_id=1, source_target_pairs={{0,17},{1,16},{2,19},{3,18},{4,21},{5,20},{6,23},{7,22},{8,25},{9,... | collective-permute-start | bytes 12296 | tf_op jit(solution)/shard_map/ppermute | solution.py:465
  17.2 3.3 %collective-permute-start.8 = (f32[6,8,128]{2,1,0:T(8,128)S(1)}, f32[6,8,128]{2,1,0:T(8,128)S(1)}, u32[]{:S(2)}, u32[]{:S(2)}) collective-permute-start(f32[6,8,128]{2,1,0:T(8,128)S(1)} %shard_map.97), channel_id=1, source_target_pairs={{0,17},{1,16},{2,19},{3,18},{4,21},{5,20},{6,23},{7,22},{8,25},{9,... | collective-permute-start | bytes 73736 | tf_op jit(solution)/shard_map/ppermute | solution.py:465
  18.9 3.1 %collective-permute-start.9 = (f32[1,8,128]{2,1,0:T(8,128)S(1)}, f32[1,8,128]{2,1,0:T(8,128)S(1)}, u32[]{:S(2)}, u32[]{:S(2)}) collective-permute-start(f32[1,8,128]{2,1,0:T(8,128)S(1)} %get-tuple-element.31.refs_5_), channel_id=1, source_target_pairs={{0,5},{1,4},{2,7},{3,6},{4,1},{5,0},{6,3},{7,2},{8,13},{9,12},{10,... | collective-permute-start | bytes 12296 | tf_op jit(solution)/shard_map/ppermute | solution.py:465

commit v8 on v7

--- a/solution.py
+++ b/solution.py
@@ -10,6 +10,7 @@
 
 SWEEPS = 3
 LANES = 128
+GROUP = 4
 AXES = ("rad", "ang", "ax")
 
 cheb_low = 0.2
@@ -43,6 +44,7 @@
         self.beyond = SWEEPS * self.sides
         self.tiles = self.cells_a // 8
         self.halo = (self.slots + 1) // 2
+        self.planes = -(-self.slots // GROUP) * GROUP
         self.pairs = self.cells_r // 2
         self.corners = self.halo - self.pairs
 
@@ -266,6 +268,24 @@
             total += charge
         return (1.0 - weight) * center + (weight * inverse) * total
 
+    product = functools.partial(jnp.dot, preferred_element_type=jnp.float32)
+
+    def project(number, group, sums):
+        flat = grown[GROUP * group : GROUP * (group + 1)].reshape(GROUP * ring, depth)
+        high = flat.astype(jnp.bfloat16)
+        low = (flat - high.astype(jnp.float32)).astype(jnp.bfloat16)
+        spread = product(high, z_high[number]) + (
+            product(high, z_low[number]) + product(low, z_high[number])
+        )
+        sums = list(sums)
+        for slot in range(GROUP * group, min(GROUP * (group + 1), plan.slots)):
+            begin = (slot - GROUP * group) * ring
+            piece = spread[begin : begin + ring]
+            for k, part in enumerate((piece[:, :LANES], piece[:, :LANES], piece[:, LANES:])):
+                sums[k] += r_fac[number, k, pl.ds(slot, 1), :] * part
+        return sums
+
+    sums = [jnp.zeros((ring, LANES), jnp.float32) for _ in range(3)]
     source, target = first, second
     for sweep in range(1, SWEEPS):
         last = sweep == SWEEPS - 1
@@ -273,6 +293,8 @@
             fresh = relaxed(source, guard + row, weights[sweep], whole(plan, rho_own, rho_other, row))
             if last:
                 grown[row] = fresh
+                if plan.chunks == 1 and row % GROUP == GROUP - 1:
+                    sums = project(0, row // GROUP, sums)
             else:
                 target[guard + row] = fresh
         for side in range(plan.sides):
@@ -285,32 +307,29 @@
                 else:
                     target[place] = fresh
         source, target = target, source
-
-    flat = grown[...].reshape(grown.shape[0] * ring, depth)
-    high = flat.astype(jnp.bfloat16)
-    low = (flat - high.astype(jnp.float32)).astype(jnp.bfloat16)
-    product = functools.partial(jnp.dot, preferred_element_type=jnp.float32)
-
-    def chunk(number, carry):
-        spread = product(high, z_high[number]) + (
-            product(high, z_low[number]) + product(low, z_high[number])
-        )
-        sums = [jnp.zeros((ring, LANES), jnp.float32) for _ in range(3)]
-        for slot in range(plan.slots):
-            piece = spread[slot * ring : (slot + 1) * ring]
-            for k, part in enumerate((piece[:, :LANES], piece[:, :LANES], piece[:, LANES:])):
-                sums[k] += r_fac[number, k, pl.ds(slot, 1), :] * part
+    if plan.chunks == 1:
+        for group in range(rows // GROUP, plan.planes // GROUP):
+            sums = project(0, group, sums)
+
+    def finish(number, sums):
         total = [
             jnp.sum(a_fac[number, turn] * sums[k], axis=0, keepdims=True)
             for k, turn in enumerate((0, 1, 0))
         ]
         total.append(jnp.zeros((5, LANES), jnp.float32))
         force_out[number] = jnp.concatenate(total, axis=0)
-        return carry
 
     if plan.chunks == 1:
-        chunk(0, 0)
+        finish(0, sums)
     else:
+
+        def chunk(number, carry):
+            sums = [jnp.zeros((ring, LANES), jnp.float32) for _ in range(3)]
+            for group in range(plan.planes // GROUP):
+                sums = project(number, group, sums)
+            finish(number, sums)
+            return carry
+
         lax.fori_loop(0, plan.chunks, chunk, 0)
 
 
@@ -454,7 +473,7 @@
     grown, force = call(
         sweeps_kernel,
         plan,
-        [(2 * plan.halo, ring, depth), (chunks, 8, LANES)],
+        [(plan.planes, ring, depth), (chunks, 8, LANES)],
         [pltpu.VMEM(shape, jnp.float32) for shape in scratch],
         10**9,
         10**7,

time: 22.9 us -> 22.8 us (level)
  no operation moved by 1% of the time
where the time goes in v8:
time: 22.8 us; the launch traced here: 22.7 us
  starting transfers between devices  13.5 us (59%)
  Pallas kernels  5.59 us (25%)
  waiting for transfers between devices  2.85 us (12%)
  between operations  0.69 us (3%)
    ppermute x8, starting transfers between devices, send(): return lax.ppermute(value, AXES, plan.moves(move))  13 us
    pallas_call x14, Pallas kernels, call(): pl.pallas_call(functools.partial(kernel, plan), out_shape=[out if hasattr...  5.59 us
    ppermute x8, waiting for transfers between devices, send(): return lax.ppermute(value, AXES, plan.moves(move))  2.63 us
    ppermute x1, starting transfers between devices, shards(): potential_other = lax.ppermute(potential, 'ax', swap)  0.52 us
  transfers between devices with their start and end apart: 10, of which 4 were waited for; matrix products, arithmetic and copies ran while one was open for 0% of the time, Pallas kernels for 12%

profile of v8, /device:TPU:0, one launch (start us, length us, event | category | flops | bytes accessed | tf_op | source)
XLA Modules:
  0.0 22.7 jit_solution(4164880672767975770)
XLA Ops:
  0.6 0.5 %collective-permute-start = (f32[16,48,128]{2,1,0:T(8,128)}, f32[16,48,128]{2,1,0:T(8,128)S(1)}, u32[]{:S(2)}, u32[]{:S(2)}) collective-permute-start(f32[16,48,128]{2,1,0:T(8,128)} %refs_5_.1), channel_id=1, source_target_pairs={{0,1},{1,0},{2,3},{3,2},{4,5},{5,4},{6,7},{7,6},{8,9},{9,8},{10,11... | collective-permute-start | bytes 1179656 | tf_op jit(solution)/shard_map/ppermute | solution.py:446
  1.1 0.1 collective-permute-start.1
  1.2 1.3 %shard_map.86 = (bf16[1,256,256]{2,1,0:T(8,128)(2,1)S(1)}, bf16[1,256,256]{2,1,0:T(8,128)(2,1)S(1)}, f32[1,2,56,128]{3,2,1,0:T(8,128)S(1)}, f32[1,3,19,128]{3,2,...) custom-call(s32[3,128]{1,0:T(4,128)} %refs_0_.1, ...), custom_call_target="tpu_custom_call" | custom-call | flops 1000000 | bytes 1000000 | tf_op jit(solution)/shard_map/pallas_call | solution.py:429
  2.5 0.2 collective-permute-done.pot_other
  2.7 0.6 %shard_map.87.begun = f32[17,56,256]{2,1,0:T(8,128)S(1)} custom-call(f32[16,48,128]{2,1,0:T(8,128)S(1)} %get-tuple-element.18.pot_own, f32[16,48,128]{2,1,0:T(8,128)S(1)} %collective-permute-done.pot_other, f32[4,24,256]{2,1,0:T(8,128)S(1)} %get-tuple-element.19.coef), custom_call_target="tpu_custom_call" | custom-call | flops 10000000 | bytes 10000000 | tf_op jit(solution)/shard_map/pallas_call | solution.py:429
  3.4 0.0 collective-permute-done.1.rho_other
  3.4 2.2 %shard_map.88 = (f32[20,56,256]{2,1,0:T(8,128)S(1)}, f32[1,8,128]{2,1,0:T(8,128)S(1)}) custom-call(f32[17,56,256]{2,1,0:T(8,128)S(1)} %shard_map.87.begun, f32[16,48,128]{2,1,0:T(8,128)S(1)} %get-tuple-element.20.rho_own, f32[16,48,128]{2,1,0:T(8,128)S(1)} %collective-permute-done.1.rho_other, f32[4,24,256]{2,1,0:T(8,128)S(1)} %get-tuple-element.19.coef, ...), custom_call_target="tpu_custom_call" | custom-call | flops 1000000000 | bytes 10000000 | tf_op jit(solution)/shard_map/pallas_call | solution.py:429
  5.6 2.7 %collective-permute-start.2 = (f32[3,8,128]{2,1,0:T(8,128)S(1)}, f32[3,8,128]{2,1,0:T(8,128)S(1)}, u32[]{:S(2)}, u32[]{:S(2)}) collective-permute-start(f32[3,8,128]{2,1,0:T(8,128)S(1)} %shard_map.89.after.even), channel_id=1, source_target_pairs={{0,3},{1,2},{2,1},{3,0},{4,7},{5,6},{6,5},{7,4},{8,11},{9,10},{10,... | collective-permute-start | bytes 36872 | tf_op jit(solution)/shard_map/ppermute | solution.py:484
  8.3 3.6 %collective-permute-start.3 = (f32[10,8,128]{2,1,0:T(8,128)S(1)}, f32[10,8,128]{2,1,0:T(8,128)S(1)}, u32[]{:S(2)}, u32[]{:S(2)}) collective-permute-start(f32[10,8,128]{2,1,0:T(8,128)S(1)} %shard_map.90.after), channel_id=1, source_target_pairs={{0,15},{1,14},{2,5},{3,4},{4,3},{5,2},{6,9},{7,8},{8,7},{9,6},{10,... | collective-permute-start | bytes 122888 | tf_op jit(solution)/shard_map/ppermute | solution.py:484
  11.9 0.0 collective-permute-done.2.even_in
  11.9 0.6 %collective-permute-start.4 = (f32[1,8,128]{2,1,0:T(8,128)S(1)}, f32[1,8,128]{2,1,0:T(8,128)S(1)}, u32[]{:S(2)}, u32[]{:S(2)}) collective-permute-start(f32[1,8,128]{2,1,0:T(8,128)S(1)} %shard_map.92.refs_0_.after), channel_id=1, source_target_pairs={{0,9},{1,8},{2,11},{3,10},{4,13},{5,12},{6,15},{7,14},{8,1},{9,0},... | collective-permute-start | bytes 12296 | tf_op jit(solution)/shard_map/ppermute | solution.py:484
  12.5 1.6 %collective-permute-start.7 = (f32[8,8,128]{2,1,0:T(8,128)S(1)}, f32[8,8,128]{2,1,0:T(8,128)S(1)}, u32[]{:S(2)}, u32[]{:S(2)}) collective-permute-start(f32[8,8,128]{2,1,0:T(8,128)S(1)} %shard_map.95), channel_id=1, source_target_pairs={{0,3},{1,2},{2,1},{3,0},{4,7},{5,6},{6,5},{7,4},{8,11},{9,10},{10,... | collective-permute-start | bytes 98312 | tf_op jit(solution)/shard_map/ppermute | solution.py:484
  14.0 1.3 %collective-permute-start.6 = (f32[12,8,128]{2,1,0:T(8,128)S(1)}, f32[12,8,128]{2,1,0:T(8,128)S(1)}, u32[]{:S(2)}, u32[]{:S(2)}) collective-permute-start(f32[12,8,128]{2,1,0:T(8,128)S(1)} %shard_map.94), channel_id=1, source_target_pairs={{0,17},{1,16},{2,19},{3,18},{4,21},{5,20},{6,23},{7,22},{8,25},{9,... | collective-permute-start | bytes 147464 | tf_op jit(solution)/shard_map/ppermute | solution.py:484
  15.3 0.0 collective-permute-done.3.value
  15.3 0.5 %collective-permute-done.4.refs_1_ = f32[1,8,128]{2,1,0:T(8,128)S(1)} collective-permute-done((f32[1,8,128]{2,1,0:T(8,128)S(1)}, f32[1,8,128]{2,1,0:T(8,128)S(1)}, u32[]{:S(2)}, u32[]{:S(2)}) %collective-permute-start.4) | collective-permute-done | bytes 4128 | tf_op jit(solution)/shard_map/ppermute | solution.py:484
  15.8 1.3 %collective-permute-start.5 = (f32[1,8,128]{2,1,0:T(8,128)S(1)}, f32[1,8,128]{2,1,0:T(8,128)S(1)}, u32[]{:S(2)}, u32[]{:S(2)}) collective-permute-start(f32[1,8,128]{2,1,0:T(8,128)S(1)} %get-tuple-element.27.first.after), channel_id=1, source_target_pairs={{0,17},{1,16},{2,19},{3,18},{4,21},{5,20},{6,23},{7,22},{8,25},{9,... | collective-permute-start | bytes 12296 | tf_op jit(solution)/shard_map/ppermute | solution.py:484
  17.1 0.5 %collective-permute-start.8 = (f32[6,8,128]{2,1,0:T(8,128)S(1)}, f32[6,8,128]{2,1,0:T(8,128)S(1)}, u32[]{:S(2)}, u32[]{:S(2)}) collective-permute-start(f32[6,8,128]{2,1,0:T(8,128)S(1)} %shard_map.97), channel_id=1, source_target_pairs={{0,17},{1,16},{2,19},{3,18},{4,21},{5,20},{6,23},{7,22},{8,25},{9,... | collective-permute-start | bytes 73736 | tf_op jit(solution)/shard_map/ppermute | solution.py:484
  17.6 0.0 collective-permute-done.7.refs_1_
  17.6 1.3 %collective-permute-done.5.second = f32[1,8,128]{2,1,0:T(8,128)S(1)} collective-permute-done((f32[1,8,128]{2,1,0:T(8,128)S(1)}, f32[1,8,128]{2,1,0:T(8,128)S(1)}, u32[]{:S(2)}, u32[]{:S(2)}) %collective-permute-start.5) | collective-permute-done | bytes 4128 | tf_op jit(solution)/shard_map/ppermute | solution.py:484
  18.9 1.5 %collective-permute-start.9 = (f32[1,8,128]{2,1,0:T(8,128)S(1)}, f32[1,8,128]{2,1,0:T(8,128)S(1)}, u32[]{:S(2)}, u32[]{:S(2)}) collective-permute-start(f32[1,8,128]{2,1,0:T(8,128)S(1)} %get-tuple-element.31.refs_5_), channel_id=1, source_target_pairs={{0,5},{1,4},{2,7},{3,6},{4,1},{5,0},{6,3},{7,2},{8,13},{9,12},{10,... | collective-permute-start | bytes 12296 | tf_op jit(solution)/shard_map/ppermute | solution.py:484
  20.4 0.0 collective-permute-done.8.refs_2_
  20.4 0.8 %shard_map.98 = (f32[16,48,128]{2,1,0:T(8,128)}, f32[1,8,128]{2,1,0:T(8,128)S(1)}) custom-call(f32[20,56,256]{2,1,0:T(8,128)S(1)} %get-tuple-element.25.grown.refs_0_, f32[12,8,128]{2,1,0:T(8,128)S(1)} %get-tuple-element.28.refs_1_, f32[6,8,128]{2,1,0:T(8,128)S(1)} %collective-permute-done.8.refs_2_, f32[8,8,128]{2,1,0:T(8,128)S(1)} %get-tuple-element.30.refs_3_, ...), custom_call_target="tpu_custom_call" | custom-call | flops 100000 | bytes 1000000 | tf_op jit(solution)/shard_map/pallas_call | solution.py:429
  21.2 0.8 %collective-permute-done.9.part = f32[1,8,128]{2,1,0:T(8,128)S(1)} collective-permute-done((f32[1,8,128]{2,1,0:T(8,128)S(1)}, f32[1,8,128]{2,1,0:T(8,128)S(1)}, u32[]{:S(2)}, u32[]{:S(2)}) %collective-permute-start.9) | collective-permute-done | bytes 4128 | tf_op jit(solution)/shard_map/ppermute | solution.py:484
  22.0 0.6 %shard_map.99 = f32[3,4]{1,0:T(4,128)} custom-call(f32[1,8,128]{2,1,0:T(8,128)S(1)} %get-tuple-element.33.force, f32[1,8,128]{2,1,0:T(8,128)S(1)} %collective-permute-done.9.part), custom_call_target="tpu_custom_call" | custom-call | flops 100000 | bytes 100000 | tf_op jit(solution)/shard_map/pallas_call | solution.py:429
  (10 shorter events, 0.1 us)
Async XLA Ops:
  0.6 2.1 %collective-permute-start = (f32[16,48,128]{2,1,0:T(8,128)}, f32[16,48,128]{2,1,0:T(8,128)S(1)}, u32[]{:S(2)}, u32[]{:S(2)}) collective-permute-start(f32[16,48,128]{2,1,0:T(8,128)} %refs_5_.1), channel_id=1, source_target_pairs={{0,1},{1,0},{2,3},{3,2},{4,5},{5,4},{6,7},{7,6},{8,9},{9,8},{10,11... | collective-permute-start | bytes 1179656 | tf_op jit(solution)/shard_map/ppermute | solution.py:446
  1.1 2.2 %collective-permute-start.1 = (f32[16,48,128]{2,1,0:T(8,128)}, f32[16,48,128]{2,1,0:T(8,128)S(1)}, u32[]{:S(2)}, u32[]{:S(2)}) collective-permute-start(f32[16,48,128]{2,1,0:T(8,128)} %refs_6_.1), channel_id=1, source_target_pairs={{0,1},{1,0},{2,3},{3,2},{4,5},{5,4},{6,7},{7,6},{8,9},{9,8},{10,11... | collective-permute-start | bytes 1179656 | tf_op jit(solution)/shard_map/ppermute | solution.py:447
  5.6 6.3 %collective-permute-start.2 = (f32[3,8,128]{2,1,0:T(8,128)S(1)}, f32[3,8,128]{2,1,0:T(8,128)S(1)}, u32[]{:S(2)}, u32[]{:S(2)}) collective-permute-start(f32[3,8,128]{2,1,0:T(8,128)S(1)} %shard_map.89.after.even), channel_id=1, source_target_pairs={{0,3},{1,2},{2,1},{3,0},{4,7},{5,6},{6,5},{7,4},{8,11},{9,10},{10,... | collective-permute-start | bytes 36872 | tf_op jit(solution)/shard_map/ppermute | solution.py:484
  8.3 7.0 %collective-permute-start.3 = (f32[10,8,128]{2,1,0:T(8,128)S(1)}, f32[10,8,128]{2,1,0:T(8,128)S(1)}, u32[]{:S(2)}, u32[]{:S(2)}) collective-permute-start(f32[10,8,128]{2,1,0:T(8,128)S(1)} %shard_map.90.after), channel_id=1, source_target_pairs={{0,15},{1,14},{2,5},{3,4},{4,3},{5,2},{6,9},{7,8},{8,7},{9,6},{10,... | collective-permute-start | bytes 122888 | tf_op jit(solution)/shard_map/ppermute | solution.py:484
  11.9 3.9 %collective-permute-start.4 = (f32[1,8,128]{2,1,0:T(8,128)S(1)}, f32[1,8,128]{2,1,0:T(8,128)S(1)}, u32[]{:S(2)}, u32[]{:S(2)}) collective-permute-start(f32[1,8,128]{2,1,0:T(8,128)S(1)} %shard_map.92.refs_0_.after), channel_id=1, source_target_pairs={{0,9},{1,8},{2,11},{3,10},{4,13},{5,12},{6,15},{7,14},{8,1},{9,0},... | collective-permute-start | bytes 12296 | tf_op jit(solution)/shard_map/ppermute | solution.py:484
  12.5 5.2 %collective-permute-start.7 = (f32[8,8,128]{2,1,0:T(8,128)S(1)}, f32[8,8,128]{2,1,0:T(8,128)S(1)}, u32[]{:S(2)}, u32[]{:S(2)}) collective-permute-start(f32[8,8,128]{2,1,0:T(8,128)S(1)} %shard_map.95), channel_id=1, source_target_pairs={{0,3},{1,2},{2,1},{3,0},{4,7},{5,6},{6,5},{7,4},{8,11},{9,10},{10,... | collective-permute-start | bytes 98312 | tf_op jit(solution)/shard_map/ppermute | solution.py:484
  14.0 4.9 %collective-permute-start.6 = (f32[12,8,128]{2,1,0:T(8,128)S(1)}, f32[12,8,128]{2,1,0:T(8,128)S(1)}, u32[]{:S(2)}, u32[]{:S(2)}) collective-permute-start(f32[12,8,128]{2,1,0:T(8,128)S(1)} %shard_map.94), channel_id=1, source_target_pairs={{0,17},{1,16},{2,19},{3,18},{4,21},{5,20},{6,23},{7,22},{8,25},{9,... | collective-permute-start | bytes 147464 | tf_op jit(solution)/shard_map/ppermute | solution.py:484
  15.8 3.1 %collective-permute-start.5 = (f32[1,8,128]{2,1,0:T(8,128)S(1)}, f32[1,8,128]{2,1,0:T(8,128)S(1)}, u32[]{:S(2)}, u32[]{:S(2)}) collective-permute-start(f32[1,8,128]{2,1,0:T(8,128)S(1)} %get-tuple-element.27.first.after), channel_id=1, source_target_pairs={{0,17},{1,16},{2,19},{3,18},{4,21},{5,20},{6,23},{7,22},{8,25},{9,... | collective-permute-start | bytes 12296 | tf_op jit(solution)/shard_map/ppermute | solution.py:484
  17.1 3.3 %collective-permute-start.8 = (f32[6,8,128]{2,1,0:T(8,128)S(1)}, f32[6,8,128]{2,1,0:T(8,128)S(1)}, u32[]{:S(2)}, u32[]{:S(2)}) collective-permute-start(f32[6,8,128]{2,1,0:T(8,128)S(1)} %shard_map.97), channel_id=1, source_target_pairs={{0,17},{1,16},{2,19},{3,18},{4,21},{5,20},{6,23},{7,22},{8,25},{9,... | collective-permute-start | bytes 73736 | tf_op jit(solution)/shard_map/ppermute | solution.py:484
  18.9 3.1 %collective-permute-start.9 = (f32[1,8,128]{2,1,0:T(8,128)S(1)}, f32[1,8,128]{2,1,0:T(8,128)S(1)}, u32[]{:S(2)}, u32[]{:S(2)}) collective-permute-start(f32[1,8,128]{2,1,0:T(8,128)S(1)} %get-tuple-element.31.refs_5_), channel_id=1, source_target_pairs={{0,5},{1,4},{2,7},{3,6},{4,1},{5,0},{6,3},{7,2},{8,13},{9,12},{10,... | collective-permute-start | bytes 12296 | tf_op jit(solution)/shard_map/ppermute | solution.py:484
